TPU v7x, 32 devices: a whole 2x2x4 slice. The times are simulated.
32 devices in a mesh: dom: 8 (over z, y), rep: 4 (over x, core).
Axes of the slice: x: 2, y: 2, z: 4, core: 2. Of those that a mesh axis runs over, the one named last changes fastest.
Arguments:
- features: bfloat16 [4, 16384, 602], P('rep', 'dom'), may hold values from -6 to 6
- nbr_index: int32 [4, 3, 16384, 25], P('rep', None, 'dom'), may hold values from 0 to 2303, as said below
- nbr_mask: int32 [4, 3, 16384, 25], P('rep', None, 'dom'), may hold values from 0 to 1, as said below
- send_rows: int32 [4, 8, 8, 32], P('rep', 'dom'), may hold values from 0 to 2047
- send_count: int32 [4, 8, 8], P('rep', 'dom'), may hold values from 0 to 32, as said below
- labels: int32 [4, 128], P('rep', 'dom'), may hold values from 0 to 40
- seed_mask: int32 [4, 128], P('rep', 'dom'), may hold values from 0 to 1
- w_first: float32 [1204, 256], replicated, may hold values from -0.15625 to 0.15625
- w_rest: float32 [2, 512, 256], replicated, may hold values from -6 to 6
- w_head: float32 [256, 41], replicated, may hold values from -6 to 6
- biases: float32 [809], replicated, may hold values from -3 to 3
- stat_big: float32 [1204, 1204], P('rep'), as said below
- root_big: float32 [1204, 1204], P('rep'), as said below
- stat_mid: float32 [2, 512, 512], P(None, 'rep'), as said below
- root_mid: float32 [2, 512, 512], P(None, 'rep'), as said below
- stat_sq: float32 [4, 256, 256], P(None, 'rep'), as said below
- root_sq: float32 [4, 256, 256], replicated, as said below
- stat_hr: float32 [41, 41], replicated, as said below
- root_hr: float32 [41, 41], replicated, as said below
- bias_m: float32 [809], replicated, may hold values from -7.6293945e-06 to 7.6293945e-06
- bias_v: float32 [809], replicated, may hold values from 2.7506863e-16 to 1.1002745e-15
Outputs:
- loss_sum: float32 [], replicated
- seed_total: float32 [], replicated
- grad_norm: float32 [], replicated
- grad_first: float32 [1204, 256], P('rep')
- grad_rest: float32 [2, 512, 256], P(None, 'rep')
- grad_head: float32 [256, 41], P('rep')
- new_bias_m: float32 [809], replicated
- new_bias_v: float32 [809], replicated
- new_stat_big: float32 [1204, 1204], P('rep')
- new_stat_mid: float32 [2, 512, 512], P(None, 'rep')
- new_stat_sq: float32 [4, 256, 256], P(None, 'rep')
- new_stat_hr: float32 [41, 41], replicated
- new_first: float32 [1204, 256], P('rep')
- new_rest: float32 [2, 512, 256], P(None, 'rep')
- new_head: float32 [256, 41], P('rep')
- new_biases: float32 [809], replicated
- first_low: bfloat16 [1204, 256], P('rep')
- rest_low: bfloat16 [2, 512, 256], P(None, 'rep')
- head_low: bfloat16 [256, 41], P('rep')
Inputs may be any that keep to these rules, and one draw needn't show every extreme that they name: `nbr_index`: a slot refers to an own row or to a slot s < send_count[b, q, p] of a sending partition q. `nbr_mask`: in layer one only the first 25 slots, in layers two and three only the first 10 slots may be valid; some nodes have no valid slot. `send_count`: zero from a partition to itself. `stat_big`: symmetric. `stat_mid`: symmetric. `stat_sq`: symmetric. `stat_hr`: symmetric. `root_big`: symmetric. `root_mid`: symmetric. `root_sq`: symmetric. `root_hr`: symmetric.
All inputs are finite; a program needn't handle non-finite values.
Results may differ from a plain program's by a relative error of at most 0.013.
Values may be sent and summed in bfloat16 or wider, within the bound.
A program may use at most 192 MiB of HBM per device.

v0:
```python
import jax
import jax.numpy as jnp
from jax import lax
from jax.sharding import PartitionSpec as P

STEP = 5


clip_limit = 0.0001
decay = 0.5
shampoo_rate = 1.0
beta_one = 0.9
beta_two = 0.999
bias_rate = 0.05
weight_decay = 0.01
adam_eps = 1e-08
norm_eps = 1e-06
highest = lax.Precision.HIGHEST


def activate(z):
    act = jax.nn.gelu(z, approximate=True)
    return act * lax.rsqrt(jnp.sum(act * act, axis=-1, keepdims=True) + norm_eps)


def count_matrix(nbr, mask, columns):
    nodes, slots = nbr.shape
    column_ids = jnp.arange(columns, dtype=jnp.int32)[None, :]
    mask_low = mask.astype(jnp.bfloat16)

    def add_slot(slot, total):
        picks = lax.dynamic_slice_in_dim(nbr, slot, 1, 1)
        weight = lax.dynamic_slice_in_dim(mask_low, slot, 1, 1)
        return total + (picks == column_ids).astype(jnp.bfloat16) * weight

    return lax.fori_loop(0, slots, add_slot, jnp.zeros((nodes, columns), jnp.bfloat16))


def layer_forward(h, weight, bias, nbr, mask, send_list, valid):
    nodes, width = h.shape
    hb = h.astype(jnp.bfloat16)
    outgoing = (
        jnp.take(hb, send_list, axis=0).reshape(valid.shape[0], valid.shape[1], width)
        * valid[:, :, None]
    )
    incoming = lax.all_to_all(outgoing, "dom", split_axis=0, concat_axis=0, tiled=True)
    table = jnp.concatenate([hb, incoming.reshape(-1, width)], axis=0)
    counts = count_matrix(nbr, mask, table.shape[0])
    degree = jnp.maximum(jnp.sum(mask, axis=1), 1).astype(jnp.float32)[:, None]
    gathered = jnp.dot(counts, table, preferred_element_type=jnp.float32)
    joined = jnp.concatenate([hb, (gathered / degree).astype(jnp.bfloat16)], axis=1)
    z = jnp.dot(joined, weight.astype(jnp.bfloat16), preferred_element_type=jnp.float32) + bias
    return (activate(z), (joined, counts, degree, z))


def layer_backward(grad_out, weight, kept, send_list, valid, need_input):
    joined, counts, degree, z = kept
    nodes = joined.shape[0]
    width = joined.shape[1] // 2
    grad_z = jax.vjp(activate, z)[1](grad_out)[0].astype(jnp.bfloat16)
    grad_w = jnp.einsum("nk,nh->kh", joined, grad_z, preferred_element_type=jnp.float32)
    grad_b = jnp.sum(grad_z.astype(jnp.float32), axis=0)
    if not need_input:
        return (grad_w, grad_b, None)
    grad_joined = jnp.einsum(
        "nh,kh->nk", grad_z, weight.astype(jnp.bfloat16), preferred_element_type=jnp.float32
    )
    grad_gathered = (grad_joined[:, width:] / degree).astype(jnp.bfloat16)
    grad_table = jnp.einsum("nj,nw->jw", counts, grad_gathered, preferred_element_type=jnp.float32)
    returned = (
        grad_table[nodes:].reshape(valid.shape[0], valid.shape[1], width).astype(jnp.bfloat16)
    )
    returned = lax.all_to_all(returned, "dom", split_axis=0, concat_axis=0, tiled=True)
    sent_back = (returned * valid[:, :, None]).reshape(-1, width)
    placement = (send_list[:, None] == jnp.arange(nodes, dtype=jnp.int32)[None, :]).astype(
        jnp.bfloat16
    )
    scattered = jnp.einsum("sn,sw->nw", placement, sent_back, preferred_element_type=jnp.float32)
    return (grad_w, grad_b, grad_joined[:, :width] + grad_table[:nodes] + scattered)


def shampoo(grad, weight, left, left_root, right, right_root, part, right_split):
    count = left.shape[0]
    grad_rows = lax.dynamic_slice_in_dim(grad, part * count, count, 0)
    weight_rows = lax.dynamic_slice_in_dim(weight, part * count, count, 0)
    new_left = decay * left + (1.0 - decay) * jnp.dot(grad_rows, grad.T, precision=highest)
    if right_split:
        cols = right.shape[0]
        grad_cols = lax.dynamic_slice_in_dim(grad, part * cols, cols, 1)
        new_right = decay * right + (1.0 - decay) * jnp.dot(grad_cols.T, grad, precision=highest)
    else:
        new_right = decay * right + (1.0 - decay) * jnp.dot(grad.T, grad, precision=highest)
    step = jnp.dot(jnp.dot(left_root, grad, precision=highest), right_root, precision=highest)
    return (grad_rows, new_left, new_right, weight_rows - shampoo_rate * step)


def shards(
    features,
    nbr_index,
    nbr_mask,
    send_rows,
    send_count,
    labels,
    seed_mask,
    w_first,
    w_rest,
    w_head,
    biases,
    stat_big,
    root_big,
    stat_mid,
    root_mid,
    stat_sq,
    root_sq,
    stat_hr,
    root_hr,
    bias_m,
    bias_v,
):
    hidden = w_rest.shape[2]
    peers = send_rows.shape[2]
    cap = send_rows.shape[3]
    send_list = send_rows.reshape(-1)
    valid = (jnp.arange(cap)[None, :] < send_count.reshape(peers, 1)).astype(jnp.bfloat16)
    weights = [w_first, w_rest[0], w_rest[1]]
    state = features[0].astype(jnp.float32)
    kept = []
    for level in range(3):
        state, saved = layer_forward(
            state,
            weights[level],
            biases[level * hidden : (level + 1) * hidden],
            nbr_index[0, level],
            nbr_mask[0, level],
            send_list,
            valid,
        )
        kept.append(saved)
    seeds = labels.shape[1]
    top = state[:seeds].astype(jnp.bfloat16)
    head_low_w = w_head.astype(jnp.bfloat16)
    logits = jnp.dot(top, head_low_w, preferred_element_type=jnp.float32) + biases[3 * hidden :]
    lse = jax.nn.logsumexp(logits, axis=1)
    onehot = (labels[0][:, None] == jnp.arange(logits.shape[1])[None, :]).astype(jnp.float32)
    picked = jnp.sum(logits * onehot, axis=1)
    seed_weight = seed_mask[0].astype(jnp.float32)
    loss_sum, seed_total = lax.psum(
        (jnp.sum((lse - picked) * seed_weight), jnp.sum(seed_weight)), ("dom", "rep")
    )
    grad_logits = (
        (jnp.exp(logits - lse[:, None]) - onehot) * (seed_weight / seed_total)[:, None]
    ).astype(jnp.bfloat16)
    grad_head = jnp.einsum("sh,sc->hc", top, grad_logits, preferred_element_type=jnp.float32)
    grad_hbias = jnp.sum(grad_logits.astype(jnp.float32), axis=0)
    grad_head, grad_hbias = (grad_head, grad_hbias)
    grad_top = jnp.einsum("sc,hc->sh", grad_logits, head_low_w, preferred_element_type=jnp.float32)
    grad_state = jnp.zeros(state.shape, jnp.float32).at[:seeds].set(grad_top)
    results = [None, None, None]
    for level in (2, 1, 0):
        grad_w, grad_b, grad_state = layer_backward(
            grad_state, weights[level], kept[level], send_list, valid, level > 0
        )
        results[level] = (grad_w, grad_b)
    grad_bias = jnp.concatenate([results[0][1], results[1][1], results[2][1], grad_hbias])
    grad_one, grad_two, grad_three = (results[0][0], results[1][0], results[2][0])
    grad_one, grad_two, grad_three, grad_head, grad_bias = lax.psum(
        (grad_one, grad_two, grad_three, grad_head, grad_bias), ("dom", "rep")
    )
    everything = (grad_one, grad_two, grad_three, grad_head, grad_bias)
    grad_norm = jnp.sqrt(sum((jnp.sum(g * g) for g in everything)))
    factor = clip_limit / jnp.maximum(grad_norm, clip_limit)
    grad_one, grad_two, grad_three, grad_head, grad_bias = [g * factor for g in everything]
    part = lax.axis_index("rep")
    head_rows = stat_sq.shape[1]
    head_root_rows = lax.dynamic_slice_in_dim(root_sq[3], part * head_rows, head_rows, 0)
    g_first, l_first, r_first, n_first = shampoo(
        grad_one, w_first, stat_big, root_big, stat_sq[0], root_sq[0], part, True
    )
    g_mid0, l_mid0, r_mid0, n_mid0 = shampoo(
        grad_two, w_rest[0], stat_mid[0], root_mid[0], stat_sq[1], root_sq[1], part, True
    )
    g_mid1, l_mid1, r_mid1, n_mid1 = shampoo(
        grad_three, w_rest[1], stat_mid[1], root_mid[1], stat_sq[2], root_sq[2], part, True
    )
    g_head, l_head, r_head, n_head = shampoo(
        grad_head, w_head, stat_sq[3], head_root_rows, stat_hr, root_hr, part, False
    )
    new_m = beta_one * bias_m + (1.0 - beta_one) * grad_bias
    new_v = beta_two * bias_v + (1.0 - beta_two) * grad_bias * grad_bias
    m_hat = new_m / (1.0 - beta_one**STEP)
    v_hat = new_v / (1.0 - beta_two**STEP)
    new_b = biases - bias_rate * (m_hat / (jnp.sqrt(v_hat) + adam_eps) + weight_decay * biases)
    new_rest = jnp.stack([n_mid0, n_mid1])
    return (
        loss_sum,
        seed_total,
        grad_norm,
        g_first,
        jnp.stack([g_mid0, g_mid1]),
        g_head,
        new_m,
        new_v,
        l_first,
        jnp.stack([l_mid0, l_mid1]),
        jnp.stack([r_first, r_mid0, r_mid1, l_head]),
        r_head,
        n_first,
        new_rest,
        n_head,
        new_b,
        n_first.astype(jnp.bfloat16),
        new_rest.astype(jnp.bfloat16),
        n_head.astype(jnp.bfloat16),
    )


def solution(mesh):
    placed = (
        P("rep", "dom", None),
        P("rep", None, "dom", None),
        P("rep", None, "dom", None),
        P("rep", "dom", None, None),
        P("rep", "dom", None),
        P("rep", "dom"),
        P("rep", "dom"),
        P(),
        P(),
        P(),
        P(),
        P("rep", None),
        P("rep", None),
        P(None, "rep", None),
        P(None, "rep", None),
        P(None, "rep", None),
        P(),
        P(),
        P(),
        P(),
        P(),
    )
    return jax.shard_map(
        shards,
        mesh=mesh,
        in_specs=placed,
        out_specs=(
            P(),
            P(),
            P(),
            P("rep", None),
            P(None, "rep", None),
            P("rep", None),
            P(),
            P(),
            P("rep", None),
            P(None, "rep", None),
            P(None, "rep", None),
            P(),
            P("rep", None),
            P(None, "rep", None),
            P("rep", None),
            P(),
            P("rep", None),
            P(None, "rep", None),
            P("rep", None),
        ),
        check_vma=False,
    )
```

profile of v0, /device:TPU:1, one launch (start us, length us, event | category | flops | bytes accessed | tf_op | source)
XLA Modules:
  0.0 1209.1 jit_solution(13326624740624876570)
XLA Ops:
  23.7 280.0 %while.44 = (s32[]{:T(128)}, bf16[2048,2304]{1,0:T(8,128)(2,1)}, s32[2048,25]{0,1:T(8,128)S(1)}, bf16[2048,25]{0,1:T(8,128)(2,1)S(1)}, s32[]{:T(128)}, /*index=5*/s32[]{:T(128)}) while((s32[]{:T(128)}, bf16[2048,2304]{1,0:T(8,128)(2,1)}, s32[2048,25]{0,1:T(8,128)S(1)}, bf16[2048,25]{0,1:T(8,128)(2,1)S(1)}, s32[]{:T(128)}, ...), condition=%wide.region_5.6_spmd.clone, body=%wide.region_4.5_spmd.clone.sunk | while | flops 33030148 | bytes 18911324 | solution.py:36
  30.4 11.3 fusion.193
  41.8 11.3 fusion.193
  121.5 11.3 fusion.193
  132.9 11.3 fusion.193
  144.3 11.3 fusion.193
  155.7 11.3 fusion.193
  167.1 11.3 fusion.193
  178.5 11.3 fusion.193
  189.9 11.3 fusion.193
  201.3 11.3 fusion.193
  303.8 282.1 %while.43 = (s32[]{:T(128)}, bf16[2048,2304]{1,0:T(8,128)(2,1)}, s32[2048,25]{0,1:T(8,128)S(1)}, bf16[2048,25]{0,1:T(8,128)(2,1)S(1)}, s32[]{:T(128)}, /*index=5*/s32[]{:T(128)}) while((s32[]{:T(128)}, bf16[2048,2304]{1,0:T(8,128)(2,1)}, s32[2048,25]{0,1:T(8,128)S(1)}, bf16[2048,25]{0,1:T(8,128)(2,1)S(1)}, s32[]{:T(128)}, ...), condition=%wide.region_1.2_spmd.clone, body=%wide.region_0.1_spmd.clone.sunk | while | flops 33030148 | bytes 18911324 | solution.py:36
  310.6 11.4 fusion.192
  322.1 11.4 fusion.192
  333.5 11.4 fusion.192
  345.0 11.4 fusion.192
  356.5 11.4 fusion.192
  368.0 11.4 fusion.192
  379.4 11.4 fusion.192
  390.9 11.4 fusion.192
  402.4 11.4 fusion.192
  413.8 11.4 fusion.192
  425.3 11.4 fusion.192
  436.8 11.4 fusion.192
  448.3 11.4 fusion.192
  459.7 11.4 fusion.192
  471.2 11.4 fusion.192
  482.7 11.4 fusion.192
  494.1 11.4 fusion.192
  505.6 11.4 fusion.192
  517.1 11.4 fusion.192
  528.6 11.4 fusion.192
  540.0 11.4 fusion.192
  551.5 11.4 fusion.192
  563.0 11.4 fusion.192
  574.5 11.4 fusion.192
  637.4 282.1 %while.45 = (s32[]{:T(128)}, bf16[2048,2304]{1,0:T(8,128)(2,1)}, s32[2048,25]{0,1:T(8,128)S(1)}, bf16[2048,25]{0,1:T(8,128)(2,1)S(1)}, s32[]{:T(128)}, /*index=5*/s32[]{:T(128)}) while((s32[]{:T(128)}, bf16[2048,2304]{1,0:T(8,128)(2,1)}, s32[2048,25]{0,1:T(8,128)S(1)}, bf16[2048,25]{0,1:T(8,128)(2,1)S(1)}, s32[]{:T(128)}, ...), condition=%wide.region_9.11_spmd.clone, body=%wide.region_8.10_spmd.clone.sunk | while | flops 33030148 | bytes 18911324 | solution.py:36
  644.3 11.4 fusion.194
  655.8 11.4 fusion.194
  667.2 11.4 fusion.194
  678.7 11.4 fusion.194
  690.2 11.4 fusion.194
  701.7 11.4 fusion.194
  713.1 11.4 fusion.194
  724.6 11.4 fusion.194
  736.1 11.4 fusion.194
  747.5 11.4 fusion.194
  759.0 11.4 fusion.194
  770.5 11.4 fusion.194
  782.0 11.4 fusion.194
  793.4 11.4 fusion.194
  804.9 11.4 fusion.194
  816.4 11.4 fusion.194
  827.9 11.4 fusion.194
  839.3 11.4 fusion.194
  850.8 11.4 fusion.194
  862.3 11.4 fusion.194
  873.8 11.4 fusion.194
  885.2 11.4 fusion.194
  896.7 11.4 fusion.194
  908.2 11.4 fusion.194
  919.6 42.7 %psum.50 = f32[]{:T(128)} all-reduce(f32[]{:T(128)} %convert_reduce_fusion.4), channel_id=1, replica_groups=mesh['dom'=8,'rep'=4] {'dom','rep'}, use_global_device_ids=true, to_apply=%region_18.20 | all-reduce | flops 1 | bytes 8 | tf_op jit(solution)/shard_map/psum | solution.py:147
  1030.9 43.2 %all-reduce.1 = (f32[]{:T(128)}, f32[256,41]{0,1:T(8,128)S(1)}, f32[809]{0:T(1024)S(1)}) all-reduce(f32[]{:T(128)} %get-tuple-element.416, f32[256,41]{0,1:T(8,128)S(1)} %fusion.115, f32[809]{0:T(1024)S(1)} %pad_maximum_fusion.15), channel_id=1, replica_groups=mesh['dom'=8,'rep'=4] {'dom','rep'}, use_global_device_ids=true, to_apply=%region_16.18 | all-reduce | flops 11306 | bytes 90448 | tf_op jit(solution)/shard_map/psum | solution.py:147
  1075.3 91.8 %all-reduce.5.cloned.1.call-done = (f32[1204,256]{1,0:T(8,128)}, f32[512,256]{1,0:T(8,128)}, f32[512,256]{1,0:T(8,128)}) async-done(((f32[1204,256]{1,0:T(8,128)}, f32[512,256]{1,0:T(8,128)}, f32[512,256]{1,0:T(8,128)}), (f32[1204,256]{1,0:T(8,128)}, f32[512,256]{1,0:T(8,128)}, f32[512,256]{1,0:T(8,128)})) %all-reduce.5.cloned.1.call-update) | async-done | bytes 2281488 | tf_op jit(solution)/shard_map/psum | solution.py:166
  (399 shorter events, 349.8 us)
Async XLA Ops:
  7.2 1176.7 %copy-start = (f32[301,1204]{1,0:T(8,128)S(1)}, f32[301,1204]{1,0:T(8,128)}, u32[]{:S(2)}) copy-start(f32[301,1204]{1,0:T(8,128)} %param.43) | copy-start | bytes 4348852
  7.2 4.5 copy-start.30
  7.2 4.6 copy-start.39
  11.9 10.8 copy-start.34
  11.9 10.9 copy-start.22
  11.9 10.9 copy-start.23
  16.3 569.7 %all-to-all-start = ((bf16[8,32,602]{2,1,0:T(8,128)(2,1)}), bf16[8,32,602]{2,1,0:T(8,128)(2,1)S(1)}, u32[]{:S(2)}, u32[]{:S(2)}) async-start(bf16[8,32,602]{2,1,0:T(8,128)(2,1)} %select_multiply_fusion), calls=%async_computation | async-start | bytes 655360 | tf_op jit(solution)/shard_map/all_to_all | solution.py:46
  586.1 10.4 copy-start.14
  586.1 10.4 copy-start.29
  596.5 2.3 copy-start.42
  598.8 1.4 copy-start.1
  600.9 16.5 %copy-start.9 = (bf16[2048,256]{0,1:T(8,128)(2,1)}, bf16[2048,256]{0,1:T(8,128)(2,1)S(1)}, u32[]{:S(2)}) copy-start(bf16[2048,256]{0,1:T(8,128)(2,1)S(1)} %multiply_convert_fusion.1) | copy-start | bytes 3145732
  601.0 10.2 copy-start.38
  605.5 11.8 all-to-all-start.1
  617.4 6.7 copy-start.7
  617.4 6.7 copy-start.10
  624.1 1.4 copy-start.40
  625.6 1.4 copy-start.3
  634.1 328.2 %all-to-all-start.2 = ((bf16[8,32,256]{2,1,0:T(8,128)(2,1)}), bf16[8,32,256]{2,1,0:T(8,128)(2,1)S(1)}, u32[]{:S(2)}, u32[]{:S(2)}) async-start(bf16[8,32,256]{2,1,0:T(8,128)(2,1)} %broadcast_multiply_fusion.5), calls=%async_computation.2 | async-start | bytes 262144 | tf_op jit(solution)/shard_map/all_to_all | solution.py:46
  962.4 6.7 copy-start.11
  969.0 1.4 copy-start.41
  969.0 1.5 copy-start.26
  969.0 1.8 copy-start.37
  969.1 9.2 slice-start
  969.1 9.2 slice-start.1
  970.5 6.1 copy-start.31
  974.5 3.7 slice-start.2
  976.5 1.0 copy-start.12
  978.3 2.7 copy-start.6
  983.1 10.6 all-to-all-start.3
  993.7 4.5 copy-start.4
  993.9 8.2 slice-start.3
  993.9 8.2 slice-start.4
  1000.3 1.0 copy-start.13
  1001.3 1.2 slice-start.5
  1002.5 2.7 copy-start.5
  1007.4 11.8 all-to-all-start.4
  1012.8 154.3 %all-reduce.5.cloned.1.call-start = ((), (), s32[]{:S(2)}) async-start(), calls=%async_computation.5 | async-start | bytes 4571136 | tf_op jit(solution)/shard_map/psum | solution.py:166
  1019.3 4.4 copy-start.2
  1023.7 2.0 copy-start.15
  1023.7 2.4 copy-start.43
  1167.1 4.1 copy-start.17
  1167.1 8.2 copy-start.8
  1171.2 5.2 copy-start.16
  1175.3 1.0 copy-start.18
  1175.3 1.2 copy-start.25
  1176.4 1.5 copy-start.27
  1176.4 2.8 copy-start.24
  1179.2 3.9 copy-start.32
  1182.7 5.6 copy-start.21
  1182.7 9.6 copy-start.20
  1182.8 8.0 copy-start.28
  1183.9 6.9 slice-start.6
  1183.9 7.8 copy-start.35
  1183.9 7.8 copy-start.36
  1183.9 8.4 copy-start.19
  1195.0 4.2 copy-start.33
Sparse Core Ops, SparseCore 0:
  1028.8 138.1 all-reduce.4
where the time goes:
time: 1230 us; the launch traced here: 1210 us
  other arithmetic  866 us (70%)
  waiting for transfers between devices  97.3 us (8%)
  blocking collectives  85.9 us (7%)
  matrix products  75.5 us (6%)
  local copies, waits for them, and re-layouts  38.9 us (3%)
  starting transfers between devices  25.2 us (2%)
  between operations  20 us (2%)
    add x75, other arithmetic, add_slot(): return total + (picks == column_ids).astype(jnp.bfloat16) * weight  840 us
    psum x1, waiting for transfers between devices, shards(): lax.psum((grad_one, grad_two, grad_three, grad_head, grad_bias), ('dom',...  91.8 us
    psum x2, blocking collectives, shards(): lax.psum((jnp.sum((lse - picked) * seed_weight), jnp.sum(seed_weight)), (...  85.9 us
  transfers between devices with their start and end apart: 6, of which 2 were waited for; matrix products, arithmetic and copies ran while one was open for 71% of the time, Pallas kernels for 0%

commit v1 on v0

--- a/solution.py
+++ b/solution.py
@@ -1,10 +1,14 @@
+import functools
+
 import jax
 import jax.numpy as jnp
 from jax import lax
+from jax.experimental import pallas as pl
+from jax.experimental.pallas import tpu as pltpu
 from jax.sharding import PartitionSpec as P
 
 STEP = 5
-
+FAN_REST = 10
 
 clip_limit = 0.0001
 decay = 0.5
@@ -15,15 +19,633 @@
 weight_decay = 0.01
 adam_eps = 1e-08
 norm_eps = 1e-06
+MASKED = 8192
+
+bf16 = jnp.bfloat16
+f32 = jnp.float32
+i32 = jnp.int32
+MESH = pl.DeviceIdType.MESH
+
+
+def nn(a, b):
+    return jnp.dot(a, b, preferred_element_type=f32)
+
+
+def nt(a, b):
+    return lax.dot_general(a, b, (((1,), (1,)), ((), ())), preferred_element_type=f32)
+
+
+def flip(a):
+    return a.astype(f32).T.astype(a.dtype)
+
+
+def round_up(a, b):
+    return (a + b - 1) // b * b
+
+
+def gelu_parts(z):
+    scale = 0.7978845608028654
+    square = z * z
+    t = jnp.tanh(scale * (z + 0.044715 * (z * square)))
+    half = 0.5 * (1.0 + t)
+    act = z * half
+    slope = half + 0.5 * z * (1.0 - t * t) * (scale * (1.0 + 3.0 * 0.044715 * square))
+    root = lax.rsqrt(jnp.sum(act * act, axis=0, keepdims=True) + norm_eps)
+    return act, slope, root
+
+
+def pull_back(act, slope, root, grad):
+    dot = jnp.sum(act * grad, axis=0, keepdims=True)
+    return (slope * (root * grad - act * (root * root * root * dot))).astype(bf16)
+
+
+def graph_kernel(
+    peers, cap, seeds,
+    c1, c2, c3, ids, col, lab, xt, w1, wr, wht, bias,
+    g_out, s_out,
+    joined, gathered, pick, chosen, far2, cblk, cinc, ctmp, crow, lrow, rdeg, lcode,
+    w1t, act1, slope1, root1, h1t, ob0, ib0, obs, ibs, gl, rc, acc, sbuf, rx, ry, rz, gout,
+    ssend, srecv, szv,
+    send_sem, recv_sem, red_send, red_recv,
+):
+    fin, nodes = xt.shape
+    hidden = w1.shape[1]
+    finp = round_up(fin, 16)
+    slots = peers * cap
+    table = nodes + slots
+    groups = table // 128
+    span = ids.shape[1]
+    local = span - slots
+    me = lax.axis_index("dom")
+    rep = lax.axis_index("rep")
+    core = lax.rem(rep, 2)
+    xpos = rep // 2
+    ypos = lax.rem(me, 2)
+    zpos = me // 2
+    nz = peers // 2
+
+    barrier = pltpu.get_barrier_semaphore()
+    for off in range(1, peers):
+        pl.semaphore_signal(barrier, inc=1, device_id={"dom": lax.rem(me + off, peers)}, device_id_type=MESH)
+    mate_c = xpos * 2 + (1 - core)
+    mate_x = (1 - xpos) * 2 + core
+    for mate in (mate_c, mate_x):
+        pl.semaphore_signal(barrier, inc=1, device_id={"rep": mate}, device_id_type=MESH)
+
+    def exchange(stage, src, dst):
+        copies = []
+        for off in range(1, peers):
+            peer = lax.rem(me + off, peers)
+            copies.append(
+                pltpu.make_async_remote_copy(
+                    src_ref=src.at[pl.ds(pl.multiple_of(peer * cap, cap), cap)],
+                    dst_ref=dst.at[pl.ds(pl.multiple_of(me * cap, cap), cap)],
+                    send_sem=send_sem.at[stage, off - 1],
+                    recv_sem=recv_sem.at[stage, off - 1],
+                    device_id={"dom": peer},
+                    device_id_type=MESH,
+                )
+            )
+        for c in copies:
+            c.start()
+        return copies
+
+    def finish(copies):
+        for c in copies:
+            c.wait()
+
+    mine = pl.ds(pl.multiple_of(me * cap, cap), cap)
+
+    pick[...] = jnp.where(
+        col[...] == lax.broadcasted_iota(i32, (slots, nodes), 1), 1.0, 0.0
+    ).astype(bf16)
+    joined[finp - 16 : finp, :] = jnp.zeros((16, nodes), bf16)
+    joined[0:fin, :] = xt[...]
+    ob0[:, finp:] = jnp.zeros((slots, ob0.shape[1] - finp), bf16)
+    ob0[:, 0:finp] = nt(pick[...], joined[0:finp, :]).astype(bf16)
+    ib0[mine, :] = jnp.zeros((cap, ib0.shape[1]), bf16)
+    for k in range(4):
+        ibs[k, mine, :] = jnp.zeros((cap, hidden), bf16)
+    pl.semaphore_wait(barrier, peers - 1 + 2)
+    sent = exchange(0, ob0, ib0)
+
+    wpad = jnp.concatenate(
+        [w1[0:fin, :], jnp.zeros((finp - fin, hidden), f32), w1[fin : 2 * fin, :], jnp.zeros((finp - fin, hidden), f32)],
+        axis=0,
+    )
+    w1t[...] = wpad.T.astype(bf16)
+    w2 = wr[0].astype(bf16)
+    w3 = wr[1].astype(bf16)
+    bcol = bias[...].T
+
+    def bias_col(level):
+        return jnp.concatenate([bcol[:, 2 * level : 2 * level + 1], bcol[:, 2 * level + 1 : 2 * level + 2]], axis=0)
+
+    pad = jnp.full((32 - c1.shape[0], 128), float(MASKED), f32)
+    for c in range(nodes // 128):
+        blk = jnp.concatenate([c1[:, c * 128 : (c + 1) * 128].astype(f32), pad], axis=0)
+        ctmp[c * 128 : (c + 1) * 128, 0:32] = blk.T
+    rdeg[0:1, :] = 1.0 / jnp.maximum(jnp.sum((c1[...] < MASKED).astype(f32), axis=0, keepdims=True), 1.0)
+    ngroups = nodes // 8
+    lane = lax.broadcasted_iota(i32, (ngroups, 256), 1)
+    code = jnp.zeros((ngroups, 256), f32)
+    for n in range(8):
+        piece = ctmp[pl.ds(n, ngroups, stride=8), :]
+        piece = jnp.concatenate([piece, piece], axis=1)
+        piece = pltpu.roll(piece, n * 32, 1) if n else piece
+        code = jnp.where((lane >> 5) == n, piece, code)
+    code = code.astype(i32)
+    crow[...] = ((code >> 7) * 8 + (lane >> 5)).astype(f32)
+    lrow[...] = (code & 127).astype(f32)
+
+    list_row = ids[0:1, :].astype(f32)
+
+    def one_hot_rows(b, _):
+        start = pl.multiple_of(b * 256, 256)
+        row = (lax.broadcasted_iota(i32, (256, span), 0) + b * 256).astype(f32)
+        chosen[pl.ds(start, 256), 0:span] = jnp.where(row == list_row, 1.0, 0.0).astype(bf16)
+        return 0
+
+    lax.fori_loop(0, nodes // 256, one_hot_rows, 0)
+    code2 = c2[...]
+    parts = jnp.concatenate([(code2 >> 7), (code2 & 127)], axis=0).astype(f32).astype(bf16)
+    found = nn(parts, chosen[:, 0:span])
+    lcode[...] = found[0:16] * 128.0 + found[16:32]
+    live = (lcode[0:FAN_REST, :] < float(MASKED)).astype(f32)
+    rdeg2 = 1.0 / jnp.maximum(jnp.sum(live, axis=0, keepdims=True), 1.0)
+
+    rows_a = lax.broadcasted_iota(i32, (groups * 8, 256), 0).astype(f32)
+    rows_b = lax.broadcasted_iota(i32, (128, 256), 0).astype(f32)
+
+    def list_counts(first, size):
+        row = (lax.broadcasted_iota(i32, (size, span), 0) + first).astype(f32)
+        total = jnp.where(row == lcode[0:1, :], 1.0, 0.0)
+        for k in range(1, FAN_REST):
+            total = total + jnp.where(row == lcode[k : k + 1, :], 1.0, 0.0)
+        return total.astype(bf16)
+
+    def own_block(b, _):
+        start = pl.multiple_of(b * 256, 256)
+        for p in range(16):
+            pair = []
+            for half in range(2):
+                g = b * 32 + p * 2 + half
+                left = jnp.where(rows_a == crow[pl.ds(g, 1), :], 1.0, 0.0).astype(bf16)
+                right = jnp.where(rows_b == lrow[pl.ds(g, 1), :], 1.0, 0.0).astype(bf16)
+                pair.append(nt(left, right))
+            for a in range(groups):
+                tile = jnp.concatenate([pair[0][a * 8 : (a + 1) * 8], pair[1][a * 8 : (a + 1) * 8]], axis=0)
+                cblk[p * 16 : (p + 1) * 16, a * 128 : (a + 1) * 128] = tile.astype(bf16)
+        cinc[pl.ds(start, 256), :] = cblk[:, nodes:]
+        gathered[:, pl.ds(start, 256)] = nt(joined[0:finp, :], cblk[:, 0:nodes])
+        for q in range(8):
+            chosen[pl.ds(pl.multiple_of(start + q * 32, 32), 32), span:] = list_counts(start + q * 32, 32)
+        return 0
+
+    lax.fori_loop(0, nodes // 256, own_block, 0)
+    for q in range(slots // 32):
+        far2[q * 32 : (q + 1) * 32, :] = list_counts(nodes + q * 32, 32)
+    code3 = c3[...].astype(f32)
+    row3 = (lax.broadcasted_iota(i32, (slots, 128), 0) + nodes).astype(f32)
+    far3 = jnp.zeros((slots, 128), f32)
+    for k in range(FAN_REST):
+        far3 = far3 + jnp.where(row3 == code3[k : k + 1, :], 1.0, 0.0)
+    far3 = far3.astype(bf16)
+    rdeg3 = 1.0 / jnp.maximum(jnp.sum((code3[0:FAN_REST] < float(MASKED)).astype(f32), axis=0, keepdims=True), 1.0)
+    r_id = lax.broadcasted_iota(i32, (local, 256), 0)
+    l_id = lax.broadcasted_iota(i32, (local, 256), 1)
+    is_self = (l_id < seeds) & (r_id == l_id + FAN_REST * seeds)
+    is_nbr = (l_id >= 128) & (l_id < 128 + seeds) & (r_id < FAN_REST * seeds) & (lax.rem(r_id, seeds) == l_id - 128)
+    spread = jnp.where(is_self | is_nbr, 1.0, 0.0).astype(bf16)
+    keep_row = ids[1:2, :].astype(f32)
+
+    finish(sent)
+    ibt = flip(ib0[...])[0:finp, :]
+    b1 = bias_col(0)
+
+    def layer_one(b, _):
+        blk = pl.ds(pl.multiple_of(b * 256, 256), 256)
+        total = gathered[:, blk] + nt(ibt, cinc[blk, :])
+        joined[finp:, blk] = (total * rdeg[0:1, blk]).astype(bf16)
+        z = nn(w1t[...], joined[:, blk]) + b1
+        act, slope, root = gelu_parts(z)
+        act1[:, blk] = act
+        slope1[:, blk] = slope
+        root1[0:1, blk] = root
+        h1t[:, blk] = (act * root).astype(bf16)
+        return 0
+
+    lax.fori_loop(0, nodes // 256, layer_one, 0)
+    obs[0] = nt(pick[...], h1t[...]).astype(bf16)
+    sent = exchange(1, obs.at[0], ibs.at[0])
+
+    own2 = nn(h1t[...], chosen[...])
+    w2t = flip(w2)
+    finish(sent)
+    agg2 = (own2[:, span:] + nn(flip(ibs[0]), far2[...])) * rdeg2
+    joined2 = jnp.concatenate([own2[:, 0:span].astype(bf16), agg2.astype(bf16)], axis=0)
+    act2, slope2, root2 = gelu_parts(nn(w2t, joined2) + bias_col(1))
+    h2 = act2 * root2 * keep_row
+    obs[1] = h2[:, 0:slots].T.astype(bf16)
+    sent = exchange(2, obs.at[1], ibs.at[1])
+
+    near3 = nn(h2[:, slots:].astype(bf16), spread)
+    w3t = flip(w3)
+    finish(sent)
+    agg3 = (near3[:, 128:] + nn(flip(ibs[1]), far3)) * rdeg3
+    joined3 = jnp.concatenate([near3[:, 0:128].astype(bf16), agg3.astype(bf16)], axis=0)
+    act3, slope3, root3 = gelu_parts(nn(w3t, joined3) + bias_col(2))
+    top = (act3 * root3).astype(bf16)
+
+    classes = wht.shape[0]
+    classp = round_up(classes, 16)
+    wht_low = jnp.concatenate([wht[...], jnp.zeros((classp - classes, hidden), f32)], axis=0).astype(bf16)
+    class_id = lax.broadcasted_iota(i32, (classp, 128), 0)
+    seed_lane = lax.broadcasted_iota(i32, (1, 128), 1) < seeds
+    weight = jnp.where(seed_lane, lab[1:2, :].astype(f32), 0.0)
+    logits = nn(wht_low, top) + bcol[0:classp, 6:7]
+    logits = jnp.where(class_id < classes, logits, -1e30)
+    peak = jnp.max(logits, axis=0, keepdims=True)
+    lse = peak + jnp.log(jnp.sum(jnp.exp(logits - peak), axis=0, keepdims=True))
+    hot = jnp.where(class_id == lab[0:1, :], 1.0, 0.0)
+    picked = jnp.sum(logits * hot, axis=0, keepdims=True)
+    loss = jnp.sum((lse - picked) * weight, axis=1, keepdims=True)
+    total = jnp.sum(weight, axis=1, keepdims=True)
+    dlog = ((jnp.exp(logits - lse) - hot) * weight).astype(bf16)
+    sc_lane = lax.broadcasted_iota(i32, (8, 128), 1)
+    ssend[0] = jnp.where(sc_lane == 0, loss, jnp.where(sc_lane == 1, total, 0.0))
+
+    seg_b = 0
+    seg_a = 4 * hidden
+    row_head = seg_a + 2 * finp
+    row_bias = row_head + classp
+
+    def put(row, value):
+        size = value.shape[0]
+        gl[0, row : row + size, :] = value[:, 0:128].astype(bf16)
+        gl[1, row : row + size, :] = value[:, 128:].astype(bf16)
+
+    ones = jnp.ones((16, 128), bf16)
+    put(row_head, nt(dlog, top))
+    bias_h = jnp.concatenate([nt(ones, dlog), jnp.zeros((16, hidden - classp), f32)], axis=1)
+    dtop = nn(wht_low.astype(f32).T.astype(bf16), dlog)
+
+    dz3 = pull_back(act3, slope3, root3, dtop)
+    dj3 = nn(w3, dz3)
+    dg3 = (dj3[hidden:] * rdeg3).astype(bf16)
+    obs[2] = nt(far3, dg3).astype(bf16)
+    sent = exchange(3, obs.at[2], ibs.at[2])
+    dloc = nt(jnp.concatenate([dj3[0:hidden].astype(bf16), dg3], axis=1), spread)
+    put(seg_b + 2 * hidden, nt(joined3, dz3))
+    bias_3 = nt(ones, dz3)
+    finish(sent)
+    dh2 = jnp.concatenate([ibs[2].astype(f32).T, dloc], axis=1) * keep_row
+
+    dz2 = pull_back(act2, slope2, root2, dh2)
+    dj2 = nn(w2, dz2)
+    dg2 = (dj2[hidden:] * rdeg2).astype(bf16)
+    obs[3] = nt(far2[...], dg2).astype(bf16)
+    sent = exchange(4, obs.at[3], ibs.at[3])
+    put(seg_b, nt(joined2, dz2))
+    bias_2 = nt(jnp.ones((16, span), bf16), dz2)
+    both = jnp.concatenate([dj2[0:hidden].astype(bf16), dg2], axis=1)
+    gathered[0:hidden, :] = nt(both, chosen[...])
+    finish(sent)
+    back = flip(ibs[3])
+
+    def layer_one_back(b, _):
+        blk = pl.ds(pl.multiple_of(b * 256, 256), 256)
+        grad = gathered[0:hidden, blk] + nn(back, pick[:, blk])
+        h1t[:, blk] = pull_back(act1[:, blk], slope1[:, blk], root1[0:1, blk], grad)
+        return 0
+
+    lax.fori_loop(0, nodes // 256, layer_one_back, 0)
+    step_rows = finp // 2
+
+    def first_grad(b, _):
+        start = pl.multiple_of(b * step_rows, 16)
+        value = nt(joined[pl.ds(start, step_rows), :], h1t[...])
+        to = pl.multiple_of(seg_a + b * step_rows, 16)
+        gl[0, pl.ds(to, step_rows), :] = value[:, 0:128].astype(bf16)
+        gl[1, pl.ds(to, step_rows), :] = value[:, 128:].astype(bf16)
+        return 0
+
+    lax.fori_loop(0, 4, first_grad, 0)
+    bias_1 = nt(jnp.ones((16, nodes), bf16), h1t[...])
+    line = lax.broadcasted_iota(i32, (16, hidden), 0)
+    put(
+        row_bias,
+        jnp.where(line == 0, bias_1, 0.0)
+        + jnp.where(line == 1, bias_2, 0.0)
+        + jnp.where(line == 2, bias_3, 0.0)
+        + jnp.where(line == 3, bias_h, 0.0),
+    )
+
+    used = []
+
+    def hop(src, dst, axis, who):
+        used.append(0)
+        k = len(used) - 1
+        return pltpu.make_async_remote_copy(
+            src_ref=src, dst_ref=dst, send_sem=red_send.at[k], recv_sem=red_recv.at[k],
+            device_id={axis: who}, device_id_type=MESH,
+        )
+
+    mate_y = zpos * 2 + (1 - ypos)
+
+    def z_mate(off):
+        return lax.rem(zpos + off, nz) * 2 + ypos
+
+    def go(*copies):
+        for c in copies:
+            c.start()
+        for c in copies:
+            c.wait()
+
+    def rows_of(start, size):
+        return pl.ds(pl.multiple_of(start, 16), size)
+
+    rows = gl.shape[1]
+    segments = ((seg_b, seg_a), (seg_a, rows - seg_a))
+
+    go(
+        hop(gl.at[1 - core], rc, "rep", mate_c),
+        hop(ssend.at[0], srecv.at[0], "rep", mate_c),
+    )
+    acc[...] = gl[core].astype(f32) + rc[...].astype(f32)
+    ssend[1] = ssend[0] + srecv[0]
+
+    copies = [hop(ssend.at[1], srecv.at[1], "rep", mate_x)]
+    for k, (base, size) in enumerate(segments):
+        half = size // 2
+        give = rows_of(base + (1 - xpos) * half, half)
+        at = slice(base // 2, base // 2 + half)
+        sbuf[at, :] = acc[give, :].astype(bf16)
+        copies.append(hop(sbuf.at[at], rx.at[at], "rep", mate_x))
+    go(*copies)
+    ssend[2] = ssend[1] + srecv[1]
+    copies = [hop(ssend.at[2], srecv.at[2], "dom", mate_y)]
+    for k, (base, size) in enumerate(segments):
+        half, quarter = size // 2, size // 4
+        keep = rows_of(base + xpos * half, half)
+        acc[keep, :] = acc[keep, :] + rx[base // 2 : base // 2 + half, :].astype(f32)
+        give = rows_of(base + xpos * half + (1 - ypos) * quarter, quarter)
+        at = slice(base // 4, base // 4 + quarter)
+        sbuf[at, :] = acc[give, :].astype(bf16)
+        copies.append(hop(sbuf.at[at], ry.at[at], "dom", mate_y))
+    go(*copies)
+    ssend[3] = ssend[2] + srecv[2]
+    szv[zpos] = ssend[3]
+    copies = []
+    for k, (base, size) in enumerate(segments):
+        half, quarter, piece = size // 2, size // 4, size // (4 * nz)
+        keep = rows_of(base + xpos * half + ypos * quarter, quarter)
+        acc[keep, :] = acc[keep, :] + ry[base // 4 : base // 4 + quarter, :].astype(f32)
+        at = slice(base // 4, base // 4 + quarter)
+        sbuf[at, :] = acc[keep, :].astype(bf16)
+        for off in range(1, nz):
+            to = lax.rem(zpos + off, nz)
+            copies.append(
+                hop(
+                    sbuf.at[rows_of(base // 4 + to * piece, piece)],
+                    rz.at[off - 1, base // (4 * nz) : base // (4 * nz) + piece],
+                    "dom",
+                    z_mate(off),
+                )
+            )
+    for off in range(1, nz):
+        copies.append(hop(ssend.at[3], szv.at[zpos], "dom", z_mate(off)))
+    go(*copies)
+    s_out[...] = szv[0] + szv[1] + szv[2] + szv[3]
+    copies = []
+    for k, (base, size) in enumerate(segments):
+        half, quarter, piece = size // 2, size // 4, size // (4 * nz)
+        here = rows_of(base + xpos * half + ypos * quarter + zpos * piece, piece)
+        got = slice(base // (4 * nz), base // (4 * nz) + piece)
+        value = acc[here, :]
+        for off in range(1, nz):
+            value = value + rz[off - 1, got, :].astype(f32)
+        gout[core, here, :] = value.astype(bf16)
+        for off in range(1, nz):
+            copies.append(
+                hop(gout.at[core, here], gout.at[core, here], "dom", z_mate(off))
+            )
+    go(*copies)
+    copies = []
+    for k, (base, size) in enumerate(segments):
+        half, quarter = size // 2, size // 4
+        part = gout.at[core, rows_of(base + xpos * half + ypos * quarter, quarter)]
+        copies.append(hop(part, part, "dom", mate_y))
+    go(*copies)
+    copies = []
+    for k, (base, size) in enumerate(segments):
+        half = size // 2
+        part = gout.at[core, rows_of(base + xpos * half, half)]
+        copies.append(hop(part, part, "rep", mate_x))
+    go(*copies)
+    go(hop(gout.at[core], gout.at[core], "rep", mate_c))
+    g_out[:, 0:128] = gout[0]
+    g_out[:, 128:] = gout[1]
+
+
+def summed_gradients(peers, cap, seeds, c1, c2, c3, ids, col, lab, xt, w1, wr, wht, bias):
+    fin, nodes = xt.shape
+    hidden = w1.shape[1]
+    finp = round_up(fin, 16)
+    wide = round_up(fin, 128)
+    slots = peers * cap
+    span = ids.shape[1]
+    classp = round_up(wht.shape[0], 16)
+    rows = 4 * hidden + 2 * finp + classp + 16
+    nz = peers // 2
+    vmem = pltpu.VMEM
+    scratch = [
+        vmem((2 * finp, nodes), bf16),
+        vmem((finp, nodes), f32),
+        vmem((slots, nodes), bf16),
+        vmem((nodes, 2 * span), bf16),
+        vmem((slots, span), bf16),
+        vmem((256, nodes + slots), bf16),
+        vmem((nodes, slots), bf16),
+        vmem((nodes, 128), f32),
+        vmem((nodes // 8, 256), f32),
+        vmem((nodes // 8, 256), f32),
+        vmem((8, nodes), f32),
+        vmem((16, span), f32),
+        vmem((hidden, 2 * finp), bf16),
+        vmem((hidden, nodes), f32),
+        vmem((hidden, nodes), f32),
+        vmem((8, nodes), f32),
+        vmem((hidden, nodes), bf16),
+        vmem((slots, wide), bf16),
+        vmem((slots, wide), bf16),
+        vmem((4, slots, hidden), bf16),
+        vmem((4, slots, hidden), bf16),
+        vmem((2, rows, 128), bf16),
+        vmem((rows, 128), bf16),
+        vmem((rows, 128), f32),
+        vmem((rows // 2, 128), bf16),
+        vmem((rows // 2, 128), bf16),
+        vmem((rows // 4, 128), bf16),
+        vmem((nz - 1, rows // (4 * nz), 128), bf16),
+        vmem((2, rows, 128), bf16),
+        vmem((4, 8, 128), f32),
+        vmem((3, 8, 128), f32),
+        vmem((nz, 8, 128), f32),
+        pltpu.SemaphoreType.DMA((5, peers - 1)),
+        pltpu.SemaphoreType.DMA((5, peers - 1)),
+        pltpu.SemaphoreType.DMA((28,)),
+        pltpu.SemaphoreType.DMA((28,)),
+    ]
+    return pl.pallas_call(
+        functools.partial(graph_kernel, peers, cap, seeds),
+        out_shape=(
+            jax.ShapeDtypeStruct((rows, hidden), bf16),
+            jax.ShapeDtypeStruct((8, 128), f32),
+        ),
+        in_specs=[pl.BlockSpec(memory_space=vmem)] * 11,
+        out_specs=(pl.BlockSpec(memory_space=vmem), pl.BlockSpec(memory_space=vmem)),
+        scratch_shapes=scratch,
+        compiler_params=pltpu.CompilerParams(
+            collective_id=0, has_side_effects=True, vmem_limit_bytes=56 * 2**20
+        ),
+        name="graph_step",
+    )(c1, c2, c3, ids, col, lab, xt, w1, wr, wht, bias)
+
+
+def shampoo(grad, scale, weight, left, left_root, right, right_root, part, right_split):
+    high = lax.Precision.HIGH
+    count = left.shape[0]
+    grad_rows = lax.dynamic_slice_in_dim(grad, part * count, count, 0)
+    weight_rows = lax.dynamic_slice_in_dim(weight, part * count, count, 0)
+    square = (1.0 - decay) * scale * scale
+    new_left = decay * left + square * lax.dot_general(
+        grad_rows, grad, (((1,), (1,)), ((), ())), preferred_element_type=f32
+    )
+    if right_split:
+        cols = right.shape[0]
+        grad_cols = lax.dynamic_slice_in_dim(grad, part * cols, cols, 1)
+    else:
+        grad_cols = grad
+    new_right = decay * right + square * lax.dot_general(
+        grad_cols, grad, (((0,), (0,)), ((), ())), preferred_element_type=f32
+    )
+    step = jnp.dot(
+        jnp.dot(left_root, grad.astype(f32), precision=high), right_root, precision=high
+    )
+    return (
+        grad_rows.astype(f32) * scale,
+        new_left,
+        new_right,
+        weight_rows - (shampoo_rate * scale) * step,
+    )
+
+
+def shards(
+    features, nbr_index, nbr_mask, send_rows, send_count, labels, seed_mask,
+    w_first, w_rest, w_head, biases,
+    stat_big, root_big, stat_mid, root_mid, stat_sq, root_sq, stat_hr, root_hr, bias_m, bias_v,
+):
+    hidden = w_rest.shape[2]
+    peers = send_rows.shape[2]
+    cap = send_rows.shape[3]
+    nodes, fin = features.shape[1], features.shape[2]
+    seeds = labels.shape[1]
+    classes = w_head.shape[1]
+    slots = peers * cap
+    finp = round_up(fin, 16)
+    classp = round_up(classes, 16)
+
+    codes = jnp.where(nbr_mask[0] == 1, nbr_index[0], MASKED)
+    codes = jnp.swapaxes(codes, 1, 2)
+    c1 = codes[0]
+    c2 = codes[1, 0:16]
+    c3 = codes[2, 0:16, 0:128]
+    valid = jnp.arange(cap)[None, :] < send_count.reshape(peers, 1)
+    send = send_rows.reshape(peers, cap)
+    col = jnp.where(valid, send, -1).reshape(slots, 1)
+    around = c3[0:FAN_REST, 0:seeds].reshape(-1)
+    own = around < nodes
+    local = round_up(seeds * (FAN_REST + 1), 256)
+    fill = local - seeds * (FAN_REST + 1)
+    ids = jnp.stack(
+        [
+            jnp.concatenate(
+                [
+                    send.reshape(-1),
+                    jnp.where(own, around, -1),
+                    jnp.arange(seeds, dtype=i32),
+                    jnp.full((fill,), -1, i32),
+                ]
+            ),
+            jnp.concatenate(
+                [
+                    valid.reshape(-1).astype(i32),
+                    own.astype(i32),
+                    jnp.ones((seeds,), i32),
+                    jnp.zeros((fill,), i32),
+                ]
+            ),
+        ]
+    )
+    lab = jnp.pad(jnp.stack([labels[0], seed_mask[0]]), ((0, 0), (0, 128 - seeds)))
+    xt = jnp.swapaxes(features[0], 0, 1)
+    bias = jnp.pad(biases, (0, 1024 - biases.shape[0])).reshape(8, 128)
+    g_all, scalars = summed_gradients(
+        peers, cap, seeds, c1, c2, c3, ids, col, lab, xt, w_first, w_rest, w_head.T, bias
+    )
+    loss_sum, seed_total = scalars[0, 0], scalars[0, 1]
+    rest = 4 * hidden
+    g_two, g_three = g_all[0 : 2 * hidden], g_all[2 * hidden : rest]
+    g_one = jnp.concatenate([g_all[rest : rest + fin], g_all[rest + finp : rest + finp + fin]])
+    at = rest + 2 * finp
+    g_top = g_all[at : at + classes].T
+    at = at + classp
+    g_bias = jnp.concatenate([g_all[at : at + 3].reshape(-1), g_all[at + 3, 0:classes]]).astype(f32)
+    wide = g_all.astype(f32)
+    grad_norm = jnp.sqrt(jnp.sum(wide * wide)) / seed_total
+    scale = clip_limit / jnp.maximum(grad_norm, clip_limit) / seed_total
+    grad_bias = g_bias * scale
+    part = lax.axis_index("rep")
+    head_rows = stat_sq.shape[1]
+    head_root_rows = lax.dynamic_slice_in_dim(root_sq[3], part * head_rows, head_rows, 0)
+    g_first, l_first, r_first, n_first = shampoo(
+        g_one, scale, w_first, stat_big, root_big, stat_sq[0], root_sq[0], part, True
+    )
+    g_mid0, l_mid0, r_mid0, n_mid0 = shampoo(
+        g_two, scale, w_rest[0], stat_mid[0], root_mid[0], stat_sq[1], root_sq[1], part, True
+    )
+    g_mid1, l_mid1, r_mid1, n_mid1 = shampoo(
+        g_three, scale, w_rest[1], stat_mid[1], root_mid[1], stat_sq[2], root_sq[2], part, True
+    )
+    g_head, l_head, r_head, n_head = shampoo(
+        g_top, scale, w_head, stat_sq[3], head_root_rows, stat_hr, root_hr, part, False
+    )
+    new_m = beta_one * bias_m + (1.0 - beta_one) * grad_bias
+    new_v = beta_two * bias_v + (1.0 - beta_two) * grad_bias * grad_bias
+    m_hat = new_m / (1.0 - beta_one**STEP)
+    v_hat = new_v / (1.0 - beta_two**STEP)
+    new_b = biases - bias_rate * (m_hat / (jnp.sqrt(v_hat) + adam_eps) + weight_decay * biases)
+    new_rest = jnp.stack([n_mid0, n_mid1])
+    return (
+        loss_sum, seed_total, grad_norm,
+        g_first, jnp.stack([g_mid0, g_mid1]), g_head,
+        new_m, new_v,
+        l_first, jnp.stack([l_mid0, l_mid1]), jnp.stack([r_first, r_mid0, r_mid1, l_head]), r_head,
+        n_first, new_rest, n_head, new_b,
+        n_first.astype(bf16), new_rest.astype(bf16), n_head.astype(bf16),
+    )
+
+
 highest = lax.Precision.HIGHEST
 
 
-def activate(z):
+def plain_activate(z):
     act = jax.nn.gelu(z, approximate=True)
     return act * lax.rsqrt(jnp.sum(act * act, axis=-1, keepdims=True) + norm_eps)
 
 
-def count_matrix(nbr, mask, columns):
+def plain_counts(nbr, mask, columns):
     nodes, slots = nbr.shape
     column_ids = jnp.arange(columns, dtype=jnp.int32)[None, :]
     mask_low = mask.astype(jnp.bfloat16)
@@ -36,7 +658,7 @@
     return lax.fori_loop(0, slots, add_slot, jnp.zeros((nodes, columns), jnp.bfloat16))
 
 
-def layer_forward(h, weight, bias, nbr, mask, send_list, valid):
+def plain_forward(h, weight, bias, nbr, mask, send_list, valid):
     nodes, width = h.shape
     hb = h.astype(jnp.bfloat16)
     outgoing = (
@@ -45,19 +667,19 @@
     )
     incoming = lax.all_to_all(outgoing, "dom", split_axis=0, concat_axis=0, tiled=True)
     table = jnp.concatenate([hb, incoming.reshape(-1, width)], axis=0)
-    counts = count_matrix(nbr, mask, table.shape[0])
+    counts = plain_counts(nbr, mask, table.shape[0])
     degree = jnp.maximum(jnp.sum(mask, axis=1), 1).astype(jnp.float32)[:, None]
     gathered = jnp.dot(counts, table, preferred_element_type=jnp.float32)
     joined = jnp.concatenate([hb, (gathered / degree).astype(jnp.bfloat16)], axis=1)
     z = jnp.dot(joined, weight.astype(jnp.bfloat16), preferred_element_type=jnp.float32) + bias
-    return (activate(z), (joined, counts, degree, z))
-
-
-def layer_backward(grad_out, weight, kept, send_list, valid, need_input):
+    return (plain_activate(z), (joined, counts, degree, z))
+
+
+def plain_backward(grad_out, weight, kept, send_list, valid, need_input):
     joined, counts, degree, z = kept
     nodes = joined.shape[0]
     width = joined.shape[1] // 2
-    grad_z = jax.vjp(activate, z)[1](grad_out)[0].astype(jnp.bfloat16)
+    grad_z = jax.vjp(plain_activate, z)[1](grad_out)[0].astype(jnp.bfloat16)
     grad_w = jnp.einsum("nk,nh->kh", joined, grad_z, preferred_element_type=jnp.float32)
     grad_b = jnp.sum(grad_z.astype(jnp.float32), axis=0)
     if not need_input:
@@ -79,7 +701,7 @@
     return (grad_w, grad_b, grad_joined[:, :width] + grad_table[:nodes] + scattered)
 
 
-def shampoo(grad, weight, left, left_root, right, right_root, part, right_split):
+def plain_shampoo(grad, weight, left, left_root, right, right_root, part, right_split):
     count = left.shape[0]
     grad_rows = lax.dynamic_slice_in_dim(grad, part * count, count, 0)
     weight_rows = lax.dynamic_slice_in_dim(weight, part * count, count, 0)
@@ -94,7 +716,7 @@
     return (grad_rows, new_left, new_right, weight_rows - shampoo_rate * step)
 
 
-def shards(
+def plain_shards(
     features,
     nbr_index,
     nbr_mask,
@@ -126,7 +748,7 @@
     state = features[0].astype(jnp.float32)
     kept = []
     for level in range(3):
-        state, saved = layer_forward(
+        state, saved = plain_forward(
             state,
             weights[level],
             biases[level * hidden : (level + 1) * hidden],
@@ -157,7 +779,7 @@
     grad_state = jnp.zeros(state.shape, jnp.float32).at[:seeds].set(grad_top)
     results = [None, None, None]
     for level in (2, 1, 0):
-        grad_w, grad_b, grad_state = layer_backward(
+        grad_w, grad_b, grad_state = plain_backward(
             grad_state, weights[level], kept[level], send_list, valid, level > 0
         )
         results[level] = (grad_w, grad_b)
@@ -173,16 +795,16 @@
     part = lax.axis_index("rep")
     head_rows = stat_sq.shape[1]
     head_root_rows = lax.dynamic_slice_in_dim(root_sq[3], part * head_rows, head_rows, 0)
-    g_first, l_first, r_first, n_first = shampoo(
+    g_first, l_first, r_first, n_first = plain_shampoo(
         grad_one, w_first, stat_big, root_big, stat_sq[0], root_sq[0], part, True
     )
-    g_mid0, l_mid0, r_mid0, n_mid0 = shampoo(
+    g_mid0, l_mid0, r_mid0, n_mid0 = plain_shampoo(
         grad_two, w_rest[0], stat_mid[0], root_mid[0], stat_sq[1], root_sq[1], part, True
     )
-    g_mid1, l_mid1, r_mid1, n_mid1 = shampoo(
+    g_mid1, l_mid1, r_mid1, n_mid1 = plain_shampoo(
         grad_three, w_rest[1], stat_mid[1], root_mid[1], stat_sq[2], root_sq[2], part, True
     )
-    g_head, l_head, r_head, n_head = shampoo(
+    g_head, l_head, r_head, n_head = plain_shampoo(
         grad_head, w_head, stat_sq[3], head_root_rows, stat_hr, root_hr, part, False
     )
     new_m = beta_one * bias_m + (1.0 - beta_one) * grad_bias
@@ -223,45 +845,26 @@
         P("rep", "dom", None),
         P("rep", "dom"),
         P("rep", "dom"),
-        P(),
-        P(),
-        P(),
-        P(),
+        P(), P(), P(), P(),
         P("rep", None),
         P("rep", None),
         P(None, "rep", None),
         P(None, "rep", None),
         P(None, "rep", None),
-        P(),
-        P(),
-        P(),
-        P(),
-        P(),
-    )
+        P(), P(), P(), P(), P(),
+    )
+    small = mesh.shape["rep"] == 4 and mesh.shape["dom"] == 8
     return jax.shard_map(
-        shards,
+        shards if small else plain_shards,
         mesh=mesh,
         in_specs=placed,
         out_specs=(
-            P(),
-            P(),
-            P(),
-            P("rep", None),
-            P(None, "rep", None),
-            P("rep", None),
-            P(),
-            P(),
-            P("rep", None),
-            P(None, "rep", None),
-            P(None, "rep", None),
-            P(),
-            P("rep", None),
-            P(None, "rep", None),
-            P("rep", None),
-            P(),
-            P("rep", None),
-            P(None, "rep", None),
-            P("rep", None),
+            P(), P(), P(),
+            P("rep", None), P(None, "rep", None), P("rep", None),
+            P(), P(),
+            P("rep", None), P(None, "rep", None), P(None, "rep", None), P(),
+            P("rep", None), P(None, "rep", None), P("rep", None), P(),
+            P("rep", None), P(None, "rep", None), P("rep", None),
         ),
         check_vma=False,
     )

time: 1230 us -> 138 us (0.11); the launches traced: 1210 us -> 137 us
  other arithmetic: 866 us -> 13.3 us
  Pallas kernels: 0 us -> 99.4 us
  waiting for transfers between devices: 97.3 us -> 0 us
  blocking collectives: 85.9 us -> 0 us
  matrix products: 75.5 us -> 12.9 us
  local copies, waits for them, and re-layouts: 38.9 us -> 7.55 us
  starting transfers between devices: 25.2 us -> 0 us
  between operations: 20 us -> 4.18 us
    add x75 -> x0, other arithmetic: 840 us -> none  [add_slot(): return total + (picks == column_ids).astype(jnp.bfloat16) * weight]
    pallas_call x0 -> x1, Pallas kernels: none -> 99.4 us  [summed_gradients(): pl.pallas_call(functools.partial(graph_kernel, peers, cap, seeds), out_sh...]
    psum x1 -> x0, waiting for transfers between devices: 91.8 us -> none  [shards(): lax.psum((grad_one, grad_two, grad_three, grad_head, grad_bias), ('dom',...]
    psum x2 -> x0, blocking collectives: 85.9 us -> none  [shards(): lax.psum((jnp.sum((lse - picked) * seed_weight), jnp.sum(seed_weight)), (...]
    dot_general x34 -> x16, matrix products: 75.5 us -> 12.9 us  [the longest x4 4.38 us: shampoo(): jnp.dot(jnp.dot(left_root, grad.astype(f32), precision=high), right_root,...]
    all_to_all x5 -> x0, starting transfers between devices: 25.1 us -> none  [the longest x3 15.4 us: layer_forward(): lax.all_to_all(outgoing, 'dom', split_axis=0, concat_axis=0, tiled=True)]
    reduce_sum x14 -> x1, other arithmetic: 16.7 us -> 2.61 us  [shards(): grad_norm = jnp.sqrt(jnp.sum(wide * wide)) / seed_total]
  transfers between devices with their start and end apart: 6 -> 0, of which waited for: 2 -> 0; matrix products, arithmetic and copies ran while one was open for 71% -> 0% of each run, Pallas kernels for 0% -> 0%
where the time goes in v1:
time: 138 us; the launch traced here: 137 us
  Pallas kernels  99.4 us (72%)
  other arithmetic  13.3 us (10%)
  matrix products  12.9 us (9%)
  local copies, waits for them, and re-layouts  7.55 us (5%)
  between operations  4.18 us (3%)
    pallas_call x1, Pallas kernels, summed_gradients(): pl.pallas_call(functools.partial(graph_kernel, peers, cap, seeds), out_sh...  99.4 us
    dot_general x4, matrix products, shampoo(): jnp.dot(jnp.dot(left_root, grad.astype(f32), precision=high), right_root,...  4.38 us
    dot_general x4, matrix products, shampoo(): lax.dot_general(grad_rows, grad, (((1,), (1,)), ((), ())), preferred_elem...  3.3 us

profile of v1, /device:TPU:1, one launch (start us, length us, event | category | flops | bytes accessed | tf_op | source)
XLA Modules:
  0.0 137.3 jit_solution(9218301661218532038)
XLA Ops:
  0.7 0.0 copy-start
  0.7 0.0 copy-start.5
  0.7 0.8 pad_add_fusion.3
  1.5 0.6 pad.8.lab
  2.1 0.8 reshape_reshape.3
  2.9 1.3 pad_bitcast_fusion.bias
  4.1 0.7 iota_compare_fusion
  4.9 0.1 reshape.114
  4.9 0.2 lt.61
  5.1 0.8 reshape.115
  5.9 0.7 broadcast_select_fusion.col
  6.6 0.0 copy-done.5
  6.6 1.6 %fusion.20 = s32[3,25,2048]{2,1,0:T(8,128)S(1)} fusion(s32[1,3,2048,25]{2,0,3,1:T(1,128)S(1)} %copy-done.5, s32[1,3,2048,25]{2,0,3,1:T(1,128)} %param.23), kind=kLoop, calls=%fused_computation.34 | loop fusion | flops 307200 | bytes 1843200 | tf_op jit(solution)/shard_map/transpose | solution.py:560
  8.2 0.0 copy-start.9
  8.2 0.1 reshape.110
  8.3 0.1 pad_add_fusion.1
  8.4 0.6 pad_add_fusion.ids
  9.0 0.7 slice_bitcast_fusion.1.c2
  9.7 0.7 slice_bitcast_fusion.c1
  10.4 0.0 copy-done.9
  10.4 0.0 slice-start
  10.4 99.4 %graph_step.1 = (bf16[2304,256]{1,0:T(8,128)(2,1)}, f32[8,128]{1,0:T(8,128)}) custom-call(s32[25,2048]{1,0:T(8,128)} %slice_bitcast_fusion.c1, s32[16,2048]{1,0:T(8,128)} %slice_bitcast_fusion.1.c2, s32[16,128]{1,0:T(8,128)} %copy-done.9, s32[2,512]{1,0:T(2,128)} %pad_add_fusion.ids, s32[256,1]{1,0:T(8,128)} %broadcast_select_fusion.col, s32[2,128]{1,0:T(2,128)} %pad.8.lab, ...), custom_call_target="tpu_custom_call" | custom-call | tf_op jit(solution)/shard_map/graph_step/pallas_call | solution.py:500
  109.8 0.0 copy-start.1
  109.8 0.0 copy-start.6
  109.8 2.6 %multiply_reduce_fusion = f32[]{:T(128)} fusion(bf16[2304,256]{1,0:T(8,128)(2,1)} %get-tuple-element.22), kind=kLoop, calls=%fused_computation.2 | loop fusion | flops 1769471 | bytes 1179652 | tf_op jit(solution)/shard_map/reduce_sum | solution.py:606
  113.1 0.0 slice-done
  113.1 0.9 fusion.39
  114.0 1.3 fusion.67
  116.8 0.0 copy-done.1
  116.8 1.6 %fusion.69 = (bf16[64,41]{0,1:T(8,128)(2,1)}, f32[64,41]{0,1:T(8,128)}) fusion(f32[64,41]{1,0:T(8,128)S(1)} %fusion.39, f32[41,41]{1,0:T(8,128)} %param.39, f32[]{:T(128)S(6)} %div.23, f32[256,41]{0,1:T(8,128)} %param.30, s32[]{:T(128)S(6)} %select_n.46), kind=kOutput, calls=%fused_computation.112 | convolution fusion | flops 653376 | bytes 43468 | tf_op jit(solution)/shard_map/dot_general | solution.py:533
  118.4 1.3 multiply_subtract_fusion
  119.7 0.7 multiply_bitcast_fusion.2
  120.4 1.5 %fusion.19 = f32[41,41]{1,0:T(8,128)} fusion(f32[41,41]{1,0:T(8,128)} %param.38, f32[]{:T(128)S(6)} %mul.235, bf16[2304,256]{1,0:T(8,128)(2,1)S(1)} %copy-done.1), kind=kOutput, calls=%fused_computation.32 | convolution fusion | flops 865715 | bytes 38028 | tf_op jit(solution)/shard_map/dot_general | solution.py:530
  121.9 1.1 fusion.11
  123.0 0.0 copy-done.6
  123.0 0.3 fusion.27
  123.4 0.4 fusion.24
  123.7 0.0 copy-start.8
  123.8 0.8 copy-done.8
  124.7 0.3 fusion.17
  125.0 0.3 fusion.15
  125.3 0.0 copy-start.7
  125.3 0.4 fusion.13
  125.7 0.7 pad_maximum_fusion.3
  126.5 0.0 copy-done.7
  126.5 0.2 fusion.5
  126.7 0.2 fusion.3
  127.0 0.8 pad_maximum_fusion.1
  127.8 0.7 pad_maximum_fusion.2
  128.5 0.0 copy-start.4
  128.5 1.1 convert_multiply_fusion
  129.6 0.0 copy-done
  129.6 0.0 copy-start.3
  129.6 1.1 fusion.35
  130.7 0.0 copy-done.4
  130.8 2.2 %fusion.68 = (bf16[301,256]{1,0:T(8,128)(2,1)}, f32[301,256]{1,0:T(8,128)}) fusion(f32[256,301]{1,0:T(8,128)S(1)} %fusion.35, f32[4,256,256]{2,1,0:T(8,128)S(1)} %copy-done.4, f32[]{:T(128)S(6)} %div.23, f32[1204,256]{1,0:T(8,128)} %w1.1, s32[]{:T(128)S(6)} %select_n.44), kind=kOutput, calls=%fused_computation.111 | convolution fusion | flops 118589184 | bytes 1425928 | tf_op jit(solution)/shard_map/dot_general | solution.py:533
  133.0 0.0 copy-done.3
  133.0 0.0 copy-start.2
  133.0 1.8 %fusion = f32[301,1204]{1,0:T(8,128)} fusion(f32[301,1204]{1,0:T(8,128)S(1)} %copy-done.3, f32[]{:T(128)S(6)} %mul.235, bf16[602,256]{1,0:T(8,128)(2,1)S(1)} %get-tuple-element.31, bf16[602,256]{1,0:T(8,128)(2,1)S(1)} %get-tuple-element.30, s32[]{:T(128)S(6)} %select_n.44), kind=kOutput, calls=%fused_computation.1 | convolution fusion | flops 188179168 | bytes 4251288 | tf_op jit(solution)/shard_map/dot_general | solution.py:522
  134.7 0.0 copy-done.2
  134.7 0.1 fusion.66
  134.8 0.3 fusion.9
  135.1 0.3 fusion.7
  135.4 0.8 fusion.62
  (15 shorter events, 0.2 us)
Async XLA Ops:
  0.7 129.0 %copy-start = (f32[301,1204]{1,0:T(8,128)S(1)}, f32[301,1204]{1,0:T(8,128)}, u32[]{:S(2)}) copy-start(f32[301,1204]{1,0:T(8,128)} %param.33) | copy-start | bytes 4348852
  0.7 5.9 %copy-start.5 = (s32[1,3,2048,25]{2,0,3,1:T(1,128)S(1)}, s32[1,3,2048,25]{2,0,3,1:T(1,128)}, u32[]{:S(2)}) copy-start(s32[1,3,2048,25]{2,0,3,1:T(1,128)} %param.22) | copy-start | bytes 1843204
  8.2 2.2 %copy-start.9 = (s32[16,128]{1,0:T(8,128)}, s32[16,128]{1,0:T(8,128)S(1)}, u32[]{:S(2)}) copy-start(s32[16,128]{1,0:T(8,128)S(1)} %slice_bitcast_fusion.2.c3) | copy-start | bytes 24580
  10.4 102.7 %slice-start = ((f32[4,256,256]{2,1,0:T(8,128)}), f32[1,256,256]{2,1,0:T(8,128)S(1)}, s32[]{:S(2)}) async-start(f32[4,256,256]{2,1,0:T(8,128)} %param.37), calls=%async_computation | async-start | bytes 524288 | tf_op jit(solution)/shard_map/slice | solution.py:611
  109.8 6.9 %copy-start.1 = (bf16[2304,256]{1,0:T(8,128)(2,1)S(1)}, bf16[2304,256]{1,0:T(8,128)(2,1)}, u32[]{:S(2)}) copy-start(bf16[2304,256]{1,0:T(8,128)(2,1)} %get-tuple-element.22) | copy-start | bytes 3538948
  109.8 13.2 %copy-start.6 = (f32[2,128,512]{2,1,0:T(8,128)S(1)}, f32[2,128,512]{2,1,0:T(8,128)}, u32[]{:S(2)}) copy-start(f32[2,128,512]{2,1,0:T(8,128)} %param.35) | copy-start | bytes 1572868
  123.7 1.0 copy-start.8
  125.3 1.2 copy-start.7
  128.5 2.2 %copy-start.4 = (f32[4,256,256]{2,1,0:T(8,128)S(1)}, f32[4,256,256]{2,1,0:T(8,128)}, u32[]{:S(2)}) copy-start(f32[4,256,256]{2,1,0:T(8,128)} %param.37) | copy-start | bytes 3145732
  129.6 3.3 %copy-start.3 = (f32[301,1204]{1,0:T(8,128)S(1)}, f32[301,1204]{1,0:T(8,128)}, u32[]{:S(2)}) copy-start(f32[301,1204]{1,0:T(8,128)} %param.32) | copy-start | bytes 4348852
  133.0 1.8 %copy-start.2 = (f32[2,512,256]{2,1,0:T(8,128)S(1)}, f32[2,512,256]{2,1,0:T(8,128)}, u32[]{:S(2)}) copy-start(f32[2,512,256]{2,1,0:T(8,128)} %wr.1) | copy-start | bytes 3145732

commit v2 on v1

v2 whole, which is shorter than its diff:
```python
import functools

import jax
import jax.numpy as jnp
from jax import lax
from jax.experimental import pallas as pl
from jax.experimental.pallas import tpu as pltpu
from jax.sharding import PartitionSpec as P

STEP = 5
FAN_REST = 10

clip_limit = 0.0001
decay = 0.5
shampoo_rate = 1.0
beta_one = 0.9
beta_two = 0.999
bias_rate = 0.05
weight_decay = 0.01
adam_eps = 1e-08
norm_eps = 1e-06
MASKED = 8192

bf16 = jnp.bfloat16
f32 = jnp.float32
i32 = jnp.int32
MESH = pl.DeviceIdType.MESH


def nn(a, b):
    return jnp.dot(a, b, preferred_element_type=f32)


def nt(a, b):
    return lax.dot_general(a, b, (((1,), (1,)), ((), ())), preferred_element_type=f32)


def flip(a):
    return a.astype(f32).T.astype(a.dtype)


def round_up(a, b):
    return (a + b - 1) // b * b


def gelu(z):
    scale = 0.7978845608028654
    return z * (0.5 + 0.5 * jnp.tanh(z * (scale + (0.044715 * scale) * (z * z))))


def gelu_slope(z):
    scale = 0.7978845608028654
    square = z * z
    half = 0.5 + 0.5 * jnp.tanh(z * (scale + (0.044715 * scale) * square))
    return half + (half - half * half) * (z * (2.0 * scale + (6.0 * 0.044715 * scale) * square))


def norm_root(act):
    return lax.rsqrt(jnp.sum(act * act, axis=0, keepdims=True) + norm_eps)


def pull_back(act, slope, root, grad):
    dot = jnp.sum(act * grad, axis=0, keepdims=True)
    return (slope * (root * grad - act * (root * root * root * dot))).astype(bf16)


def as_column(row):
    return jnp.broadcast_to(row, (8, row.shape[1])).T[:, 0:1]


def widen(row, width, value=0):
    return jnp.concatenate([row, jnp.full((1, width - row.shape[1]), value, row.dtype)], axis=1)


def graph_kernel(
    peers, cap, seeds, fan,
    code_ref, srow, scnt, lab, smask, xt, w1_hbm, wr_hbm, wht, bias,
    g_out, s_out,
    joined, gathered, pick, chosen, far2, cblk_a, cblk_b, cinc, ctmp, crow, lrow, rdeg, part2, lcode,
    w1, wr, w1t, act1, z1, root1, h1t, ob0, ib0, obs, ibs,
    gl, acc, rc, sb1, rb1, sb2, rb2, sbz, rbz, gout, ssend, srecv, szv,
    load_sem, send_sem, recv_sem, red_send, red_recv,
):
    fin, nodes = xt.shape
    hidden = w1.shape[1]
    finp = round_up(fin, 16)
    slots = peers * cap
    table = nodes + slots
    groups = table // 128
    chunks = nodes // 128
    span = far2.shape[1]
    local = span - slots
    me = lax.axis_index("dom")
    rep = lax.axis_index("rep")
    core = lax.rem(rep, 2)
    xpos = rep // 2
    ypos = lax.rem(me, 2)
    zpos = me // 2
    nz = peers // 2
    mate_c = xpos * 2 + (1 - core)
    mate_x = (1 - xpos) * 2 + core
    mate_y = zpos * 2 + (1 - ypos)

    bias = bias[...].reshape(1, bias.shape[0])
    load1 = pltpu.make_async_copy(w1_hbm, w1, load_sem.at[0])
    load2 = pltpu.make_async_copy(wr_hbm, wr, load_sem.at[1])
    load1.start()
    load2.start()
    barrier = pltpu.get_barrier_semaphore()
    for off in range(1, peers):
        pl.semaphore_signal(barrier, inc=1, device_id={"dom": lax.rem(me + off, peers)}, device_id_type=MESH)
    for mate in (mate_c, mate_x):
        pl.semaphore_signal(barrier, inc=1, device_id={"rep": mate}, device_id_type=MESH)

    def exchange(stage, src, dst):
        copies = []
        for off in range(1, peers):
            peer = lax.rem(me + off, peers)
            copies.append(
                pltpu.make_async_remote_copy(
                    src_ref=src.at[pl.ds(pl.multiple_of(peer * cap, cap), cap)],
                    dst_ref=dst.at[pl.ds(pl.multiple_of(me * cap, cap), cap)],
                    send_sem=send_sem.at[stage, off - 1],
                    recv_sem=recv_sem.at[stage, off - 1],
                    device_id={"dom": peer},
                    device_id_type=MESH,
                )
            )
        for c in copies:
            c.start()
        return copies

    def finish(copies):
        for c in copies:
            c.wait()

    mine = pl.ds(pl.multiple_of(me * cap, cap), cap)

    count = jnp.broadcast_to(scnt[...], (peers, peers))
    count = jnp.where(
        lax.broadcasted_iota(i32, (peers, peers), 0) == lax.broadcasted_iota(i32, (peers, peers), 1), count, 0
    )
    count = jnp.sum(count.astype(f32), axis=1, keepdims=True)
    in_use = lax.broadcasted_iota(i32, (peers, cap), 1).astype(f32) < count
    slot = jnp.where(in_use, srow[...].astype(f32), -1.0)
    per = 128 // cap
    slot = jnp.concatenate([slot] * per, axis=1)
    owner = lax.broadcasted_iota(i32, (peers, 128), 0)
    place = lax.broadcasted_iota(i32, (peers, 128), 1) // cap
    send_row = jnp.concatenate(
        [
            jnp.sum(jnp.where(owner == place + t * per, slot, 0.0), axis=0, keepdims=True)
            for t in range(slots // 128)
        ],
        axis=1,
    )
    send_col = as_column(send_row)
    pick[...] = jnp.where(
        send_col == lax.broadcasted_iota(i32, (slots, nodes), 1).astype(f32), 1.0, 0.0
    ).astype(bf16)
    joined[finp - 16 : finp, :] = jnp.zeros((16, nodes), bf16)
    joined[0:fin, :] = xt[...]
    ob0[:, finp:] = jnp.zeros((slots, ob0.shape[1] - finp), bf16)
    ob0[:, 0:finp] = nt(pick[...], joined[0:finp, :]).astype(bf16)
    ib0[mine, :] = jnp.zeros((cap, ib0.shape[1]), bf16)
    for k in range(4):
        ibs[k, mine, :] = jnp.zeros((cap, hidden), bf16)
    pl.semaphore_wait(barrier, peers - 1 + 2)
    sent = exchange(0, ob0, ib0)

    def codes(level, c, size):
        return code_ref[level, 0:size, c * 128 : (c + 1) * 128]

    fill = jnp.full((32 - fan, 128), float(MASKED), f32)
    fill2 = jnp.full((16 - FAN_REST, 128), float(MASKED), f32)
    for c in range(chunks):
        here = slice(c * 128, (c + 1) * 128)
        code = codes(0, c, fan)
        degree = jnp.sum((code < MASKED).astype(f32), axis=0, keepdims=True)
        rdeg[0:1, here] = 1.0 / jnp.maximum(degree, 1.0)
        ctmp[here, 0:32] = jnp.concatenate([code, fill], axis=0).T
        code = jnp.concatenate([codes(1, c, FAN_REST), fill2], axis=0).astype(i32)
        part2[0:16, here] = (code >> 7).astype(f32).astype(bf16)
        part2[16:32, here] = (code & 127).astype(f32).astype(bf16)

    ngroups = nodes // 8
    lane = lax.broadcasted_iota(i32, (ngroups, 256), 1)
    code = jnp.zeros((ngroups, 256), f32)
    for n in range(8):
        piece = ctmp[pl.ds(n, ngroups, stride=8), :]
        piece = jnp.concatenate([piece, piece], axis=1)
        piece = pltpu.roll(piece, n * 32, 1) if n else piece
        code = jnp.where((lane >> 5) == n, piece, code)
    code = code.astype(i32)
    crow[...] = ((code >> 7) * 8 + (lane >> 5)).astype(f32)
    lrow[...] = (code & 127).astype(f32)

    code3 = codes(2, 0, FAN_REST)
    lane = lax.broadcasted_iota(i32, (1, 128), 1)
    fits = 128 // seeds
    tiles, keeps = [], []
    for t in range(local // 128):
        tile = jnp.full((1, 128), -1.0, f32)
        for j in range(fits):
            k = t * fits + j
            here = lane // seeds == j
            if k < FAN_REST:
                piece = code3[k : k + 1, :]
                piece = pltpu.roll(piece, j * seeds, 1) if j else piece
                tile = jnp.where(here & (piece < nodes), piece, tile)
            elif k == FAN_REST:
                tile = jnp.where(here, (lane - j * seeds).astype(f32), tile)
        tiles.append(tile)
    list_row = jnp.concatenate([send_row] + tiles, axis=1)
    keep_row = jnp.where(list_row >= 0.0, 1.0, 0.0)

    def one_hot_rows(b, _):
        start = pl.multiple_of(b * 256, 256)
        row = (lax.broadcasted_iota(i32, (256, span), 0) + b * 256).astype(f32)
        chosen[pl.ds(start, 256), 0:span] = jnp.where(row == list_row, 1.0, 0.0).astype(bf16)
        return 0

    lax.fori_loop(0, nodes // 256, one_hot_rows, 0)
    found = nn(part2[...], chosen[:, 0:span])
    lcode[...] = found[0:16] * 128.0 + found[16:32]
    live = (lcode[0:FAN_REST, :] < float(MASKED)).astype(f32)
    rdeg2 = 1.0 / jnp.maximum(jnp.sum(live, axis=0, keepdims=True), 1.0)

    rows_a = lax.broadcasted_iota(i32, (groups * 8, 256), 0).astype(f32)
    rows_b = lax.broadcasted_iota(i32, (128, 256), 0).astype(f32)

    def list_counts(first, size):
        row = (lax.broadcasted_iota(i32, (size, span), 0) + first).astype(f32)
        total = jnp.where(row == lcode[0:1, :], 1.0, 0.0)
        for k in range(1, FAN_REST):
            total = total + jnp.where(row == lcode[k : k + 1, :], 1.0, 0.0)
        return total.astype(bf16)

    def build(b, cblk):
        start = b * 256
        for p in range(16):
            pair = []
            for half in range(2):
                g = b * 32 + p * 2 + half
                left = jnp.where(rows_a == crow[pl.ds(g, 1), :], 1.0, 0.0).astype(bf16)
                right = jnp.where(rows_b == lrow[pl.ds(g, 1), :], 1.0, 0.0).astype(bf16)
                pair.append(nt(left, right))
            for a in range(groups):
                tile = jnp.concatenate([pair[0][a * 8 : (a + 1) * 8], pair[1][a * 8 : (a + 1) * 8]], axis=0)
                if a < chunks:
                    cblk[p * 16 : (p + 1) * 16, a * 128 : (a + 1) * 128] = tile.astype(bf16)
                else:
                    at = pl.ds(pl.multiple_of(start + p * 16, 16), 16)
                    cinc[at, (a - chunks) * 128 : (a - chunks + 1) * 128] = tile.astype(bf16)
        for q in range(8):
            at = pl.ds(pl.multiple_of(start + q * 32, 32), 32)
            chosen[at, span:] = list_counts(start + q * 32, 32)

    def multiply(b, cblk):
        blk = pl.ds(pl.multiple_of(b * 256, 256), 256)
        gathered[:, blk] = nt(joined[0:finp, :], cblk[...])

    build(0, cblk_a)

    def own_blocks(i, _):
        multiply(2 * i, cblk_a)
        build(2 * i + 1, cblk_b)
        multiply(2 * i + 1, cblk_b)
        build(2 * i + 2, cblk_a)
        return 0

    last = nodes // 256 - 1
    lax.fori_loop(0, (last - 1) // 2, own_blocks, 0)
    multiply(last - 1, cblk_a)
    build(last, cblk_b)
    multiply(last, cblk_b)

    load1.wait()
    load2.wait()
    wpad = jnp.concatenate(
        [w1[0:fin, :], jnp.zeros((finp - fin, hidden), f32), w1[fin : 2 * fin, :], jnp.zeros((finp - fin, hidden), f32)],
        axis=0,
    )
    w1t[...] = wpad.T.astype(bf16)
    w2 = wr[0].astype(bf16)
    w3 = wr[1].astype(bf16)

    def bias_col(level):
        return as_column(bias[0:1, level * hidden : (level + 1) * hidden])

    finish(sent)
    ibt = flip(ib0[...])[0:finp, :]
    b1 = bias_col(0)

    def layer_one(b, _):
        blk = pl.ds(pl.multiple_of(b * 256, 256), 256)
        total = gathered[:, blk] + nt(ibt, cinc[blk, :])
        joined[finp:, blk] = (total * rdeg[0:1, blk]).astype(bf16)
        z = nn(w1t[...], joined[:, blk]) + b1
        z1[:, blk] = z
        act = gelu(z)
        root = norm_root(act)
        act1[:, blk] = act
        root1[0:1, blk] = root
        h1t[:, blk] = (act * root).astype(bf16)
        return 0

    lax.fori_loop(0, nodes // 256, layer_one, 0)
    obs[0] = nt(pick[...], h1t[...]).astype(bf16)
    sent = exchange(1, obs.at[0], ibs.at[0])

    own2 = nn(h1t[...], chosen[...])
    w2t = flip(w2)
    for q in range(slots // 32):
        far2[q * 32 : (q + 1) * 32, :] = list_counts(nodes + q * 32, 32)

    def slopes(b, _):
        blk = pl.ds(pl.multiple_of(b * 256, 256), 256)
        z1[:, blk] = gelu_slope(z1[:, blk])
        return 0

    lax.fori_loop(0, nodes // 256, slopes, 0)
    b2 = bias_col(1)
    finish(sent)
    agg2 = (own2[:, span:] + nn(flip(ibs[0]), far2[...])) * rdeg2
    joined2 = jnp.concatenate([own2[:, 0:span].astype(bf16), agg2.astype(bf16)], axis=0)
    z2 = nn(w2t, joined2) + b2
    act2 = gelu(z2)
    root2 = norm_root(act2)
    h2 = act2 * root2 * keep_row
    obs[1] = h2[:, 0:slots].T.astype(bf16)
    sent = exchange(2, obs.at[1], ibs.at[1])

    r_id = lax.broadcasted_iota(i32, (local, 256), 0)
    l_id = lax.broadcasted_iota(i32, (local, 256), 1)
    is_self = (l_id < seeds) & (r_id == l_id + FAN_REST * seeds)
    is_nbr = (l_id >= 128) & (l_id < 128 + seeds) & (r_id < FAN_REST * seeds) & (lax.rem(r_id, seeds) == l_id - 128)
    spread = jnp.where(is_self | is_nbr, 1.0, 0.0).astype(bf16)
    near3 = nn(h2[:, slots:].astype(bf16), spread)
    row3 = (lax.broadcasted_iota(i32, (slots, 128), 0) + nodes).astype(f32)
    far3 = jnp.zeros((slots, 128), f32)
    for k in range(FAN_REST):
        far3 = far3 + jnp.where(row3 == code3[k : k + 1, :], 1.0, 0.0)
    far3 = far3.astype(bf16)
    rdeg3 = 1.0 / jnp.maximum(jnp.sum((code3 < float(MASKED)).astype(f32), axis=0, keepdims=True), 1.0)
    slope2 = gelu_slope(z2)
    w3t = flip(w3)
    classes = wht.shape[0]
    classp = round_up(classes, 16)
    wht_low = jnp.concatenate([wht[...], jnp.zeros((classp - classes, hidden), f32)], axis=0)
    wh_low = wht_low.T.astype(bf16)
    wht_low = wht_low.astype(bf16)
    b3 = bias_col(2)
    bh = as_column(widen(bias[0:1, 3 * hidden : 3 * hidden + classes], 128))[0:classp]
    class_id = lax.broadcasted_iota(i32, (classp, 128), 0)
    hot = jnp.where(class_id == widen(lab[...], 128), 1.0, 0.0)
    weight = widen(smask[...].astype(f32), 128)
    finish(sent)
    agg3 = (near3[:, 128:] + nn(flip(ibs[1]), far3)) * rdeg3
    joined3 = jnp.concatenate([near3[:, 0:128].astype(bf16), agg3.astype(bf16)], axis=0)
    z3 = nn(w3t, joined3) + b3
    act3 = gelu(z3)
    slope3 = gelu_slope(z3)
    root3 = norm_root(act3)
    top = (act3 * root3).astype(bf16)

    logits = nn(wht_low, top) + bh
    logits = jnp.where(class_id < classes, logits, -1e30)
    peak = jnp.max(logits, axis=0, keepdims=True)
    lse = peak + jnp.log(jnp.sum(jnp.exp(logits - peak), axis=0, keepdims=True))
    dlog = ((jnp.exp(logits - lse) - hot) * weight).astype(bf16)
    dtop = nn(wh_low, dlog)

    dz3 = pull_back(act3, slope3, root3, dtop)
    dj3 = nn(w3, dz3)
    dg3 = (dj3[hidden:] * rdeg3).astype(bf16)
    obs[2] = nt(far3, dg3).astype(bf16)
    sent = exchange(3, obs.at[2], ibs.at[2])
    dloc = nt(jnp.concatenate([dj3[0:hidden].astype(bf16), dg3], axis=1), spread)

    seg_a = 4 * hidden
    row_head = seg_a + 2 * finp
    row_bias = row_head + classp
    rows = gl.shape[1]

    def put(row, value):
        size = value.shape[0]
        gl[0, row : row + size, :] = value[:, 0:128].astype(bf16)
        gl[1, row : row + size, :] = value[:, 128:].astype(bf16)

    picked = jnp.sum(logits * hot, axis=0, keepdims=True)
    loss = jnp.sum((lse - picked) * weight, axis=1, keepdims=True)
    total = jnp.sum(weight, axis=1, keepdims=True)
    sc_lane = lax.broadcasted_iota(i32, (8, 128), 1)
    ssend[0] = jnp.where(sc_lane == 0, loss, jnp.where(sc_lane == 1, total, 0.0))
    ones = jnp.ones((16, 128), bf16)
    put(row_head, nt(dlog, top))
    bias_h = jnp.concatenate([nt(ones, dlog), jnp.zeros((16, hidden - classp), f32)], axis=1)
    put(2 * hidden, nt(joined3, dz3))
    bias_3 = nt(ones, dz3)
    finish(sent)
    dh2 = jnp.concatenate([ibs[2].astype(f32).T, dloc], axis=1) * keep_row

    dz2 = pull_back(act2, slope2, root2, dh2)
    dj2 = nn(w2, dz2)
    dg2 = (dj2[hidden:] * rdeg2).astype(bf16)
    obs[3] = nt(far2[...], dg2).astype(bf16)
    sent = exchange(4, obs.at[3], ibs.at[3])
    put(0, nt(joined2, dz2))

    used = []

    def hop(src, dst, axis, who):
        used.append(0)
        k = len(used) - 1
        copy = pltpu.make_async_remote_copy(
            src_ref=src, dst_ref=dst, send_sem=red_send.at[k], recv_sem=red_recv.at[k],
            device_id={axis: who}, device_id_type=MESH,
        )
        copy.start()
        return copy

    def z_mate(off):
        return lax.rem(zpos + off, nz) * 2 + ypos

    def rows_of(start, size):
        return pl.ds(pl.multiple_of(start, 16), size)

    ways = ((xpos, "rep", mate_x), (ypos, "dom", mate_y))

    def parts_of(segment):
        return [(base, size, ways[order], ways[1 - order]) for base, size, order in segment]

    def core_start(segment):
        base, size = segment[0][0], sum(p[1] for p in segment)
        at = slice(base, base + size)
        return [hop(gl.at[1 - core, at], rc.at[at], "rep", mate_c)]

    def core_done(segment):
        base, size = segment[0][0], sum(p[1] for p in segment)
        at = slice(base, base + size)
        acc[at, :] = gl[core, at, :].astype(f32) + rc[at, :].astype(f32)

    def one_start(segment):
        copies = []
        for base, size, (pos, axis, mate), _ in parts_of(segment):
            half = size // 2
            at = slice(base // 2, base // 2 + half)
            sb1[at, :] = acc[rows_of(base + (1 - pos) * half, half), :].astype(bf16)
            copies.append(hop(sb1.at[at], rb1.at[at], axis, mate))
        return copies

    def one_done(segment):
        for base, size, (pos, _, _), _ in parts_of(segment):
            half = size // 2
            keep = rows_of(base + pos * half, half)
            acc[keep, :] = acc[keep, :] + rb1[base // 2 : base // 2 + half, :].astype(f32)

    def two_start(segment):
        copies = []
        for base, size, (pos, _, _), (pos2, axis, mate) in parts_of(segment):
            half, quarter = size // 2, size // 4
            at = slice(base // 4, base // 4 + quarter)
            sb2[at, :] = acc[rows_of(base + pos * half + (1 - pos2) * quarter, quarter), :].astype(bf16)
            copies.append(hop(sb2.at[at], rb2.at[at], axis, mate))
        return copies

    def two_done(segment):
        for base, size, (pos, _, _), (pos2, _, _) in parts_of(segment):
            half, quarter = size // 2, size // 4
            keep = rows_of(base + pos * half + pos2 * quarter, quarter)
            acc[keep, :] = acc[keep, :] + rb2[base // 4 : base // 4 + quarter, :].astype(f32)

    def z_start(segment):
        copies = []
        for base, size, (pos, _, _), (pos2, _, _) in parts_of(segment):
            half, quarter, piece = size // 2, size // 4, size // (4 * nz)
            at = slice(base // 4, base // 4 + quarter)
            sbz[at, :] = acc[rows_of(base + pos * half + pos2 * quarter, quarter), :].astype(bf16)
            low = base // (4 * nz)
            for off in range(1, nz):
                to = lax.rem(zpos + off, nz)
                copies.append(
                    hop(
                        sbz.at[rows_of(base // 4 + to * piece, piece)],
                        rbz.at[off - 1, low : low + piece],
                        "dom",
                        z_mate(off),
                    )
                )
        return copies

    def z_done_and_spread(segment):
        copies = []
        for base, size, (pos, _, _), (pos2, _, _) in parts_of(segment):
            half, quarter, piece = size // 2, size // 4, size // (4 * nz)
            here = rows_of(base + pos * half + pos2 * quarter + zpos * piece, piece)
            low = base // (4 * nz)
            value = acc[here, :]
            for off in range(1, nz):
                value = value + rbz[off - 1, low : low + piece, :].astype(f32)
            gout[core, here, :] = value.astype(bf16)
            part = gout.at[core, here]
            for off in range(1, nz):
                copies.append(hop(part, part, "dom", z_mate(off)))
        return copies

    def spread_two(segment):
        copies = []
        for base, size, (pos, _, _), (pos2, axis, mate) in parts_of(segment):
            half, quarter = size // 2, size // 4
            part = gout.at[core, rows_of(base + pos * half + pos2 * quarter, quarter)]
            copies += [hop(part, part, axis, mate), hop(part, part, "rep", mate_c)]
        return copies

    def spread_one(segment):
        copies = []
        for base, size, (pos, axis, mate), (pos2, _, _) in parts_of(segment):
            half, quarter = size // 2, size // 4
            part = gout.at[core, rows_of(base + pos * half, half)]
            copies.append(hop(part, part, axis, mate))
            part = gout.at[core, rows_of(base + pos * half + (1 - pos2) * quarter, quarter)]
            copies.append(hop(part, part, "rep", mate_c))
        return copies

    def spread_core(segment):
        copies = []
        for base, size, (pos, _, _), _ in parts_of(segment):
            half = size // 2
            part = gout.at[core, rows_of(base + (1 - pos) * half, half)]
            copies.append(hop(part, part, "rep", mate_c))
        return copies

    rest = ((0, 2 * hidden, 0), (2 * hidden, 2 * hidden, 1))
    first = ((seg_a, 3 * hidden, 0), (seg_a + 3 * hidden, rows - seg_a - 3 * hidden, 1))
    sums = core_start(rest) + [hop(ssend.at[0], srecv.at[0], "rep", mate_c)]

    bias_2 = nt(jnp.ones((16, span), bf16), dz2)
    both = jnp.concatenate([dj2[0:hidden].astype(bf16), dg2], axis=1)
    gathered[0:hidden, :] = nt(both, chosen[...])
    finish(sums)
    core_done(rest)
    ssend[1] = ssend[0] + srecv[0]
    sums = one_start(rest) + [hop(ssend.at[1], srecv.at[1], "rep", mate_x)]
    finish(sent)
    back = flip(ibs[3])

    def layer_one_back(b, _):
        blk = pl.ds(pl.multiple_of(b * 256, 256), 256)
        grad = gathered[0:hidden, blk] + nn(back, pick[:, blk])
        h1t[:, blk] = pull_back(act1[:, blk], z1[:, blk], root1[0:1, blk], grad)
        return 0

    lax.fori_loop(0, nodes // 256, layer_one_back, 0)
    finish(sums)
    one_done(rest)
    ssend[2] = ssend[1] + srecv[1]
    sums = two_start(rest) + [hop(ssend.at[2], srecv.at[2], "dom", mate_y)]
    step_rows = finp // 2

    def first_grad(b, _):
        start = pl.multiple_of(b * step_rows, 16)
        value = nt(joined[pl.ds(start, step_rows), :], h1t[...])
        to = pl.multiple_of(seg_a + b * step_rows, 16)
        gl[0, pl.ds(to, step_rows), :] = value[:, 0:128].astype(bf16)
        gl[1, pl.ds(to, step_rows), :] = value[:, 128:].astype(bf16)
        return 0

    lax.fori_loop(0, 4, first_grad, 0)
    bias_1 = nt(jnp.ones((16, nodes), bf16), h1t[...])
    line = lax.broadcasted_iota(i32, (16, hidden), 0)
    put(
        row_bias,
        jnp.where(line == 0, bias_1, 0.0)
        + jnp.where(line == 1, bias_2, 0.0)
        + jnp.where(line == 2, bias_3, 0.0)
        + jnp.where(line == 3, bias_h, 0.0),
    )
    now = core_start(first)
    finish(sums)
    two_done(rest)
    ssend[3] = ssend[2] + srecv[2]
    szv[zpos] = ssend[3]
    sums = z_start(rest)
    for off in range(1, nz):
        sums.append(hop(ssend.at[3], szv.at[zpos], "dom", z_mate(off)))
    finish(now)
    core_done(first)
    now = one_start(first)
    finish(sums)
    sums = z_done_and_spread(rest)
    s_out[...] = szv[0] + szv[1] + szv[2] + szv[3]
    finish(now)
    one_done(first)
    now = two_start(first)
    finish(sums)
    sums = spread_two(rest)
    finish(now)
    two_done(first)
    now = z_start(first)
    finish(sums)
    sums = spread_one(rest)
    finish(now)
    now = z_done_and_spread(first)
    finish(sums)
    sums = spread_core(rest)
    finish(now)
    now = spread_two(first)
    finish(sums)
    finish(now)
    now = spread_one(first)
    finish(now)
    now = spread_core(first)
    finish(now)
    out = pltpu.make_async_copy(gout, g_out, load_sem.at[0])
    out.start()
    out.wait()


def summed_gradients(peers, cap, seeds, fan, codes, srow, scnt, lab, smask, xt, w1, wr, wht, bias):
    fin, nodes = xt.shape
    hidden = w1.shape[1]
    finp = round_up(fin, 16)
    wide = round_up(fin, 128)
    slots = peers * cap
    span = slots + round_up(seeds * (FAN_REST + 1), 128)
    classp = round_up(wht.shape[0], 16)
    rows = 4 * hidden + 2 * finp + classp + 16
    nz = peers // 2
    vmem = pltpu.VMEM
    sems = 60
    scratch = [
        vmem((2 * finp, nodes), bf16),
        vmem((finp, nodes), f32),
        vmem((slots, nodes), bf16),
        vmem((nodes, 2 * span), bf16),
        vmem((slots, span), bf16),
        vmem((256, nodes), bf16),
        vmem((256, nodes), bf16),
        vmem((nodes, slots), bf16),
        vmem((nodes, 128), f32),
        vmem((nodes // 8, 256), f32),
        vmem((nodes // 8, 256), f32),
        vmem((8, nodes), f32),
        vmem((32, nodes), bf16),
        vmem((16, span), f32),
        vmem(w1.shape, f32),
        vmem(wr.shape, f32),
        vmem((hidden, 2 * finp), bf16),
        vmem((hidden, nodes), f32),
        vmem((hidden, nodes), f32),
        vmem((8, nodes), f32),
        vmem((hidden, nodes), bf16),
        vmem((slots, wide), bf16),
        vmem((slots, wide), bf16),
        vmem((4, slots, hidden), bf16),
        vmem((4, slots, hidden), bf16),
        vmem((2, rows, 128), bf16),
        vmem((rows, 128), f32),
        vmem((rows, 128), bf16),
        vmem((rows // 2, 128), bf16),
        vmem((rows // 2, 128), bf16),
        vmem((rows // 4, 128), bf16),
        vmem((rows // 4, 128), bf16),
        vmem((rows // 4, 128), bf16),
        vmem((nz - 1, rows // (4 * nz), 128), bf16),
        vmem((2, rows, 128), bf16),
        vmem((4, 8, 128), f32),
        vmem((3, 8, 128), f32),
        vmem((nz, 8, 128), f32),
        pltpu.SemaphoreType.DMA((2,)),
        pltpu.SemaphoreType.DMA((5, peers - 1)),
        pltpu.SemaphoreType.DMA((5, peers - 1)),
        pltpu.SemaphoreType.DMA((sems,)),
        pltpu.SemaphoreType.DMA((sems,)),
    ]
    inside = pl.BlockSpec(memory_space=vmem)
    outside = pl.BlockSpec(memory_space=pl.ANY)
    return pl.pallas_call(
        functools.partial(graph_kernel, peers, cap, seeds, fan),
        out_shape=(
            jax.ShapeDtypeStruct((2, rows, 128), bf16),
            jax.ShapeDtypeStruct((8, 128), f32),
        ),
        in_specs=[inside] * 6 + [outside] * 2 + [inside] * 2,
        out_specs=(outside, inside),
        scratch_shapes=scratch,
        compiler_params=pltpu.CompilerParams(
            collective_id=0, has_side_effects=True, vmem_limit_bytes=48 * 2**20
        ),
        name="graph_step",
    )(codes, srow, scnt, lab, smask, xt, w1, wr, wht, bias)


def split_dot(a, b):
    high = a.astype(bf16)
    low = (a - high.astype(f32)).astype(bf16)
    return nn(high, b) + nn(low, b)


def three_dot(a, b):
    high = b.astype(bf16)
    low = (b - high.astype(f32)).astype(bf16)
    return split_dot(a, high) + nn(a.astype(bf16), low)


def update_kernel(
    fin,
    g_all, scalars, w1, wr, wht, bias, st1, rt1, stm, rtm, sts, rts, sth, rth, bm, bv,
    loss_o, total_o, norm_o, g1_o, gr_o, gh_o, m_o, v_o, l1_o, lm_o, ls_o, lh_o, n1_o, nr_o, nh_o, nb_o,
    n1_low, nr_low, nh_low,
    g1, g_mine, w_mine, full, gb,
):
    hidden = w1.shape[1]
    classes = wht.shape[0]
    classp = round_up(classes, 16)
    finp = round_up(fin, 16)
    seg_a = 4 * hidden
    part = lax.axis_index("rep")

    def grads(start, size):
        return jnp.concatenate(
            [g_all[0, start : start + size, :], g_all[1, start : start + size, :]], axis=1
        )

    total = scalars[0:1, 1:2]
    square = jnp.zeros((16, hidden), f32)
    for r in range(0, g_all.shape[1], 16):
        g = grads(r, 16).astype(f32)
        square = square + g * g
    square = jnp.sum(jnp.sum(square, axis=0, keepdims=True), axis=1, keepdims=True)
    norm = jnp.sqrt(square) / total
    scale = clip_limit / jnp.maximum(norm, clip_limit) / total
    loss_o[...] = scalars[0:1, 0:1]
    total_o[...] = total
    norm_o[...] = norm
    lift = (1.0 - decay) * scale * scale
    move = shampoo_rate * scale

    g1[0:fin, :] = grads(seg_a, finp)[0:fin].astype(f32)
    g1[fin : 2 * fin, :] = grads(seg_a + finp, finp)[0:fin].astype(f32)
    count = st1.shape[0]
    for i in range(2 * fin // count):

        @pl.when(part == i)
        def _():
            g_mine[...] = g1[i * count : (i + 1) * count, :]
            w_mine[...] = w1[i * count : (i + 1) * count, :]

    g_rows = g_mine[...]
    g_low = g1[...].astype(bf16)
    g1_o[...] = g_rows * scale
    l1_o[...] = decay * st1[...] + lift * nt(g_rows.astype(bf16), g_low)
    full[0] = nn(g1[...].T.astype(bf16), g_low)
    step = three_dot(split_dot(rt1[...], g_low), rts[0])
    fresh = w_mine[...] - move * step
    n1_o[...] = fresh
    n1_low[...] = fresh.astype(bf16)

    for i in range(2):
        g = grads(i * 2 * hidden, 2 * hidden)
        count = stm.shape[1]
        at = pl.ds(pl.multiple_of(part * count, count), count)
        base = pl.ds(pl.multiple_of(i * 2 * hidden + part * count, 16), count)
        g_rows = jnp.concatenate([g_all[0, base, :], g_all[1, base, :]], axis=1)
        gr_o[i] = g_rows.astype(f32) * scale
        lm_o[i] = decay * stm[i] + lift * nt(g_rows, g)
        full[1 + i] = nn(flip(g), g)
        step = three_dot(split_dot(rtm[i], g), rts[1 + i])
        fresh = wr[i, at, :] - move * step
        nr_o[i] = fresh
        nr_low[i] = fresh.astype(bf16)

    gt = grads(seg_a + 2 * finp, classp)
    full[3] = nn(flip(gt), gt)
    count = sts.shape[1]
    mine = pl.ds(pl.multiple_of(part * count, count), count)
    for i in range(4):
        ls_o[i] = decay * sts[i] + lift * full[i, mine, :]
    lh_o[...] = decay * sth[...] + lift * nt(gt, gt)[0:classes, 0:classes]
    root = rts[3, mine, :]
    high = root.astype(bf16)
    low = (root - high.astype(f32)).astype(bf16)
    left = (nt(gt, high) + nt(gt, low))[0:classes]
    step = three_dot(rth[...], left)
    gt_mine = jnp.zeros((classes, count), f32)
    wt_mine = jnp.zeros((classes, count), f32)
    gt_wide = gt.astype(f32)
    for i in range(hidden // count):
        here = slice(i * count, (i + 1) * count)
        gt_mine = jnp.where(part == i, gt_wide[0:classes, here], gt_mine)
        wt_mine = jnp.where(part == i, wht[:, here], wt_mine)
    gh_o[...] = gt_mine * scale
    fresh = wt_mine - move * step
    nh_o[...] = fresh
    nh_low[...] = fresh.astype(bf16)

    lines = grads(seg_a + 2 * finp + classp, 16).astype(f32)
    for i in range(4):
        gb[0:1, i * hidden : (i + 1) * hidden] = lines[i : i + 1, :]
    size = bias.shape[0]
    g = gb[0:1, 0:size] * scale
    bias = bias[...].reshape(1, size)
    new_m = beta_one * bm[...].reshape(1, size) + (1.0 - beta_one) * g
    new_v = beta_two * bv[...].reshape(1, size) + (1.0 - beta_two) * g * g
    m_hat = new_m / (1.0 - beta_one**STEP)
    v_hat = new_v / (1.0 - beta_two**STEP)
    m_o[...] = new_m.reshape(size)
    v_o[...] = new_v.reshape(size)
    fresh = bias - bias_rate * (m_hat / (jnp.sqrt(v_hat) + adam_eps) + weight_decay * bias)
    nb_o[...] = fresh.reshape(size)


def updates(fin, *args):
    g_all, scalars, w1, wr, wht, bias, st1, rt1, stm, rtm, sts, rts, sth, rth, bm, bv = args
    hidden = w1.shape[1]
    classes = wht.shape[0]
    count = sts.shape[1]
    n1 = (st1.shape[0], hidden)
    nr = (2, stm.shape[1], hidden)
    nh = (classes, count)

    def of(shape, kind=f32):
        return jax.ShapeDtypeStruct(shape, kind)

    one = of((1, 1))
    line = of(bias.shape)
    shapes = (
        one, one, one, of(n1), of(nr), of(nh), line, line,
        of(st1.shape), of(stm.shape), of(sts.shape), of(sth.shape),
        of(n1), of(nr), of(nh), line, of(n1, bf16), of(nr, bf16), of(nh, bf16),
    )
    inside = pl.BlockSpec(memory_space=pltpu.VMEM)
    return pl.pallas_call(
        functools.partial(update_kernel, fin),
        out_shape=shapes,
        in_specs=[inside] * len(args),
        out_specs=(inside,) * len(shapes),
        scratch_shapes=[
            pltpu.VMEM((2 * fin, hidden), f32),
            pltpu.VMEM(n1, f32),
            pltpu.VMEM(n1, f32),
            pltpu.VMEM((4, hidden, hidden), f32),
            pltpu.VMEM((1, 4 * hidden), f32),
        ],
        compiler_params=pltpu.CompilerParams(vmem_limit_bytes=40 * 2**20),
        name="update_step",
    )(*args)


def shards(
    features, nbr_index, nbr_mask, send_rows, send_count, labels, seed_mask,
    w_first, w_rest, w_head, biases,
    stat_big, root_big, stat_mid, root_mid, stat_sq, root_sq, stat_hr, root_hr, bias_m, bias_v,
):
    peers = send_rows.shape[2]
    cap = send_rows.shape[3]
    fin = features.shape[2]
    fan = nbr_index.shape[3]
    seeds = labels.shape[1]

    codes = jnp.where(nbr_mask[0] == 1, nbr_index[0], MASKED).astype(f32)

    g_all, scalars = summed_gradients(
        peers, cap, seeds, fan,
        jnp.swapaxes(codes, 1, 2),
        send_rows[0, 0], send_count[0], labels, seed_mask,
        jnp.swapaxes(features[0], 0, 1), w_first, w_rest, w_head.T, biases,
    )
    out = list(
        updates(
            fin, g_all, scalars, w_first, w_rest, w_head.T, biases,
            stat_big, root_big, stat_mid, root_mid, stat_sq, root_sq, stat_hr, root_hr,
            bias_m, bias_v,
        )
    )
    for i in (0, 1, 2):
        out[i] = out[i].reshape(())
    for i in (5, 14, 18):
        out[i] = out[i].T
    return tuple(out)


highest = lax.Precision.HIGHEST


def plain_activate(z):
    act = jax.nn.gelu(z, approximate=True)
    return act * lax.rsqrt(jnp.sum(act * act, axis=-1, keepdims=True) + norm_eps)


def plain_counts(nbr, mask, columns):
    nodes, slots = nbr.shape
    column_ids = jnp.arange(columns, dtype=jnp.int32)[None, :]
    mask_low = mask.astype(jnp.bfloat16)

    def add_slot(slot, total):
        picks = lax.dynamic_slice_in_dim(nbr, slot, 1, 1)
        weight = lax.dynamic_slice_in_dim(mask_low, slot, 1, 1)
        return total + (picks == column_ids).astype(jnp.bfloat16) * weight

    return lax.fori_loop(0, slots, add_slot, jnp.zeros((nodes, columns), jnp.bfloat16))


def plain_forward(h, weight, bias, nbr, mask, send_list, valid):
    nodes, width = h.shape
    hb = h.astype(jnp.bfloat16)
    outgoing = (
        jnp.take(hb, send_list, axis=0).reshape(valid.shape[0], valid.shape[1], width)
        * valid[:, :, None]
    )
    incoming = lax.all_to_all(outgoing, "dom", split_axis=0, concat_axis=0, tiled=True)
    table = jnp.concatenate([hb, incoming.reshape(-1, width)], axis=0)
    counts = plain_counts(nbr, mask, table.shape[0])
    degree = jnp.maximum(jnp.sum(mask, axis=1), 1).astype(jnp.float32)[:, None]
    gathered = jnp.dot(counts, table, preferred_element_type=jnp.float32)
    joined = jnp.concatenate([hb, (gathered / degree).astype(jnp.bfloat16)], axis=1)
    z = jnp.dot(joined, weight.astype(jnp.bfloat16), preferred_element_type=jnp.float32) + bias
    return (plain_activate(z), (joined, counts, degree, z))


def plain_backward(grad_out, weight, kept, send_list, valid, need_input):
    joined, counts, degree, z = kept
    nodes = joined.shape[0]
    width = joined.shape[1] // 2
    grad_z = jax.vjp(plain_activate, z)[1](grad_out)[0].astype(jnp.bfloat16)
    grad_w = jnp.einsum("nk,nh->kh", joined, grad_z, preferred_element_type=jnp.float32)
    grad_b = jnp.sum(grad_z.astype(jnp.float32), axis=0)
    if not need_input:
        return (grad_w, grad_b, None)
    grad_joined = jnp.einsum(
        "nh,kh->nk", grad_z, weight.astype(jnp.bfloat16), preferred_element_type=jnp.float32
    )
    grad_gathered = (grad_joined[:, width:] / degree).astype(jnp.bfloat16)
    grad_table = jnp.einsum("nj,nw->jw", counts, grad_gathered, preferred_element_type=jnp.float32)
    returned = (
        grad_table[nodes:].reshape(valid.shape[0], valid.shape[1], width).astype(jnp.bfloat16)
    )
    returned = lax.all_to_all(returned, "dom", split_axis=0, concat_axis=0, tiled=True)
    sent_back = (returned * valid[:, :, None]).reshape(-1, width)
    placement = (send_list[:, None] == jnp.arange(nodes, dtype=jnp.int32)[None, :]).astype(
        jnp.bfloat16
    )
    scattered = jnp.einsum("sn,sw->nw", placement, sent_back, preferred_element_type=jnp.float32)
    return (grad_w, grad_b, grad_joined[:, :width] + grad_table[:nodes] + scattered)


def plain_shampoo(grad, weight, left, left_root, right, right_root, part, right_split):
    count = left.shape[0]
    grad_rows = lax.dynamic_slice_in_dim(grad, part * count, count, 0)
    weight_rows = lax.dynamic_slice_in_dim(weight, part * count, count, 0)
    new_left = decay * left + (1.0 - decay) * jnp.dot(grad_rows, grad.T, precision=highest)
    if right_split:
        cols = right.shape[0]
        grad_cols = lax.dynamic_slice_in_dim(grad, part * cols, cols, 1)
        new_right = decay * right + (1.0 - decay) * jnp.dot(grad_cols.T, grad, precision=highest)
    else:
        new_right = decay * right + (1.0 - decay) * jnp.dot(grad.T, grad, precision=highest)
    step = jnp.dot(jnp.dot(left_root, grad, precision=highest), right_root, precision=highest)
    return (grad_rows, new_left, new_right, weight_rows - shampoo_rate * step)


def plain_shards(
    features,
    nbr_index,
    nbr_mask,
    send_rows,
    send_count,
    labels,
    seed_mask,
    w_first,
    w_rest,
    w_head,
    biases,
    stat_big,
    root_big,
    stat_mid,
    root_mid,
    stat_sq,
    root_sq,
    stat_hr,
    root_hr,
    bias_m,
    bias_v,
):
    hidden = w_rest.shape[2]
    peers = send_rows.shape[2]
    cap = send_rows.shape[3]
    send_list = send_rows.reshape(-1)
    valid = (jnp.arange(cap)[None, :] < send_count.reshape(peers, 1)).astype(jnp.bfloat16)
    weights = [w_first, w_rest[0], w_rest[1]]
    state = features[0].astype(jnp.float32)
    kept = []
    for level in range(3):
        state, saved = plain_forward(
            state,
            weights[level],
            biases[level * hidden : (level + 1) * hidden],
            nbr_index[0, level],
            nbr_mask[0, level],
            send_list,
            valid,
        )
        kept.append(saved)
    seeds = labels.shape[1]
    top = state[:seeds].astype(jnp.bfloat16)
    head_low_w = w_head.astype(jnp.bfloat16)
    logits = jnp.dot(top, head_low_w, preferred_element_type=jnp.float32) + biases[3 * hidden :]
    lse = jax.nn.logsumexp(logits, axis=1)
    onehot = (labels[0][:, None] == jnp.arange(logits.shape[1])[None, :]).astype(jnp.float32)
    picked = jnp.sum(logits * onehot, axis=1)
    seed_weight = seed_mask[0].astype(jnp.float32)
    loss_sum, seed_total = lax.psum(
        (jnp.sum((lse - picked) * seed_weight), jnp.sum(seed_weight)), ("dom", "rep")
    )
    grad_logits = (
        (jnp.exp(logits - lse[:, None]) - onehot) * (seed_weight / seed_total)[:, None]
    ).astype(jnp.bfloat16)
    grad_head = jnp.einsum("sh,sc->hc", top, grad_logits, preferred_element_type=jnp.float32)
    grad_hbias = jnp.sum(grad_logits.astype(jnp.float32), axis=0)
    grad_head, grad_hbias = (grad_head, grad_hbias)
    grad_top = jnp.einsum("sc,hc->sh", grad_logits, head_low_w, preferred_element_type=jnp.float32)
    grad_state = jnp.zeros(state.shape, jnp.float32).at[:seeds].set(grad_top)
    results = [None, None, None]
    for level in (2, 1, 0):
        grad_w, grad_b, grad_state = plain_backward(
            grad_state, weights[level], kept[level], send_list, valid, level > 0
        )
        results[level] = (grad_w, grad_b)
    grad_bias = jnp.concatenate([results[0][1], results[1][1], results[2][1], grad_hbias])
    grad_one, grad_two, grad_three = (results[0][0], results[1][0], results[2][0])
    grad_one, grad_two, grad_three, grad_head, grad_bias = lax.psum(
        (grad_one, grad_two, grad_three, grad_head, grad_bias), ("dom", "rep")
    )
    everything = (grad_one, grad_two, grad_three, grad_head, grad_bias)
    grad_norm = jnp.sqrt(sum((jnp.sum(g * g) for g in everything)))
    factor = clip_limit / jnp.maximum(grad_norm, clip_limit)
    grad_one, grad_two, grad_three, grad_head, grad_bias = [g * factor for g in everything]
    part = lax.axis_index("rep")
    head_rows = stat_sq.shape[1]
    head_root_rows = lax.dynamic_slice_in_dim(root_sq[3], part * head_rows, head_rows, 0)
    g_first, l_first, r_first, n_first = plain_shampoo(
        grad_one, w_first, stat_big, root_big, stat_sq[0], root_sq[0], part, True
    )
    g_mid0, l_mid0, r_mid0, n_mid0 = plain_shampoo(
        grad_two, w_rest[0], stat_mid[0], root_mid[0], stat_sq[1], root_sq[1], part, True
    )
    g_mid1, l_mid1, r_mid1, n_mid1 = plain_shampoo(
        grad_three, w_rest[1], stat_mid[1], root_mid[1], stat_sq[2], root_sq[2], part, True
    )
    g_head, l_head, r_head, n_head = plain_shampoo(
        grad_head, w_head, stat_sq[3], head_root_rows, stat_hr, root_hr, part, False
    )
    new_m = beta_one * bias_m + (1.0 - beta_one) * grad_bias
    new_v = beta_two * bias_v + (1.0 - beta_two) * grad_bias * grad_bias
    m_hat = new_m / (1.0 - beta_one**STEP)
    v_hat = new_v / (1.0 - beta_two**STEP)
    new_b = biases - bias_rate * (m_hat / (jnp.sqrt(v_hat) + adam_eps) + weight_decay * biases)
    new_rest = jnp.stack([n_mid0, n_mid1])
    return (
        loss_sum,
        seed_total,
        grad_norm,
        g_first,
        jnp.stack([g_mid0, g_mid1]),
        g_head,
        new_m,
        new_v,
        l_first,
        jnp.stack([l_mid0, l_mid1]),
        jnp.stack([r_first, r_mid0, r_mid1, l_head]),
        r_head,
        n_first,
        new_rest,
        n_head,
        new_b,
        n_first.astype(jnp.bfloat16),
        new_rest.astype(jnp.bfloat16),
        n_head.astype(jnp.bfloat16),
    )


def solution(mesh):
    placed = (
        P("rep", "dom", None),
        P("rep", None, "dom", None),
        P("rep", None, "dom", None),
        P("rep", "dom", None, None),
        P("rep", "dom", None),
        P("rep", "dom"),
        P("rep", "dom"),
        P(), P(), P(), P(),
        P("rep", None),
        P("rep", None),
        P(None, "rep", None),
        P(None, "rep", None),
        P(None, "rep", None),
        P(), P(), P(), P(), P(),
    )
    small = mesh.shape["rep"] == 4 and mesh.shape["dom"] == 8
    return jax.shard_map(
        shards if small else plain_shards,
        mesh=mesh,
        in_specs=placed,
        out_specs=(
            P(), P(), P(),
            P("rep", None), P(None, "rep", None), P("rep", None),
            P(), P(),
            P("rep", None), P(None, "rep", None), P(None, "rep", None), P(),
            P("rep", None), P(None, "rep", None), P("rep", None), P(),
            P("rep", None), P(None, "rep", None), P("rep", None),
        ),
        check_vma=False,
    )
```

time: 138 us -> 94.5 us (0.68)
  matrix products: 12.9 us -> 0 us
  other arithmetic: 13.3 us -> 1.88 us
  Pallas kernels: 99.4 us -> 90 us
  local copies, waits for them, and re-layouts: 7.55 us -> 1.3 us
  between operations: 4.18 us -> 1.04 us
    dot_general x16 -> x0, matrix products: 12.9 us -> none  [the longest x4 4.38 us: shampoo(): jnp.dot(jnp.dot(left_root, grad.astype(f32), precision=high), right_root,...]
    pallas_call x1 -> x2, Pallas kernels: 99.4 us -> 90 us  [the longest x1 84.8 us: summed_gradients(): pl.pallas_call(functools.partial(graph_kernel, peers, cap, seeds, fan), o...]
    another operation x7 -> x0, other arithmetic: 3.74 us -> none  [the longest x1 0.83 us: shards(): jnp.stack([l_mid0, l_mid1])]
    reduce_sum x1 -> x0, other arithmetic: 2.61 us -> none  [shards(): grad_norm = jnp.sqrt(jnp.sum(wide * wide)) / seed_total]
    reshape x4 -> x0, local copies, waits for them, and re-layouts: 2.2 us -> none  [the longest x1 1.28 us: shards(): bias = jnp.pad(biases, (0, 1024 - biases.shape[0])).reshape(8, 128)]
    mul x2 -> x0, other arithmetic: 1.8 us -> none  [shampoo(): grad_rows.astype(f32) * scale]
    slice x8 -> x0, local copies, waits for them, and re-layouts: 1.49 us -> none  [the longest x1 1.34 us: shards(): loss_sum, seed_total = (scalars[0, 0], scalars[0, 1])]
    squeeze x4 -> x0, local copies, waits for them, and re-layouts: 1.39 us -> none  [the longest x1 0.72 us: shards(): c1 = codes[0]]
where the time goes in v2:
time: 94.5 us; the launch traced here: 94.2 us
  Pallas kernels  90 us (95%)
  other arithmetic  1.88 us (2%)
  local copies, waits for them, and re-layouts  1.3 us (1%)
  between operations  1.04 us (1%)
    pallas_call x1, Pallas kernels, summed_gradients(): pl.pallas_call(functools.partial(graph_kernel, peers, cap, seeds, fan), o...  84.8 us
    pallas_call x1, Pallas kernels, updates(): pl.pallas_call(functools.partial(update_kernel, fin), out_shape=shapes, i...  5.12 us

profile of v2, /device:TPU:1, one launch (start us, length us, event | category | flops | bytes accessed | tf_op | source)
XLA Modules:
  0.0 94.2 jit_solution(11544666793207504735)
XLA Ops:
  0.7 0.0 copy-start.11
  0.7 0.0 copy-start
  0.7 0.0 copy-start.8
  0.7 0.0 copy-start.17
  0.7 0.0 copy-start.16
  0.7 0.0 copy-start.15
  0.7 0.0 copy-start.14
  0.7 1.9 %fusion.1.code_ref = f32[3,25,2048]{2,1,0:T(8,128)S(1)} fusion(s32[1,3,2048,25]{2,0,3,1:T(1,128)} %param.22, s32[1,3,2048,25]{2,0,3,1:T(1,128)} %param.23), kind=kLoop, calls=%fused_computation.2 | loop fusion | flops 460800 | bytes 1843200 | tf_op jit(solution)/shard_map/transpose | solution.py:866
  2.6 0.0 copy-done.11
  2.6 0.0 copy-done
  2.6 0.0 copy-done.8
  2.6 0.0 copy-done.17
  2.7 0.0 copy-done.16
  2.7 0.0 copy-done.15
  2.7 0.0 copy-done.14
  2.7 0.0 copy-start.1
  2.7 1.2 %copy-done.1 = f32[2,512,256]{2,1,0:T(8,128)S(1)} copy-done((f32[2,512,256]{2,1,0:T(8,128)S(1)}, f32[2,512,256]{2,1,0:T(8,128)}, u32[]{:S(2)}) %copy-start.1) | copy-done | bytes 1048600
  3.9 0.0 copy-start.2
  3.9 0.0 copy-start.3
  3.9 0.0 copy-start.4
  3.9 0.0 copy-start.5
  3.9 0.0 copy-start.6
  3.9 0.0 copy-start.7
  4.0 0.0 copy-start.9
  4.0 0.0 copy-start.10
  4.0 0.0 copy-start.12
  4.0 0.0 copy-start.13
  4.0 84.8 %graph_step.1 = (bf16[2,2304,128]{2,1,0:T(8,128)(2,1)S(1)}, f32[8,128]{1,0:T(8,128)S(1)}) custom-call(f32[3,25,2048]{2,1,0:T(8,128)S(1)} %fusion.1.code_ref, s32[8,32]{1,0:T(8,128)S(1)} %bitcast.18, s32[1,8]{1,0:T(1,128)S(1)} %bitcast.19, s32[1,16]{1,0:T(1,128)S(1)} %copy-done.16, s32[1,16]{1,0:T(1,128)S(1)} %copy-done.17, bf16[602,2048]{1,0:T(8,128)(2,1)} %bitcast.20, ...), custom_call_target="tpu_custom_call" | custom-call | tf_op jit(solution)/shard_map/graph_step/pallas_call | solution.py:679
  88.9 0.0 copy-done.2
  88.9 0.0 copy-done.3
  88.9 0.0 copy-done.4
  88.9 0.0 copy-done.5
  88.9 0.0 copy-done.6
  88.9 0.0 copy-done.7
  88.9 0.0 copy-done.9
  88.9 0.0 copy-done.10
  88.9 0.0 copy-done.12
  88.9 0.0 copy-done.13
  89.0 5.1 %update_step.1 = (f32[1,1]{1,0:T(1,128)}, f32[1,1]{1,0:T(1,128)}, f32[1,1]{1,0:T(1,128)}, f32[301,256]{1,0:T(8,128)}, f32[2,128,256]{2,1,0:T(8,128)}, /*index=5*...) custom-call(bf16[2,2304,128]{2,1,0:T(8,128)(2,1)S(1)} %get-tuple-ele, ...), custom_call_target="tpu_custom_call" | custom-call | tf_op jit(solution)/shard_map/update_step/pallas_call | solution.py:834
Async XLA Ops:
  0.7 2.0 %copy-start.11 = (f32[809]{0:T(1024)S(1)}, f32[809]{0:T(1024)}, u32[]{:S(2)}) copy-start(f32[809]{0:T(1024)} %bias.3) | copy-start | bytes 9712
  0.7 2.0 %copy-start = (f32[1204,256]{1,0:T(8,128)S(1)}, f32[1204,256]{1,0:T(8,128)}, u32[]{:S(2)}) copy-start(f32[1204,256]{1,0:T(8,128)} %w1.1) | copy-start | bytes 3698692
  0.7 2.0 %copy-start.8 = (f32[256,41]{0,1:T(8,128)S(1)}, f32[256,41]{0,1:T(8,128)}, u32[]{:S(2)}) copy-start(f32[256,41]{0,1:T(8,128)} %param.30) | copy-start | bytes 125956
  0.7 2.0 %copy-start.17 = (s32[1,16]{1,0:T(1,128)S(1)}, s32[1,16]{1,0:T(1,128)}, u32[]{:S(2)}) copy-start(s32[1,16]{1,0:T(1,128)} %smask.1) | copy-start | bytes 196
  0.7 2.0 %copy-start.16 = (s32[1,16]{1,0:T(1,128)S(1)}, s32[1,16]{1,0:T(1,128)}, u32[]{:S(2)}) copy-start(s32[1,16]{1,0:T(1,128)} %lab.1) | copy-start | bytes 196
  0.7 2.0 %copy-start.15 = (s32[1,1,8]{2,1,0:T(1,128)S(1)}, s32[1,1,8]{2,1,0:T(1,128)}, u32[]{:S(2)}) copy-start(s32[1,1,8]{2,1,0:T(1,128)} %param.25) | copy-start | bytes 100
  0.7 2.0 %copy-start.14 = (s32[1,1,8,32]{3,2,1,0:T(8,128)S(1)}, s32[1,1,8,32]{3,2,1,0:T(8,128)}, u32[]{:S(2)}) copy-start(s32[1,1,8,32]{3,2,1,0:T(8,128)} %param.24) | copy-start | bytes 3076
  2.7 1.2 %copy-start.1 = (f32[2,512,256]{2,1,0:T(8,128)S(1)}, f32[2,512,256]{2,1,0:T(8,128)}, u32[]{:S(2)}) copy-start(f32[2,512,256]{2,1,0:T(8,128)} %wr.1) | copy-start | bytes 3145732
  3.9 84.9 %copy-start.2 = (f32[301,1204]{1,0:T(8,128)S(1)}, f32[301,1204]{1,0:T(8,128)}, u32[]{:S(2)}) copy-start(f32[301,1204]{1,0:T(8,128)} %st1.1) | copy-start | bytes 4348852
  3.9 85.0 %copy-start.3 = (f32[301,1204]{1,0:T(8,128)S(1)}, f32[301,1204]{1,0:T(8,128)}, u32[]{:S(2)}) copy-start(f32[301,1204]{1,0:T(8,128)} %rt1.1) | copy-start | bytes 4348852
  3.9 85.0 %copy-start.4 = (f32[4,256,256]{2,1,0:T(8,128)S(1)}, f32[4,256,256]{2,1,0:T(8,128)}, u32[]{:S(2)}) copy-start(f32[4,256,256]{2,1,0:T(8,128)} %rts.1) | copy-start | bytes 3145732
  3.9 85.0 %copy-start.5 = (f32[2,128,512]{2,1,0:T(8,128)S(1)}, f32[2,128,512]{2,1,0:T(8,128)}, u32[]{:S(2)}) copy-start(f32[2,128,512]{2,1,0:T(8,128)} %stm.1) | copy-start | bytes 1572868
  3.9 85.0 %copy-start.6 = (f32[2,128,512]{2,1,0:T(8,128)S(1)}, f32[2,128,512]{2,1,0:T(8,128)}, u32[]{:S(2)}) copy-start(f32[2,128,512]{2,1,0:T(8,128)} %rtm.1) | copy-start | bytes 1572868
  3.9 85.0 %copy-start.7 = (f32[4,64,256]{2,1,0:T(8,128)S(1)}, f32[4,64,256]{2,1,0:T(8,128)}, u32[]{:S(2)}) copy-start(f32[4,64,256]{2,1,0:T(8,128)} %sts.1) | copy-start | bytes 786436
  4.0 85.0 %copy-start.9 = (f32[41,41]{1,0:T(8,128)S(1)}, f32[41,41]{1,0:T(8,128)}, u32[]{:S(2)}) copy-start(f32[41,41]{1,0:T(8,128)} %sth.1) | copy-start | bytes 20176
  4.0 85.0 %copy-start.10 = (f32[41,41]{1,0:T(8,128)S(1)}, f32[41,41]{1,0:T(8,128)}, u32[]{:S(2)}) copy-start(f32[41,41]{1,0:T(8,128)} %rth.1) | copy-start | bytes 20176
  4.0 85.0 %copy-start.12 = (f32[809]{0:T(1024)S(1)}, f32[809]{0:T(1024)}, u32[]{:S(2)}) copy-start(f32[809]{0:T(1024)} %bm.1) | copy-start | bytes 9712
  4.0 85.0 %copy-start.13 = (f32[809]{0:T(1024)S(1)}, f32[809]{0:T(1024)}, u32[]{:S(2)}) copy-start(f32[809]{0:T(1024)} %bv.1) | copy-start | bytes 9712

commit v3 on v2

v3 whole, which is shorter than its diff:
```python
import functools

import jax
import jax.numpy as jnp
from jax import lax
from jax.experimental import pallas as pl
from jax.experimental.pallas import tpu as pltpu
from jax.sharding import PartitionSpec as P

STEP = 5
FAN_REST = 10

clip_limit = 0.0001
decay = 0.5
shampoo_rate = 1.0
beta_one = 0.9
beta_two = 0.999
bias_rate = 0.05
weight_decay = 0.01
adam_eps = 1e-08
norm_eps = 1e-06
MASKED = 8192

bf16 = jnp.bfloat16
f32 = jnp.float32
i32 = jnp.int32
MESH = pl.DeviceIdType.MESH


def nn(a, b):
    return jnp.dot(a, b, preferred_element_type=f32)


def nt(a, b):
    return lax.dot_general(a, b, (((1,), (1,)), ((), ())), preferred_element_type=f32)


def flip(a):
    return a.astype(f32).T.astype(a.dtype)


def round_up(a, b):
    return (a + b - 1) // b * b


def gelu(z):
    scale = 0.7978845608028654
    return z * (0.5 + 0.5 * jnp.tanh(z * (scale + (0.044715 * scale) * (z * z))))


def gelu_slope(z):
    scale = 0.7978845608028654
    square = z * z
    half = 0.5 + 0.5 * jnp.tanh(z * (scale + (0.044715 * scale) * square))
    return half + (half - half * half) * (z * (2.0 * scale + (6.0 * 0.044715 * scale) * square))


def norm_root(act, axis):
    return lax.rsqrt(jnp.sum(act * act, axis=axis, keepdims=True) + norm_eps)


def pull_back(act, slope, root, grad, axis):
    dot = jnp.sum(act * grad, axis=axis, keepdims=True)
    return (slope * (root * grad - act * (root * root * root * dot))).astype(bf16)


def as_column(row):
    return jnp.broadcast_to(row, (8, row.shape[1])).T[:, 0:1]


def widen(row, width, value=0):
    return jnp.concatenate([row, jnp.full((1, width - row.shape[1]), value, row.dtype)], axis=1)


def graph_kernel(
    peers, cap, seeds, fan,
    nbr_hbm, msk_hbm, xt_hbm, w1_hbm, wr_hbm, srow_hbm, scnt_hbm, lab_hbm, smask_hbm, wht_hbm, bias_hbm,
    g_out, s_out,
    nbr, msk, xt, srow, scnt, lab, smask, wht, bias, joined, near, chosen, far2, far2t, grad1, ctmp, crow, lrow, lcode, crow2, lrow2, rdeg,
    w1, wr, w1t, act1, slope1, root1, h1t, ob0, ib0, ob1, ib1, ob2, ib2, ob3, ib3, ob4, ib4, ob5, ib5,
    gl, acc, rc, sbq, rbq, sbz, rbz, gout, ssend, srecv, sqv, szv,
    load_sem, send_sem, recv_sem, red_send, red_recv,
):
    fin, nodes = xt.shape
    hidden = w1.shape[1]
    finp = round_up(fin, 16)
    slots = peers * cap
    table = nodes + slots
    groups = table // 128
    chunks = nodes // 128
    blocks = nodes // 256
    span = far2.shape[0]
    local = span - slots
    me = lax.axis_index("dom")
    rep = lax.axis_index("rep")
    core = lax.rem(rep, 2)
    xpos = rep // 2
    ypos = lax.rem(me, 2)
    zpos = me // 2
    nz = peers // 2
    mate_c = xpos * 2 + (1 - core)
    mate_x = (1 - xpos) * 2 + core
    mate_y = zpos * 2 + (1 - ypos)

    loads = [
        pltpu.make_async_copy(src, dst, load_sem.at[k])
        for k, (src, dst) in enumerate(
            (
                (srow_hbm, srow), (scnt_hbm, scnt), (xt_hbm, xt), (nbr_hbm, nbr), (msk_hbm, msk),
                (w1_hbm, w1), (wr_hbm, wr), (lab_hbm, lab), (smask_hbm, smask), (wht_hbm, wht), (bias_hbm, bias),
            )
        )
    ]
    for load in loads:
        load.start()
    barrier = pltpu.get_barrier_semaphore()
    for off in range(1, peers):
        pl.semaphore_signal(barrier, inc=1, device_id={"dom": lax.rem(me + off, peers)}, device_id_type=MESH)
    for mate in (mate_c, mate_x):
        pl.semaphore_signal(barrier, inc=1, device_id={"rep": mate}, device_id_type=MESH)
    mate_xy = {"dom": mate_y, "rep": mate_x}
    pl.semaphore_signal(barrier, inc=1, device_id=mate_xy, device_id_type=MESH)

    def exchange(stage, src, dst, same=False):
        size = dst.shape[0] // peers
        copies = []
        for off in range(1, peers):
            peer = lax.rem(me + off, peers)
            copies.append(
                pltpu.make_async_remote_copy(
                    src_ref=src if same else src.at[pl.ds(pl.multiple_of(peer * size, 16), size)],
                    dst_ref=dst.at[pl.ds(pl.multiple_of(me * size, 16), size)],
                    send_sem=send_sem.at[stage, off - 1],
                    recv_sem=recv_sem.at[stage, off - 1],
                    device_id={"dom": peer},
                    device_id_type=MESH,
                )
            )
        for c in copies:
            c.start()
        return copies

    started = []

    def finish(copies):
        for c in copies:
            c.wait_recv()
        started.extend(copies)

    loads[0].wait()
    loads[1].wait()
    count = jnp.broadcast_to(scnt[...], (peers, peers))
    count = jnp.where(
        lax.broadcasted_iota(i32, (peers, peers), 0) == lax.broadcasted_iota(i32, (peers, peers), 1), count, 0
    )
    count = jnp.sum(count.astype(f32), axis=1, keepdims=True)
    in_use = lax.broadcasted_iota(i32, (peers, cap), 1).astype(f32) < count
    slot = jnp.where(in_use, srow[...].astype(f32), -1.0)
    per = 128 // cap
    slot = jnp.concatenate([slot] * per, axis=1)
    owner = lax.broadcasted_iota(i32, (peers, 128), 0)
    place = lax.broadcasted_iota(i32, (peers, 128), 1) // cap
    send_row = jnp.concatenate(
        [
            jnp.sum(jnp.where(owner == place + t * per, slot, 0.0), axis=0, keepdims=True)
            for t in range(slots // 128)
        ],
        axis=1,
    )
    node_id = lax.broadcasted_iota(i32, (256, nodes), 1).astype(f32)
    send_col = as_column(send_row)
    for r in range(0, slots, 256):
        chosen[r : r + 256, :] = jnp.where(send_col[r : r + 256] == node_id, 1.0, 0.0).astype(bf16)
    line = lax.broadcasted_iota(i32, (16, nodes), 0)
    joined[finp - 16 : finp, :] = jnp.where(line == 16 - (finp - fin), 1.0, 0.0).astype(bf16)
    r_id = lax.broadcasted_iota(i32, (2 * seeds, local), 0)
    l_id = lax.broadcasted_iota(i32, (2 * seeds, local), 1)
    is_self = (r_id < seeds) & (l_id == r_id + FAN_REST * seeds)
    is_nbr = (r_id >= seeds) & (l_id < FAN_REST * seeds) & (lax.rem(l_id, seeds) == r_id - seeds)
    spread = jnp.where(is_self | is_nbr, 1.0, 0.0)
    spread_t = spread.T.astype(bf16)
    spread = spread.astype(bf16)
    loads[2].wait()
    joined[0:fin, :] = xt[...]
    ob0[:, finp:] = jnp.zeros((slots, ob0.shape[1] - finp), bf16)
    ob0[:, 0:finp] = nt(chosen[0:slots, :], joined[0:finp, :]).astype(bf16)
    for buf in (ib0, ib1, ib2, ib3, ib4, ib5):
        size = buf.shape[0] // peers
        buf[pl.ds(pl.multiple_of(me * size, 16), size), :] = jnp.zeros((size, buf.shape[1]), bf16)
    pl.semaphore_wait(barrier, peers - 1 + 3)
    sent = exchange(0, ob0, ib0)

    loads[3].wait()
    loads[4].wait()

    def codes(level, size, here):
        at = slice(0, size)
        return jnp.where(msk[level, at, 0, here] == 1, nbr[level, at, 0, here], MASKED).astype(f32)

    code3 = codes(2, FAN_REST, slice(0, 128))
    code3t = jnp.concatenate([code3, jnp.full((16 - FAN_REST, 128), float(MASKED), f32)], axis=0).T[0:seeds]
    degree = jnp.sum(jnp.where(code3t < float(MASKED), 1.0, 0.0), axis=1, keepdims=True)
    rdeg3 = 1.0 / jnp.maximum(degree, 1.0)
    tiled = jnp.concatenate([code3t] * peers, axis=0)
    r_id = lax.broadcasted_iota(i32, (peers * seeds, 128), 0)
    l_id = lax.broadcasted_iota(i32, (peers * seeds, 128), 1)
    wanted = jnp.where(l_id < cap, nodes + (r_id // seeds) * cap + l_id, -1).astype(f32)
    far3 = jnp.zeros(wanted.shape, f32)
    for k in range(FAN_REST):
        far3 = far3 + jnp.where(wanted == tiled[:, k : k + 1], 1.0, 0.0)
    ob5[...] = far3.astype(bf16)
    sent_far = exchange(5, ob5, ib5)

    fill = jnp.full((32 - fan, 128), float(MASKED), f32)
    fill2 = jnp.full((16 - FAN_REST, 128), float(MASKED), f32)
    for c in range(chunks):
        here = slice(c * 128, (c + 1) * 128)
        code = codes(0, fan, here)
        degree = jnp.sum((code < MASKED).astype(f32), axis=0, keepdims=True)
        rdeg[0:1, here] = 1.0 / jnp.maximum(degree, 1.0)
        code2 = jnp.concatenate([codes(1, FAN_REST, here), fill2], axis=0).astype(i32)
        ctmp[here, 0:64] = jnp.concatenate(
            [code, fill, (code2 >> 7).astype(f32), (code2 & 127).astype(f32)], axis=0
        ).T

    def grouped(source, count, width):
        each = 256 // width
        lane = lax.broadcasted_iota(i32, (count, 256), 1) // width
        code = jnp.zeros((count, 256), f32)
        for n in range(each):
            piece = source[pl.ds(n, count, stride=each), :]
            piece = jnp.concatenate([piece, piece], axis=1)
            piece = pltpu.roll(piece, n * width, 1) if n else piece
            code = jnp.where(lane == n, piece, code)
        code = code.astype(i32)
        return ((code >> 7) * each + lane).astype(f32), (code & 127).astype(f32)

    crow[...], lrow[...] = grouped(ctmp, nodes // 8, 32)

    lane = lax.broadcasted_iota(i32, (1, 128), 1)
    fits = 128 // seeds
    tiles = []
    for t in range(local // 128):
        tile = jnp.full((1, 128), -1.0, f32)
        for j in range(fits):
            k = t * fits + j
            here = lane // seeds == j
            if k < FAN_REST:
                piece = code3[k : k + 1, :]
                piece = pltpu.roll(piece, j * seeds, 1) if j else piece
                tile = jnp.where(here & (piece < nodes), piece, tile)
            elif k == FAN_REST:
                tile = jnp.where(here, (lane - j * seeds).astype(f32), tile)
        tiles.append(tile)
    local_col = as_column(jnp.concatenate(tiles, axis=1))
    for r in range(0, local, 256):
        chosen[slots + r : slots + r + 256, :] = jnp.where(
            local_col[r : r + 256] == node_id, 1.0, 0.0
        ).astype(bf16)
    keep = jnp.where(jnp.concatenate([send_col, local_col], axis=0) >= 0.0, 1.0, 0.0)
    found = nn(chosen[0:span, :], ctmp[...].astype(bf16))
    lcode[...] = pltpu.roll(found, 96, 1) * 128.0 + pltpu.roll(found, 80, 1)
    lane = lax.broadcasted_iota(i32, (span, 128), 1)
    degree = jnp.sum(
        jnp.where((lcode[...] < float(MASKED)) & (lane < FAN_REST), 1.0, 0.0), axis=1, keepdims=True
    )
    rdeg2 = 1.0 / jnp.maximum(degree, 1.0)
    crow2[...], lrow2[...] = grouped(lcode, span // 16, 16)

    rows_a = lax.broadcasted_iota(i32, (groups * 8, 256), 0).astype(f32)
    rows_b = lax.broadcasted_iota(i32, (128, 256), 0).astype(f32)
    rows_c = lax.broadcasted_iota(i32, (groups * 16, 256), 0).astype(f32)

    def list_counts(b, _):
        for p in range(16):
            g = b * 16 + p
            left = jnp.where(rows_c == crow2[pl.ds(g, 1), :], 1.0, 0.0).astype(bf16)
            right = jnp.where(rows_b == lrow2[pl.ds(g, 1), :], 1.0, 0.0).astype(bf16)
            value = nt(left, right).astype(bf16)
            for a in range(groups):
                tile = value[a * 16 : (a + 1) * 16]
                if a < chunks:
                    chosen[pl.ds(pl.multiple_of(span + g * 16, 16), 16), a * 128 : (a + 1) * 128] = tile
                else:
                    at = pl.ds(pl.multiple_of(g * 16, 16), 16)
                    far2[at, (a - chunks) * 128 : (a - chunks + 1) * 128] = tile
        return 0

    lax.fori_loop(0, span // 256, list_counts, 0)

    def build(b, _):
        for p in range(16):
            pair = []
            for half in range(2):
                g = b * 32 + p * 2 + half
                left = jnp.where(rows_a == crow[pl.ds(g, 1), :], 1.0, 0.0).astype(bf16)
                right = jnp.where(rows_b == lrow[pl.ds(g, 1), :], 1.0, 0.0).astype(bf16)
                pair.append(nt(left, right))
            at = pl.ds(pl.multiple_of(b * 256 + p * 16, 16), 16)
            for a in range(groups):
                tile = jnp.concatenate([pair[0][a * 8 : (a + 1) * 8], pair[1][a * 8 : (a + 1) * 8]], axis=0)
                near[at, a * 128 : (a + 1) * 128] = tile.astype(bf16)
        return 0

    lax.fori_loop(0, blocks, build, 0)

    for load in loads[5:]:
        load.wait()
    bias = bias[...].reshape(1, bias.shape[0])
    wpad = jnp.concatenate(
        [w1[0:fin, :], jnp.zeros((finp - fin, hidden), f32), w1[fin : 2 * fin, :], jnp.zeros((finp - fin, hidden), f32)],
        axis=0,
    )
    w1t[...] = wpad.T.astype(bf16)
    b1 = as_column(bias[0:1, 0:hidden])

    finish(sent)
    ibt = flip(ib0[...])[0:finp, :]

    def block(b):
        return pl.ds(b * 256 if isinstance(b, int) else pl.multiple_of(b * 256, 256), 256)

    def gather(b):
        blk = block(b)
        total = nt(joined[0:finp, :], near[blk, 0:nodes]) + nt(ibt, near[blk, nodes:])
        joined[finp:, blk] = (total * rdeg[0:1, blk]).astype(bf16)

    def product(b):
        blk = block(b)
        grad1[:, blk] = nn(w1t[...], joined[:, blk]) + b1

    def activate(b):
        blk = block(b)
        z = grad1[:, blk]
        act = gelu(z)
        slope1[:, blk] = gelu_slope(z)
        root = norm_root(act, 0)
        act1[:, blk] = act
        root1[0:1, blk] = root
        h1t[:, blk] = (act * root).astype(bf16)

    gather(0)
    far2t[...] = flip(far2[...])
    w2 = wr[0].astype(bf16)
    w3 = wr[1].astype(bf16)
    product(0)
    gather(1)

    def layer_one(b, _):
        activate(b - 2)
        product(b - 1)
        gather(b)
        return 0

    lax.fori_loop(2, blocks, layer_one, 0)
    activate(blocks - 2)
    product(blocks - 1)
    activate(blocks - 1)
    sent_rows = nt(chosen[0:slots, :], h1t[...]).astype(bf16)
    ob1[...] = sent_rows
    sent = exchange(1, ob1, ib1)

    own2 = nt(chosen[slots:, :], h1t[...])
    finish(sent_far)
    far3r = ib5[...].astype(f32)[:, 0:cap]
    spots = peers * cap
    r_id = lax.broadcasted_iota(i32, (peers * seeds, spots), 0) // seeds
    l_id = lax.broadcasted_iota(i32, (peers * seeds, spots), 1) // cap
    collect = jnp.where(r_id == l_id, jnp.concatenate([far3r] * peers, axis=1), 0.0)
    scatter = collect.T.astype(bf16)
    collect = collect.astype(bf16)

    finish(sent)

    def rows_two(own_self, own_sum, at):
        agg = (own_sum + nn(far2[at, :], ib1[...])) * rdeg2[at]
        both = jnp.concatenate([own_self, agg.astype(bf16)], axis=1)
        z = nn(both, w2) + bias[0:1, hidden : 2 * hidden]
        act = gelu(z)
        root = norm_root(act, 1)
        return both, z, act, root, (act * (root * keep[at])).astype(bf16)

    out_at, in_at = slice(0, slots), slice(slots, span)
    joined2a, z2a, act2a, root2a, h2a = rows_two(sent_rows, own2[local:span], out_at)
    ob2[...] = nn(collect, h2a).astype(bf16)
    sent = exchange(2, ob2, ib2)

    joined2b, z2b, act2b, root2b, h2b = rows_two(own2[0:local].astype(bf16), own2[span:], in_at)
    near3 = nn(spread, h2b)
    slope2b = gelu_slope(z2b)
    classes = wht.shape[0]
    classp = round_up(classes, 16)
    wht_low = jnp.concatenate([wht[...], jnp.zeros((classp - classes, hidden), f32)], axis=0).astype(bf16)
    bh = widen(bias[0:1, 3 * hidden : 3 * hidden + classes], classp)
    class_id = lax.broadcasted_iota(i32, (seeds, classp), 1)
    label = as_column(widen(lab[...].astype(f32), 128))[0:seeds]
    hot = jnp.where(class_id.astype(f32) == label, 1.0, 0.0)
    weight = as_column(widen(smask[...].astype(f32), 128))[0:seeds]
    finish(sent)
    total = near3[seeds:]
    for q in range(peers):
        total = total + ib2[q * seeds : (q + 1) * seeds, :].astype(f32)
    joined3 = jnp.concatenate([near3[0:seeds].astype(bf16), (total * rdeg3).astype(bf16)], axis=1)
    z3 = nn(joined3, w3) + bias[0:1, 2 * hidden : 3 * hidden]
    act3 = gelu(z3)
    slope3 = gelu_slope(z3)
    root3 = norm_root(act3, 1)
    top = (act3 * root3).astype(bf16)

    logits = nt(top, wht_low) + bh
    logits = jnp.where(class_id < classes, logits, -1e30)
    peak = jnp.max(logits, axis=1, keepdims=True)
    lse = peak + jnp.log(jnp.sum(jnp.exp(logits - peak), axis=1, keepdims=True))
    dlog = ((jnp.exp(logits - lse) - hot) * weight).astype(bf16)
    dtop = nn(dlog, wht_low)

    dz3 = pull_back(act3, slope3, root3, dtop, 1)
    dj3 = nt(dz3, w3)
    dg3 = (dj3[:, hidden:] * rdeg3).astype(bf16)
    ob3[...] = dg3
    sent = exchange(3, ob3, ib3, same=True)
    dloc = nn(spread_t, jnp.concatenate([dj3[:, 0:hidden].astype(bf16), dg3], axis=0))

    seg_a = 4 * hidden
    row_head = seg_a + 2 * finp
    row_bias = row_head + classp
    rows = gl.shape[1]

    def put(row, value):
        size = value.shape[0]
        gl[0, row : row + size, :] = value[:, 0:128].astype(bf16)
        gl[1, row : row + size, :] = value[:, 128:].astype(bf16)

    picked = jnp.sum(logits * hot, axis=1, keepdims=True)
    loss = jnp.sum((lse - picked) * weight, axis=0, keepdims=True)
    total = jnp.sum(weight, axis=0, keepdims=True)
    sc_lane = lax.broadcasted_iota(i32, (8, 128), 1)
    ssend[0] = jnp.where(sc_lane == 0, loss, jnp.where(sc_lane == 1, total, 0.0))
    dz2b = pull_back(act2b, slope2b, root2b, dloc * keep[in_at], 1)
    dj2b = nt(dz2b, w2)
    dg2b = (dj2b[:, hidden:] * rdeg2[in_at]).astype(bf16)
    near_ret = nn(far2t[:, in_at], dg2b)
    slope2a = gelu_slope(z2a)
    put(row_head, nn(dlog.astype(f32).T.astype(bf16), top))
    put(2 * hidden, nn(joined3.astype(f32).T.astype(bf16), dz3))
    bias_3 = jnp.sum(dz3.astype(f32), axis=0, keepdims=True)
    bias_h = widen(jnp.sum(dlog.astype(f32), axis=0, keepdims=True), hidden)
    finish(sent)

    dh2a = nn(scatter, ib3[...]) * keep[out_at]
    dz2a = pull_back(act2a, slope2a, root2a, dh2a, 1)
    dj2a = nt(dz2a, w2)
    dg2a = (dj2a[:, hidden:] * rdeg2[out_at]).astype(bf16)
    ob4[...] = (near_ret + nn(far2t[:, out_at], dg2a)).astype(bf16)
    sent = exchange(4, ob4, ib4)
    put(0, nn(flip(joined2a), dz2a) + nn(flip(joined2b), dz2b))

    used = []

    def hop(src, dst, who):
        used.append(0)
        k = len(used) - 1
        copy = pltpu.make_async_remote_copy(
            src_ref=src, dst_ref=dst, send_sem=red_send.at[k], recv_sem=red_recv.at[k],
            device_id=who, device_id_type=MESH,
        )
        copy.start()
        return copy

    def rows_of(start, size):
        return pl.ds(pl.multiple_of(start, 16), size)

    to_core = {"rep": mate_c}
    plane = (
        xpos * 2 + ypos,
        (
            ((1 - xpos) * 2 + ypos, {"rep": mate_x}),
            (xpos * 2 + 1 - ypos, {"dom": mate_y}),
            ((1 - xpos) * 2 + 1 - ypos, mate_xy),
        ),
    )
    others = [lax.rem(zpos + off, nz) for off in range(1, nz)]
    column = (zpos, tuple((to, {"dom": to * 2 + ypos}) for to in others))

    def summing(start, size, out_sem, one, two):
        (mine1, group1), (mine2, group2) = one, two
        quarter = size // (len(group1) + 1)
        piece = quarter // (len(group2) + 1)
        whole = slice(start, start + size)
        at1, at2 = start // 4, start // (4 * nz)
        at1, at2 = slice(at1, at1 + quarter), slice(at2, at2 + piece)
        kept = rows_of(start + mine1 * quarter, quarter)
        here = rows_of(start + mine1 * quarter + mine2 * piece, piece)
        copies = [hop(gl.at[1 - core, whole], rc.at[whole], to_core)]
        yield
        finish(copies)
        value = gl[core, whole, :].astype(f32) + rc[whole, :].astype(f32)
        acc[whole, :] = value
        sbq[whole, :] = value.astype(bf16)
        copies = [
            hop(sbq.at[rows_of(start + to * quarter, quarter)], rbq.at[k, at1], who)
            for k, (to, who) in enumerate(group1)
        ]
        yield
        finish(copies)
        value = acc[kept, :]
        for k in range(len(group1)):
            value = value + rbq[k, at1, :].astype(f32)
        acc[kept, :] = value
        sbz[at1, :] = value.astype(bf16)
        copies = [
            hop(sbz.at[rows_of(start // 4 + to * piece, piece)], rbz.at[k, at2], who)
            for k, (to, who) in enumerate(group2)
        ]
        yield
        finish(copies)
        value = acc[here, :]
        for k in range(len(group2)):
            value = value + rbz[k, at2, :].astype(f32)
        gout[core, here, :] = value.astype(bf16)
        part = gout.at[core, here]
        copies = [hop(part, part, who) for _, who in group2]
        yield
        finish(copies)
        part = gout.at[core, kept]
        copies = [hop(part, part, who) for _, who in group1]
        copies.append(hop(part, part, to_core))
        yield
        finish(copies)
        copies = []
        for to, _ in group1:
            part = gout.at[core, rows_of(start + to * quarter, quarter)]
            copies.append(hop(part, part, to_core))
        yield
        finish(copies)
        out = [
            pltpu.make_async_copy(gout.at[h, whole], g_out.at[h, whole], load_sem.at[out_sem + h])
            for h in range(2)
        ]
        for c in out:
            c.start()
        yield
        for c in out:
            c.wait()

    def summing_scalars():
        copies = [hop(ssend.at[0], srecv.at[0], to_core)]
        yield
        finish(copies)
        ssend[1] = ssend[0] + srecv[0]
        mine = plane[0]
        sqv[mine] = ssend[1]
        copies = [hop(ssend.at[1], sqv.at[mine], who) for _, who in plane[1]]
        yield
        finish(copies)
        ssend[2] = sqv[0] + sqv[1] + sqv[2] + sqv[3]
        szv[zpos] = ssend[2]
        copies = [hop(ssend.at[2], szv.at[zpos], who) for _, who in column[1]]
        yield
        finish(copies)
        total = szv[0]
        for k in range(1, nz):
            total = total + szv[k]
        s_out[...] = total

    def go_on(*runs):
        for run in runs:
            next(run, None)

    cut = seg_a + 2 * (4 * nz * 16)
    rest = summing(0, seg_a, 4, plane, column)
    first = summing(seg_a, cut - seg_a, 0, column, plane)
    second = summing(cut, rows - cut, 2, plane, column)
    scalars = summing_scalars()
    go_on(rest, scalars)

    bias_2 = jnp.sum(dz2a.astype(f32), axis=0, keepdims=True) + jnp.sum(dz2b.astype(f32), axis=0, keepdims=True)
    line = lax.broadcasted_iota(i32, (16, hidden), 0)
    put(
        row_bias,
        jnp.where(line == 1, bias_2, 0.0) + jnp.where(line == 2, bias_3, 0.0) + jnp.where(line == 3, bias_h, 0.0),
    )
    both = flip(
        jnp.concatenate(
            [dj2a[:, 0:hidden].astype(bf16), dj2b[:, 0:hidden].astype(bf16), dg2a, dg2b], axis=0
        )
    )
    grad1[...] = nn(both, chosen[...])
    go_on(rest, scalars)
    finish(sent)
    back = flip(ib4[...])

    def layer_one_back(b, _):
        blk = block(b)
        grad = grad1[:, blk] + nn(back, chosen[0:slots, blk])
        h1t[:, blk] = pull_back(act1[:, blk], slope1[:, blk], root1[0:1, blk], grad, 0)
        return 0

    lax.fori_loop(0, blocks, layer_one_back, 0)
    size = cut - seg_a
    put(seg_a, nt(joined[0:size, :], h1t[...]))
    go_on(first, rest, scalars)
    put(cut, nt(joined[size:, :], h1t[...]))
    go_on(second, first)
    for _ in range(5):
        go_on(second, first, rest, scalars)
    go_on(second, first)
    go_on(second)
    for c in started:
        c.wait_send()


def in_hbm(*arrays):
    return [pltpu.with_memory_space_constraint(a, pltpu.HBM) for a in arrays]


def summed_gradients(peers, cap, seeds, fan, nbr, msk, xt, w1, wr, srow, scnt, lab, smask, wht, bias):
    fin, nodes = xt.shape
    hidden = w1.shape[1]
    finp = round_up(fin, 16)
    wide = round_up(fin, 128)
    slots = peers * cap
    span = slots + round_up(seeds * (FAN_REST + 1), 256)
    classp = round_up(wht.shape[0], 16)
    rows = 4 * hidden + 2 * finp + classp + 16
    nz = peers // 2
    vmem = pltpu.VMEM
    sems = 64
    some = peers * seeds
    scratch = [
        vmem(nbr.shape, i32),
        vmem(msk.shape, i32),
        vmem(xt.shape, bf16),
        vmem(srow.shape, i32),
        vmem(scnt.shape, i32),
        vmem(lab.shape, i32),
        vmem(smask.shape, i32),
        vmem(wht.shape, f32),
        vmem(bias.shape, f32),
        vmem((2 * finp, nodes), bf16),
        vmem((nodes, nodes + slots), bf16),
        vmem((2 * span, nodes), bf16),
        vmem((span, slots), bf16),
        vmem((slots, span), bf16),
        vmem((hidden, nodes), f32),
        vmem((nodes, 128), f32),
        vmem((nodes // 8, 256), f32),
        vmem((nodes // 8, 256), f32),
        vmem((span, 128), f32),
        vmem((span // 16, 256), f32),
        vmem((span // 16, 256), f32),
        vmem((8, nodes), f32),
        vmem(w1.shape, f32),
        vmem(wr.shape, f32),
        vmem((hidden, 2 * finp), bf16),
        vmem((hidden, nodes), f32),
        vmem((hidden, nodes), f32),
        vmem((8, nodes), f32),
        vmem((hidden, nodes), bf16),
        vmem((slots, wide), bf16),
        vmem((slots, wide), bf16),
        vmem((slots, hidden), bf16),
        vmem((slots, hidden), bf16),
        vmem((some, hidden), bf16),
        vmem((some, hidden), bf16),
        vmem((seeds, hidden), bf16),
        vmem((some, hidden), bf16),
        vmem((slots, hidden), bf16),
        vmem((slots, hidden), bf16),
        vmem((some, 128), bf16),
        vmem((some, 128), bf16),
        vmem((2, rows, 128), bf16),
        vmem((rows, 128), f32),
        vmem((rows, 128), bf16),
        vmem((rows, 128), bf16),
        vmem((3, rows // 4, 128), bf16),
        vmem((rows // 4, 128), bf16),
        vmem((nz - 1, rows // (4 * nz), 128), bf16),
        vmem((2, rows, 128), bf16),
        vmem((4, 8, 128), f32),
        vmem((3, 8, 128), f32),
        vmem((4, 8, 128), f32),
        vmem((nz, 8, 128), f32),
        pltpu.SemaphoreType.DMA((11,)),
        pltpu.SemaphoreType.DMA((6, peers - 1)),
        pltpu.SemaphoreType.DMA((6, peers - 1)),
        pltpu.SemaphoreType.DMA((sems,)),
        pltpu.SemaphoreType.DMA((sems,)),
    ]
    inside = pl.BlockSpec(memory_space=vmem)
    outside = pl.BlockSpec(memory_space=pl.ANY)
    return pl.pallas_call(
        functools.partial(graph_kernel, peers, cap, seeds, fan),
        out_shape=(
            jax.ShapeDtypeStruct((2, rows, 128), bf16),
            jax.ShapeDtypeStruct((8, 128), f32),
        ),
        in_specs=[outside] * 11,
        out_specs=(outside, inside),
        scratch_shapes=scratch,
        compiler_params=pltpu.CompilerParams(
            collective_id=0, has_side_effects=True, vmem_limit_bytes=47 * 2**20
        ),
        cost_estimate=pl.CostEstimate(flops=24 * 10**9, bytes_accessed=12 * 2**20, transcendentals=2**20),
        name="graph_step",
    )(*in_hbm(nbr, msk, xt, w1, wr, srow, scnt, lab, smask, wht, bias))


def split_dot(a, b):
    high = a.astype(bf16)
    low = (a - high.astype(f32)).astype(bf16)
    return nn(high, b) + nn(low, b)


def three_dot(a, b):
    high = b.astype(bf16)
    low = (b - high.astype(f32)).astype(bf16)
    return split_dot(a, high) + nn(a.astype(bf16), low)


def update_kernel(
    fin,
    g_all, scalars, wht, bias, sth, rth, bm, bv,
    w1, wr, st1, rt1, stm, rtm, sts, rts,
    loss_o, total_o, norm_o, gh_o, m_o, v_o, lh_o, nh_o, nb_o, nh_low,
    g1_hbm, gr_hbm, l1_hbm, lm_hbm, ls_hbm, n1_hbm, nr_hbm, n1_low_hbm, nr_low_hbm,
    g1_o, gr_o, l1_o, lm_o, ls_o, n1_o, nr_o, n1_low, nr_low,
    g1, g_mine, w_mine, full, gb, out_sem,
):
    hidden = w1.shape[1]
    classes = wht.shape[0]
    classp = round_up(classes, 16)
    finp = round_up(fin, 16)
    seg_a = 4 * hidden
    part = lax.axis_index("rep")

    stores = []

    def store(src, dst):
        copy = pltpu.make_async_copy(src, dst, out_sem.at[len(stores)])
        stores.append(copy)
        copy.start()

    def grads(start, size):
        return jnp.concatenate(
            [g_all[0, start : start + size, :], g_all[1, start : start + size, :]], axis=1
        )

    total = scalars[0:1, 1:2]
    square = jnp.zeros((16, hidden), f32)
    spare = lax.broadcasted_iota(i32, (16, hidden), 0) >= 16 - (finp - fin)
    for r in range(0, g_all.shape[1], 16):
        g = grads(r, 16).astype(f32)
        if r == seg_a + 2 * finp - 16:
            g = jnp.where(spare, 0.0, g)
        square = square + g * g
    square = jnp.sum(jnp.sum(square, axis=0, keepdims=True), axis=1, keepdims=True)
    norm = jnp.sqrt(square) / total
    scale = clip_limit / jnp.maximum(norm, clip_limit) / total
    loss_o[...] = scalars[0:1, 0:1]
    total_o[...] = total
    norm_o[...] = norm
    lift = (1.0 - decay) * scale * scale
    move = shampoo_rate * scale

    g1[0:fin, :] = grads(seg_a, finp)[0:fin].astype(f32)
    g1[fin : 2 * fin, :] = grads(seg_a + finp, finp)[0:fin].astype(f32)
    count = st1.shape[0]
    g_low = g1[...].astype(bf16)
    full[0] = nn(g1[...].T.astype(bf16), g_low)
    half = split_dot(rt1[...], g_low)
    for i in range(2 * fin // count):

        @pl.when(part == i)
        def _():
            g_mine[...] = g1[i * count : (i + 1) * count, :]
            w_mine[...] = w1[i * count : (i + 1) * count, :]

    g_rows = g_mine[...]
    g1_o[...] = g_rows * scale
    store(g1_o, g1_hbm)
    fresh = w_mine[...] - move * three_dot(half, rts[0])
    n1_o[...] = fresh
    n1_low[...] = fresh.astype(bf16)
    store(n1_o, n1_hbm)
    store(n1_low, n1_low_hbm)
    product = nt(g_rows.astype(bf16), g_low)
    l1_o[...] = decay * st1[...] + lift * product
    store(l1_o, l1_hbm)

    count = stm.shape[1]
    at = pl.ds(pl.multiple_of(part * count, count), count)
    products = []
    for i in range(2):
        g = grads(i * 2 * hidden, 2 * hidden)
        base = pl.ds(pl.multiple_of(i * 2 * hidden + part * count, 16), count)
        g_rows = jnp.concatenate([g_all[0, base, :], g_all[1, base, :]], axis=1)
        gr_o[i] = g_rows.astype(f32) * scale
        full[1 + i] = nn(flip(g), g)
        products.append((nt(g_rows, g), three_dot(split_dot(rtm[i], g), rts[1 + i])))
    store(gr_o, gr_hbm)
    for i, (product, step) in enumerate(products):
        lm_o[i] = decay * stm[i] + lift * product
        fresh = wr[i, at, :] - move * step
        nr_o[i] = fresh
        nr_low[i] = fresh.astype(bf16)
    store(lm_o, lm_hbm)
    store(nr_o, nr_hbm)
    store(nr_low, nr_low_hbm)

    gt = grads(seg_a + 2 * finp, classp)
    full[3] = nn(flip(gt), gt)
    count = sts.shape[1]
    mine = pl.ds(pl.multiple_of(part * count, count), count)
    for i in range(4):
        ls_o[i] = decay * sts[i] + lift * full[i, mine, :]
    store(ls_o, ls_hbm)
    lh_o[...] = decay * sth[...] + lift * nt(gt, gt)[0:classes, 0:classes]
    root = rts[3, mine, :]
    high = root.astype(bf16)
    low = (root - high.astype(f32)).astype(bf16)
    left = (nt(gt, high) + nt(gt, low))[0:classes]
    step = three_dot(rth[...], left)
    gt_mine = jnp.zeros((classes, count), f32)
    wt_mine = jnp.zeros((classes, count), f32)
    gt_wide = gt.astype(f32)
    for i in range(hidden // count):
        here = slice(i * count, (i + 1) * count)
        gt_mine = jnp.where(part == i, gt_wide[0:classes, here], gt_mine)
        wt_mine = jnp.where(part == i, wht[:, here], wt_mine)
    gh_o[...] = gt_mine * scale
    fresh = wt_mine - move * step
    nh_o[...] = fresh
    nh_low[...] = fresh.astype(bf16)

    lines = grads(seg_a + 2 * finp + classp, 16).astype(f32)
    gb[0:1, 0:hidden] = grads(seg_a + finp - 16, 16).astype(f32)[fin - finp + 16 : fin - finp + 17, :]
    for i in range(1, 4):
        gb[0:1, i * hidden : (i + 1) * hidden] = lines[i : i + 1, :]
    size = bias.shape[0]
    g = gb[0:1, 0:size] * scale
    bias = bias[...].reshape(1, size)
    new_m = beta_one * bm[...].reshape(1, size) + (1.0 - beta_one) * g
    new_v = beta_two * bv[...].reshape(1, size) + (1.0 - beta_two) * g * g
    m_hat = new_m / (1.0 - beta_one**STEP)
    v_hat = new_v / (1.0 - beta_two**STEP)
    m_o[...] = new_m.reshape(size)
    v_o[...] = new_v.reshape(size)
    fresh = bias - bias_rate * (m_hat / (jnp.sqrt(v_hat) + adam_eps) + weight_decay * bias)
    nb_o[...] = fresh.reshape(size)
    for copy in stores:
        copy.wait()


def updates(fin, g_all, scalars, w1, wr, wht, bias, st1, rt1, stm, rtm, sts, rts, sth, rth, bm, bv):
    hidden = w1.shape[1]
    classes = wht.shape[0]
    count = sts.shape[1]
    n1 = (st1.shape[0], hidden)
    nr = (2, stm.shape[1], hidden)
    nh = (classes, count)

    def of(shape, kind=f32):
        return jax.ShapeDtypeStruct(shape, kind)

    def room(a):
        return pltpu.VMEM(a.shape, a.dtype)

    one = of((1, 1))
    line = of(bias.shape)
    small = [one, one, one, of(nh), line, line, of(sth.shape), of(nh), line, of(nh, bf16)]
    large = [of(n1), of(nr), of(st1.shape), of(stm.shape), of(sts.shape), of(n1), of(nr), of(n1, bf16), of(nr, bf16)]
    loaded = [w1, wr, st1, rt1, stm, rtm, sts, rts]
    inside = pl.BlockSpec(memory_space=pltpu.VMEM)
    outside = pl.BlockSpec(memory_space=pl.ANY)
    (loss, total, norm, gh, m, v, lh, nh_new, nb, nh_low, g1, gr, l1, lm, ls, n1_new, nr_new, n1_low, nr_low) = pl.pallas_call(
        functools.partial(update_kernel, fin),
        out_shape=tuple(small + large),
        in_specs=[inside] * (8 + len(loaded)),
        out_specs=(inside,) * len(small) + (outside,) * len(large),
        scratch_shapes=[room(a) for a in large] + [
            pltpu.VMEM((2 * fin, hidden), f32),
            pltpu.VMEM(n1, f32),
            pltpu.VMEM(n1, f32),
            pltpu.VMEM((4, hidden, hidden), f32),
            pltpu.VMEM((1, 4 * hidden), f32),
            pltpu.SemaphoreType.DMA((len(large),)),
        ],
        compiler_params=pltpu.CompilerParams(vmem_limit_bytes=40 * 2**20),
        name="update_step",
    )(g_all, scalars, wht, bias, sth, rth, bm, bv, *loaded)
    return [
        loss, total, norm, g1, gr, gh, m, v, l1, lm, ls, lh, n1_new, nr_new, nh_new, nb, n1_low, nr_low, nh_low
    ]


def shards(
    features, nbr_index, nbr_mask, send_rows, send_count, labels, seed_mask,
    w_first, w_rest, w_head, biases,
    stat_big, root_big, stat_mid, root_mid, stat_sq, root_sq, stat_hr, root_hr, bias_m, bias_v,
):
    peers = send_rows.shape[2]
    cap = send_rows.shape[3]
    fin = features.shape[2]
    fan = nbr_index.shape[3]
    seeds = labels.shape[1]

    def lines(a):
        return jnp.transpose(a, (1, 3, 0, 2))

    g_all, scalars = summed_gradients(
        peers, cap, seeds, fan,
        lines(nbr_index), lines(nbr_mask), jnp.swapaxes(features[0], 0, 1), w_first, w_rest,
        send_rows[0, 0], send_count[0], labels, seed_mask, w_head.T, biases,
    )
    out = list(
        updates(
            fin, g_all, scalars, w_first, w_rest, w_head.T, biases,
            stat_big, root_big, stat_mid, root_mid, stat_sq, root_sq, stat_hr, root_hr,
            bias_m, bias_v,
        )
    )
    for i in (0, 1, 2):
        out[i] = out[i].reshape(())
    for i in (5, 14, 18):
        out[i] = out[i].T
    return tuple(out)


highest = lax.Precision.HIGHEST


def plain_activate(z):
    act = jax.nn.gelu(z, approximate=True)
    return act * lax.rsqrt(jnp.sum(act * act, axis=-1, keepdims=True) + norm_eps)


def plain_counts(nbr, mask, columns):
    nodes, slots = nbr.shape
    column_ids = jnp.arange(columns, dtype=jnp.int32)[None, :]
    mask_low = mask.astype(jnp.bfloat16)

    def add_slot(slot, total):
        picks = lax.dynamic_slice_in_dim(nbr, slot, 1, 1)
        weight = lax.dynamic_slice_in_dim(mask_low, slot, 1, 1)
        return total + (picks == column_ids).astype(jnp.bfloat16) * weight

    return lax.fori_loop(0, slots, add_slot, jnp.zeros((nodes, columns), jnp.bfloat16))


def plain_forward(h, weight, bias, nbr, mask, send_list, valid):
    nodes, width = h.shape
    hb = h.astype(jnp.bfloat16)
    outgoing = (
        jnp.take(hb, send_list, axis=0).reshape(valid.shape[0], valid.shape[1], width)
        * valid[:, :, None]
    )
    incoming = lax.all_to_all(outgoing, "dom", split_axis=0, concat_axis=0, tiled=True)
    table = jnp.concatenate([hb, incoming.reshape(-1, width)], axis=0)
    counts = plain_counts(nbr, mask, table.shape[0])
    degree = jnp.maximum(jnp.sum(mask, axis=1), 1).astype(jnp.float32)[:, None]
    gathered = jnp.dot(counts, table, preferred_element_type=jnp.float32)
    joined = jnp.concatenate([hb, (gathered / degree).astype(jnp.bfloat16)], axis=1)
    z = jnp.dot(joined, weight.astype(jnp.bfloat16), preferred_element_type=jnp.float32) + bias
    return (plain_activate(z), (joined, counts, degree, z))


def plain_backward(grad_out, weight, kept, send_list, valid, need_input):
    joined, counts, degree, z = kept
    nodes = joined.shape[0]
    width = joined.shape[1] // 2
    grad_z = jax.vjp(plain_activate, z)[1](grad_out)[0].astype(jnp.bfloat16)
    grad_w = jnp.einsum("nk,nh->kh", joined, grad_z, preferred_element_type=jnp.float32)
    grad_b = jnp.sum(grad_z.astype(jnp.float32), axis=0)
    if not need_input:
        return (grad_w, grad_b, None)
    grad_joined = jnp.einsum(
        "nh,kh->nk", grad_z, weight.astype(jnp.bfloat16), preferred_element_type=jnp.float32
    )
    grad_gathered = (grad_joined[:, width:] / degree).astype(jnp.bfloat16)
    grad_table = jnp.einsum("nj,nw->jw", counts, grad_gathered, preferred_element_type=jnp.float32)
    returned = (
        grad_table[nodes:].reshape(valid.shape[0], valid.shape[1], width).astype(jnp.bfloat16)
    )
    returned = lax.all_to_all(returned, "dom", split_axis=0, concat_axis=0, tiled=True)
    sent_back = (returned * valid[:, :, None]).reshape(-1, width)
    placement = (send_list[:, None] == jnp.arange(nodes, dtype=jnp.int32)[None, :]).astype(
        jnp.bfloat16
    )
    scattered = jnp.einsum("sn,sw->nw", placement, sent_back, preferred_element_type=jnp.float32)
    return (grad_w, grad_b, grad_joined[:, :width] + grad_table[:nodes] + scattered)


def plain_shampoo(grad, weight, left, left_root, right, right_root, part, right_split):
    count = left.shape[0]
    grad_rows = lax.dynamic_slice_in_dim(grad, part * count, count, 0)
    weight_rows = lax.dynamic_slice_in_dim(weight, part * count, count, 0)
    new_left = decay * left + (1.0 - decay) * jnp.dot(grad_rows, grad.T, precision=highest)
    if right_split:
        cols = right.shape[0]
        grad_cols = lax.dynamic_slice_in_dim(grad, part * cols, cols, 1)
        new_right = decay * right + (1.0 - decay) * jnp.dot(grad_cols.T, grad, precision=highest)
    else:
        new_right = decay * right + (1.0 - decay) * jnp.dot(grad.T, grad, precision=highest)
    step = jnp.dot(jnp.dot(left_root, grad, precision=highest), right_root, precision=highest)
    return (grad_rows, new_left, new_right, weight_rows - shampoo_rate * step)


def plain_shards(
    features,
    nbr_index,
    nbr_mask,
    send_rows,
    send_count,
    labels,
    seed_mask,
    w_first,
    w_rest,
    w_head,
    biases,
    stat_big,
    root_big,
    stat_mid,
    root_mid,
    stat_sq,
    root_sq,
    stat_hr,
    root_hr,
    bias_m,
    bias_v,
):
    hidden = w_rest.shape[2]
    peers = send_rows.shape[2]
    cap = send_rows.shape[3]
    send_list = send_rows.reshape(-1)
    valid = (jnp.arange(cap)[None, :] < send_count.reshape(peers, 1)).astype(jnp.bfloat16)
    weights = [w_first, w_rest[0], w_rest[1]]
    state = features[0].astype(jnp.float32)
    kept = []
    for level in range(3):
        state, saved = plain_forward(
            state,
            weights[level],
            biases[level * hidden : (level + 1) * hidden],
            nbr_index[0, level],
            nbr_mask[0, level],
            send_list,
            valid,
        )
        kept.append(saved)
    seeds = labels.shape[1]
    top = state[:seeds].astype(jnp.bfloat16)
    head_low_w = w_head.astype(jnp.bfloat16)
    logits = jnp.dot(top, head_low_w, preferred_element_type=jnp.float32) + biases[3 * hidden :]
    lse = jax.nn.logsumexp(logits, axis=1)
    onehot = (labels[0][:, None] == jnp.arange(logits.shape[1])[None, :]).astype(jnp.float32)
    picked = jnp.sum(logits * onehot, axis=1)
    seed_weight = seed_mask[0].astype(jnp.float32)
    loss_sum, seed_total = lax.psum(
        (jnp.sum((lse - picked) * seed_weight), jnp.sum(seed_weight)), ("dom", "rep")
    )
    grad_logits = (
        (jnp.exp(logits - lse[:, None]) - onehot) * (seed_weight / seed_total)[:, None]
    ).astype(jnp.bfloat16)
    grad_head = jnp.einsum("sh,sc->hc", top, grad_logits, preferred_element_type=jnp.float32)
    grad_hbias = jnp.sum(grad_logits.astype(jnp.float32), axis=0)
    grad_head, grad_hbias = (grad_head, grad_hbias)
    grad_top = jnp.einsum("sc,hc->sh", grad_logits, head_low_w, preferred_element_type=jnp.float32)
    grad_state = jnp.zeros(state.shape, jnp.float32).at[:seeds].set(grad_top)
    results = [None, None, None]
    for level in (2, 1, 0):
        grad_w, grad_b, grad_state = plain_backward(
            grad_state, weights[level], kept[level], send_list, valid, level > 0
        )
        results[level] = (grad_w, grad_b)
    grad_bias = jnp.concatenate([results[0][1], results[1][1], results[2][1], grad_hbias])
    grad_one, grad_two, grad_three = (results[0][0], results[1][0], results[2][0])
    grad_one, grad_two, grad_three, grad_head, grad_bias = lax.psum(
        (grad_one, grad_two, grad_three, grad_head, grad_bias), ("dom", "rep")
    )
    everything = (grad_one, grad_two, grad_three, grad_head, grad_bias)
    grad_norm = jnp.sqrt(sum((jnp.sum(g * g) for g in everything)))
    factor = clip_limit / jnp.maximum(grad_norm, clip_limit)
    grad_one, grad_two, grad_three, grad_head, grad_bias = [g * factor for g in everything]
    part = lax.axis_index("rep")
    head_rows = stat_sq.shape[1]
    head_root_rows = lax.dynamic_slice_in_dim(root_sq[3], part * head_rows, head_rows, 0)
    g_first, l_first, r_first, n_first = plain_shampoo(
        grad_one, w_first, stat_big, root_big, stat_sq[0], root_sq[0], part, True
    )
    g_mid0, l_mid0, r_mid0, n_mid0 = plain_shampoo(
        grad_two, w_rest[0], stat_mid[0], root_mid[0], stat_sq[1], root_sq[1], part, True
    )
    g_mid1, l_mid1, r_mid1, n_mid1 = plain_shampoo(
        grad_three, w_rest[1], stat_mid[1], root_mid[1], stat_sq[2], root_sq[2], part, True
    )
    g_head, l_head, r_head, n_head = plain_shampoo(
        grad_head, w_head, stat_sq[3], head_root_rows, stat_hr, root_hr, part, False
    )
    new_m = beta_one * bias_m + (1.0 - beta_one) * grad_bias
    new_v = beta_two * bias_v + (1.0 - beta_two) * grad_bias * grad_bias
    m_hat = new_m / (1.0 - beta_one**STEP)
    v_hat = new_v / (1.0 - beta_two**STEP)
    new_b = biases - bias_rate * (m_hat / (jnp.sqrt(v_hat) + adam_eps) + weight_decay * biases)
    new_rest = jnp.stack([n_mid0, n_mid1])
    return (
        loss_sum,
        seed_total,
        grad_norm,
        g_first,
        jnp.stack([g_mid0, g_mid1]),
        g_head,
        new_m,
        new_v,
        l_first,
        jnp.stack([l_mid0, l_mid1]),
        jnp.stack([r_first, r_mid0, r_mid1, l_head]),
        r_head,
        n_first,
        new_rest,
        n_head,
        new_b,
        n_first.astype(jnp.bfloat16),
        new_rest.astype(jnp.bfloat16),
        n_head.astype(jnp.bfloat16),
    )


def solution(mesh):
    placed = (
        P("rep", "dom", None),
        P("rep", None, "dom", None),
        P("rep", None, "dom", None),
        P("rep", "dom", None, None),
        P("rep", "dom", None),
        P("rep", "dom"),
        P("rep", "dom"),
        P(), P(), P(), P(),
        P("rep", None),
        P("rep", None),
        P(None, "rep", None),
        P(None, "rep", None),
        P(None, "rep", None),
        P(), P(), P(), P(), P(),
    )
    small = mesh.shape["rep"] == 4 and mesh.shape["dom"] == 8
    return jax.shard_map(
        shards if small else plain_shards,
        mesh=mesh,
        in_specs=placed,
        out_specs=(
            P(), P(), P(),
            P("rep", None), P(None, "rep", None), P("rep", None),
            P(), P(),
            P("rep", None), P(None, "rep", None), P(None, "rep", None), P(),
            P("rep", None), P(None, "rep", None), P("rep", None), P(),
            P("rep", None), P(None, "rep", None), P("rep", None),
        ),
        check_vma=False,
    )
```

time: 94.5 us -> 83.3 us (0.88)
  Pallas kernels: 90 us -> 82.1 us
  other arithmetic: 1.88 us -> 0 us
  local copies, waits for them, and re-layouts: 1.3 us -> 0.06 us
    pallas_call x1, Pallas kernels: 84.8 us -> 76.5 us  [summed_gradients(): pl.pallas_call(functools.partial(graph_kernel, peers, cap, seeds, fan), o...]
    transpose x1 -> x0, other arithmetic: 1.88 us -> none  [shards(): jnp.swapaxes(codes, 1, 2)]
    unnamed x36 -> x28, local copies, waits for them, and re-layouts: 1.3 us -> 0.06 us
where the time goes in v3:
time: 83.3 us; the launch traced here: 83.2 us
  Pallas kernels  82.1 us (99%)
  between operations  1.07 us (1%)
    pallas_call x1, Pallas kernels, summed_gradients(): pl.pallas_call(functools.partial(graph_kernel, peers, cap, seeds, fan), o...  76.5 us
    pallas_call x1, Pallas kernels, updates(): pl.pallas_call(functools.partial(update_kernel, fin), out_shape=tuple(sma...  5.52 us

profile of v3, /device:TPU:1, one launch (start us, length us, event | category | flops | bytes accessed | tf_op | source)
XLA Modules:
  0.0 83.2 jit_solution(16232486637228363299)
XLA Ops:
  0.7 0.0 copy-start
  0.7 0.0 copy-start.1
  0.7 0.0 copy-start.2
  0.7 0.0 copy-start.3
  0.7 0.0 copy-start.4
  0.7 0.0 copy-start.5
  0.7 0.0 copy-start.6
  0.7 0.0 copy-start.7
  0.7 0.0 copy-start.8
  0.8 0.0 copy-start.9
  0.8 0.0 copy-start.10
  0.8 0.0 copy-start.11
  0.8 0.0 copy-start.12
  0.8 0.0 copy-start.13
  0.8 76.5 %graph_step.1 = (bf16[2,2304,128]{2,1,0:T(8,128)(2,1)S(1)}, f32[8,128]{1,0:T(8,128)S(1)}) custom-call(s32[3,25,1,2048]{3,2,1,0:T(1,128)} %bitcast.17, s32[3,25,1,2048]{3,2,1,0:T(1,128)} %bitcast.18, bf16[602,2048]{1,0:T(8,128)(2,1)} %bitcast.16, f32[1204,256]{1,0:T(8,128)} %w1.1, f32[2,512,256]{2,1,0:T(8,128)} %wr.1, s32[8,32]{1,0:T(8,128)} %bitcast.22, ...), custom_call_target="tpu_custom_call" | custom-call | flops 24000000000 | bytes 12582912 | tf_op jit(solution)/shard_map/graph_step/pallas_call | solution.py:692
  77.4 0.0 copy-done
  77.4 0.0 copy-done.1
  77.4 0.0 copy-done.2
  77.4 0.0 copy-done.3
  77.4 0.0 copy-done.4
  77.4 0.0 copy-done.5
  77.4 0.0 copy-done.6
  77.4 0.0 copy-done.7
  77.4 0.0 copy-done.8
  77.4 0.0 copy-done.9
  77.5 0.0 copy-done.10
  77.5 0.0 copy-done.11
  77.5 0.0 copy-done.12
  77.5 0.0 copy-done.13
  77.5 5.5 %update_step.1 = (f32[1,1]{1,0:T(1,128)}, f32[1,1]{1,0:T(1,128)}, f32[1,1]{1,0:T(1,128)}, f32[41,64]{1,0:T(8,128)}, f32[809]{0:T(1024)}, /*index=5*/f32[809]{0:T...) custom-call(bf16[2,2304,128]{2,1,0:T(8,128)(2,1)S(1)} %get-tuple-ele, ...), custom_call_target="tpu_custom_call" | custom-call | tf_op jit(solution)/shard_map/update_step/pallas_call | solution.py:876
Async XLA Ops:
  0.7 76.7 %copy-start = (f32[301,1204]{1,0:T(8,128)S(1)}, f32[301,1204]{1,0:T(8,128)}, u32[]{:S(2)}) copy-start(f32[301,1204]{1,0:T(8,128)} %st1.1) | copy-start | bytes 4348852
  0.7 76.7 %copy-start.1 = (f32[301,1204]{1,0:T(8,128)S(1)}, f32[301,1204]{1,0:T(8,128)}, u32[]{:S(2)}) copy-start(f32[301,1204]{1,0:T(8,128)} %rt1.1) | copy-start | bytes 4348852
  0.7 76.7 %copy-start.2 = (f32[1204,256]{1,0:T(8,128)S(1)}, f32[1204,256]{1,0:T(8,128)}, u32[]{:S(2)}) copy-start(f32[1204,256]{1,0:T(8,128)} %w1.1) | copy-start | bytes 3698692
  0.7 76.7 %copy-start.3 = (f32[2,512,256]{2,1,0:T(8,128)S(1)}, f32[2,512,256]{2,1,0:T(8,128)}, u32[]{:S(2)}) copy-start(f32[2,512,256]{2,1,0:T(8,128)} %wr.1) | copy-start | bytes 3145732
  0.7 76.7 %copy-start.4 = (f32[4,256,256]{2,1,0:T(8,128)S(1)}, f32[4,256,256]{2,1,0:T(8,128)}, u32[]{:S(2)}) copy-start(f32[4,256,256]{2,1,0:T(8,128)} %rts.1) | copy-start | bytes 3145732
  0.7 76.7 %copy-start.5 = (f32[2,128,512]{2,1,0:T(8,128)S(1)}, f32[2,128,512]{2,1,0:T(8,128)}, u32[]{:S(2)}) copy-start(f32[2,128,512]{2,1,0:T(8,128)} %stm.1) | copy-start | bytes 1572868
  0.7 76.7 %copy-start.6 = (f32[2,128,512]{2,1,0:T(8,128)S(1)}, f32[2,128,512]{2,1,0:T(8,128)}, u32[]{:S(2)}) copy-start(f32[2,128,512]{2,1,0:T(8,128)} %rtm.1) | copy-start | bytes 1572868
  0.7 76.7 %copy-start.7 = (f32[4,64,256]{2,1,0:T(8,128)S(1)}, f32[4,64,256]{2,1,0:T(8,128)}, u32[]{:S(2)}) copy-start(f32[4,64,256]{2,1,0:T(8,128)} %sts.1) | copy-start | bytes 786436
  0.7 76.7 %copy-start.8 = (f32[256,41]{0,1:T(8,128)S(1)}, f32[256,41]{0,1:T(8,128)}, u32[]{:S(2)}) copy-start(f32[256,41]{0,1:T(8,128)} %param.30) | copy-start | bytes 125956
  0.8 76.7 %copy-start.9 = (f32[41,41]{1,0:T(8,128)S(1)}, f32[41,41]{1,0:T(8,128)}, u32[]{:S(2)}) copy-start(f32[41,41]{1,0:T(8,128)} %sth.1) | copy-start | bytes 20176
  0.8 76.7 %copy-start.10 = (f32[41,41]{1,0:T(8,128)S(1)}, f32[41,41]{1,0:T(8,128)}, u32[]{:S(2)}) copy-start(f32[41,41]{1,0:T(8,128)} %rth.1) | copy-start | bytes 20176
  0.8 76.7 %copy-start.11 = (f32[809]{0:T(1024)S(1)}, f32[809]{0:T(1024)}, u32[]{:S(2)}) copy-start(f32[809]{0:T(1024)} %bias.1) | copy-start | bytes 9712
  0.8 76.7 %copy-start.12 = (f32[809]{0:T(1024)S(1)}, f32[809]{0:T(1024)}, u32[]{:S(2)}) copy-start(f32[809]{0:T(1024)} %bm.1) | copy-start | bytes 9712
  0.8 76.7 %copy-start.13 = (f32[809]{0:T(1024)S(1)}, f32[809]{0:T(1024)}, u32[]{:S(2)}) copy-start(f32[809]{0:T(1024)} %bv.1) | copy-start | bytes 9712

commit v4 on v3

--- a/solution.py
+++ b/solution.py
@@ -333,7 +333,6 @@
         blk = block(b)
         z = grad1[:, blk]
         act = gelu(z)
-        slope1[:, blk] = gelu_slope(z)
         root = norm_root(act, 0)
         act1[:, blk] = act
         root1[0:1, blk] = root
@@ -361,6 +360,13 @@
     sent = exchange(1, ob1, ib1)
 
     own2 = nt(chosen[slots:, :], h1t[...])
+
+    def slopes(b, _):
+        blk = block(b)
+        slope1[:, blk] = gelu_slope(grad1[:, blk])
+        return 0
+
+    lax.fori_loop(0, blocks, slopes, 0)
     finish(sent_far)
     far3r = ib5[...].astype(f32)[:, 0:cap]
     spots = peers * cap
@@ -531,14 +537,14 @@
         for to, _ in group1:
             part = gout.at[core, rows_of(start + to * quarter, quarter)]
             copies.append(hop(part, part, to_core))
+        out = [
+            pltpu.make_async_copy(gout.at[h, whole], g_out.at[h, whole], load_sem.at[out_sem + k])
+            for k, h in enumerate((core, 1 - core))
+        ]
+        out[0].start()
         yield
         finish(copies)
-        out = [
-            pltpu.make_async_copy(gout.at[h, whole], g_out.at[h, whole], load_sem.at[out_sem + h])
-            for h in range(2)
-        ]
-        for c in out:
-            c.start()
+        out[1].start()
         yield
         for c in out:
             c.wait()
@@ -596,14 +602,14 @@
         h1t[:, blk] = pull_back(act1[:, blk], slope1[:, blk], root1[0:1, blk], grad, 0)
         return 0
 
-    lax.fori_loop(0, blocks, layer_one_back, 0)
+    lax.fori_loop(0, blocks, layer_one_back, 0, unroll=2)
     size = cut - seg_a
     put(seg_a, nt(joined[0:size, :], h1t[...]))
     go_on(first, rest, scalars)
     put(cut, nt(joined[size:, :], h1t[...]))
     go_on(second, first)
     for _ in range(5):
-        go_on(second, first, rest, scalars)
+        go_on(second, rest, first, scalars)
     go_on(second, first)
     go_on(second)
     for c in started:

time: 83.3 us -> 80.7 us (0.969)
  Pallas kernels: 82.1 us -> 79.5 us
    pallas_call x1, Pallas kernels: 76.5 us -> 73.9 us  [summed_gradients(): pl.pallas_call(functools.partial(graph_kernel, peers, cap, seeds, fan), o...]
where the time goes in v4:
time: 80.7 us; the launch traced here: 80.6 us
  Pallas kernels  79.5 us (99%)
  between operations  1.07 us (1%)
    pallas_call x1, Pallas kernels, summed_gradients(): pl.pallas_call(functools.partial(graph_kernel, peers, cap, seeds, fan), o...  73.9 us
    pallas_call x1, Pallas kernels, updates(): pl.pallas_call(functools.partial(update_kernel, fin), out_shape=tuple(sma...  5.52 us

profile of v4, /device:TPU:1, one launch (start us, length us, event | category | flops | bytes accessed | tf_op | source)
XLA Modules:
  0.0 80.6 jit_solution(9155554369503708947)
XLA Ops:
  0.7 0.0 copy-start
  0.7 0.0 copy-start.1
  0.7 0.0 copy-start.2
  0.7 0.0 copy-start.3
  0.7 0.0 copy-start.4
  0.7 0.0 copy-start.5
  0.7 0.0 copy-start.6
  0.7 0.0 copy-start.7
  0.7 0.0 copy-start.8
  0.8 0.0 copy-start.9
  0.8 0.0 copy-start.10
  0.8 0.0 copy-start.11
  0.8 0.0 copy-start.12
  0.8 0.0 copy-start.13
  0.8 73.9 %graph_step.1 = (bf16[2,2304,128]{2,1,0:T(8,128)(2,1)S(1)}, f32[8,128]{1,0:T(8,128)S(1)}) custom-call(s32[3,25,1,2048]{3,2,1,0:T(1,128)} %bitcast.17, s32[3,25,1,2048]{3,2,1,0:T(1,128)} %bitcast.18, bf16[602,2048]{1,0:T(8,128)(2,1)} %bitcast.16, f32[1204,256]{1,0:T(8,128)} %w1.1, f32[2,512,256]{2,1,0:T(8,128)} %wr.1, s32[8,32]{1,0:T(8,128)} %bitcast.22, ...), custom_call_target="tpu_custom_call" | custom-call | flops 24000000000 | bytes 12582912 | tf_op jit(solution)/shard_map/graph_step/pallas_call | solution.py:698
  74.7 0.0 copy-done
  74.8 0.0 copy-done.1
  74.8 0.0 copy-done.2
  74.8 0.0 copy-done.3
  74.8 0.0 copy-done.4
  74.8 0.0 copy-done.5
  74.8 0.0 copy-done.6
  74.8 0.0 copy-done.7
  74.8 0.0 copy-done.8
  74.8 0.0 copy-done.9
  74.8 0.0 copy-done.10
  74.9 0.0 copy-done.11
  74.9 0.0 copy-done.12
  74.9 0.0 copy-done.13
  74.9 5.5 %update_step.1 = (f32[1,1]{1,0:T(1,128)}, f32[1,1]{1,0:T(1,128)}, f32[1,1]{1,0:T(1,128)}, f32[41,64]{1,0:T(8,128)}, f32[809]{0:T(1024)}, /*index=5*/f32[809]{0:T...) custom-call(bf16[2,2304,128]{2,1,0:T(8,128)(2,1)S(1)} %get-tuple-ele, ...), custom_call_target="tpu_custom_call" | custom-call | tf_op jit(solution)/shard_map/update_step/pallas_call | solution.py:882
Async XLA Ops:
  0.7 74.1 %copy-start = (f32[301,1204]{1,0:T(8,128)S(1)}, f32[301,1204]{1,0:T(8,128)}, u32[]{:S(2)}) copy-start(f32[301,1204]{1,0:T(8,128)} %st1.1) | copy-start | bytes 4348852
  0.7 74.1 %copy-start.1 = (f32[301,1204]{1,0:T(8,128)S(1)}, f32[301,1204]{1,0:T(8,128)}, u32[]{:S(2)}) copy-start(f32[301,1204]{1,0:T(8,128)} %rt1.1) | copy-start | bytes 4348852
  0.7 74.1 %copy-start.2 = (f32[1204,256]{1,0:T(8,128)S(1)}, f32[1204,256]{1,0:T(8,128)}, u32[]{:S(2)}) copy-start(f32[1204,256]{1,0:T(8,128)} %w1.1) | copy-start | bytes 3698692
  0.7 74.1 %copy-start.3 = (f32[2,512,256]{2,1,0:T(8,128)S(1)}, f32[2,512,256]{2,1,0:T(8,128)}, u32[]{:S(2)}) copy-start(f32[2,512,256]{2,1,0:T(8,128)} %wr.1) | copy-start | bytes 3145732
  0.7 74.1 %copy-start.4 = (f32[4,256,256]{2,1,0:T(8,128)S(1)}, f32[4,256,256]{2,1,0:T(8,128)}, u32[]{:S(2)}) copy-start(f32[4,256,256]{2,1,0:T(8,128)} %rts.1) | copy-start | bytes 3145732
  0.7 74.1 %copy-start.5 = (f32[2,128,512]{2,1,0:T(8,128)S(1)}, f32[2,128,512]{2,1,0:T(8,128)}, u32[]{:S(2)}) copy-start(f32[2,128,512]{2,1,0:T(8,128)} %stm.1) | copy-start | bytes 1572868
  0.7 74.1 %copy-start.6 = (f32[2,128,512]{2,1,0:T(8,128)S(1)}, f32[2,128,512]{2,1,0:T(8,128)}, u32[]{:S(2)}) copy-start(f32[2,128,512]{2,1,0:T(8,128)} %rtm.1) | copy-start | bytes 1572868
  0.7 74.1 %copy-start.7 = (f32[4,64,256]{2,1,0:T(8,128)S(1)}, f32[4,64,256]{2,1,0:T(8,128)}, u32[]{:S(2)}) copy-start(f32[4,64,256]{2,1,0:T(8,128)} %sts.1) | copy-start | bytes 786436
  0.7 74.1 %copy-start.8 = (f32[256,41]{0,1:T(8,128)S(1)}, f32[256,41]{0,1:T(8,128)}, u32[]{:S(2)}) copy-start(f32[256,41]{0,1:T(8,128)} %param.30) | copy-start | bytes 125956
  0.8 74.1 %copy-start.9 = (f32[41,41]{1,0:T(8,128)S(1)}, f32[41,41]{1,0:T(8,128)}, u32[]{:S(2)}) copy-start(f32[41,41]{1,0:T(8,128)} %sth.1) | copy-start | bytes 20176
  0.8 74.1 %copy-start.10 = (f32[41,41]{1,0:T(8,128)S(1)}, f32[41,41]{1,0:T(8,128)}, u32[]{:S(2)}) copy-start(f32[41,41]{1,0:T(8,128)} %rth.1) | copy-start | bytes 20176
  0.8 74.1 %copy-start.11 = (f32[809]{0:T(1024)S(1)}, f32[809]{0:T(1024)}, u32[]{:S(2)}) copy-start(f32[809]{0:T(1024)} %bias.1) | copy-start | bytes 9712
  0.8 74.1 %copy-start.12 = (f32[809]{0:T(1024)S(1)}, f32[809]{0:T(1024)}, u32[]{:S(2)}) copy-start(f32[809]{0:T(1024)} %bm.1) | copy-start | bytes 9712
  0.8 74.1 %copy-start.13 = (f32[809]{0:T(1024)S(1)}, f32[809]{0:T(1024)}, u32[]{:S(2)}) copy-start(f32[809]{0:T(1024)} %bv.1) | copy-start | bytes 9712

commit v5 on v4

--- a/solution.py
+++ b/solution.py
@@ -72,10 +72,24 @@
     return jnp.concatenate([row, jnp.full((1, width - row.shape[1]), value, row.dtype)], axis=1)
 
 
+def split_dot(a, b):
+    high = a.astype(bf16)
+    low = (a - high.astype(f32)).astype(bf16)
+    return nn(high, b) + nn(low, b)
+
+
+def three_dot(a, b):
+    high = b.astype(bf16)
+    low = (b - high.astype(f32)).astype(bf16)
+    return split_dot(a, high) + nn(a.astype(bf16), low)
+
+
 def graph_kernel(
     peers, cap, seeds, fan,
     nbr_hbm, msk_hbm, xt_hbm, w1_hbm, wr_hbm, srow_hbm, scnt_hbm, lab_hbm, smask_hbm, wht_hbm, bias_hbm,
-    g_out, s_out,
+    rtm_hbm, rts_hbm,
+    g_out, s_out, left_out, right_out, move_out, square_out, w1_out, wr_out,
+    rtm, rts, full,
     nbr, msk, xt, srow, scnt, lab, smask, wht, bias, joined, near, chosen, far2, far2t, grad1, ctmp, crow, lrow, lcode, crow2, lrow2, rdeg,
     w1, wr, w1t, act1, slope1, root1, h1t, ob0, ib0, ob1, ib1, ob2, ib2, ob3, ib3, ob4, ib4, ob5, ib5,
     gl, acc, rc, sbq, rbq, sbz, rbz, gout, ssend, srecv, sqv, szv,
@@ -108,6 +122,7 @@
             (
                 (srow_hbm, srow), (scnt_hbm, scnt), (xt_hbm, xt), (nbr_hbm, nbr), (msk_hbm, msk),
                 (w1_hbm, w1), (wr_hbm, wr), (lab_hbm, lab), (smask_hbm, smask), (wht_hbm, wht), (bias_hbm, bias),
+                (rtm_hbm, rtm), (rts_hbm, rts),
             )
         )
     ]
@@ -367,6 +382,20 @@
         return 0
 
     lax.fori_loop(0, blocks, slopes, 0)
+    first_rows = w1_out.shape[0]
+    for i in range(2 * fin // first_rows):
+
+        @pl.when(rep == i)
+        def _():
+            w1_out[...] = w1[i * first_rows : (i + 1) * first_rows, :]
+
+    rest_rows = wr_out.shape[1]
+    for i in range(2):
+        wr_out[i] = wr[i, pl.ds(pl.multiple_of(rep * rest_rows, 8), rest_rows), :]
+    b2 = bias[0:1, hidden : 2 * hidden]
+    self_local = own2[0:local].astype(bf16)
+    z_sent = nn(sent_rows, w2[0:hidden]) + b2
+    z_local = nn(self_local, w2[0:hidden]) + b2
     finish(sent_far)
     far3r = ib5[...].astype(f32)[:, 0:cap]
     spots = peers * cap
@@ -378,21 +407,22 @@
 
     finish(sent)
 
-    def rows_two(own_self, own_sum, at):
-        agg = (own_sum + nn(far2[at, :], ib1[...])) * rdeg2[at]
-        both = jnp.concatenate([own_self, agg.astype(bf16)], axis=1)
-        z = nn(both, w2) + bias[0:1, hidden : 2 * hidden]
+    def rows_two(own_self, own_z, own_sum, at):
+        agg = ((own_sum + nn(far2[at, :], ib1[...])) * rdeg2[at]).astype(bf16)
+        z = own_z + nn(agg, w2[hidden:])
         act = gelu(z)
         root = norm_root(act, 1)
-        return both, z, act, root, (act * (root * keep[at])).astype(bf16)
+        return jnp.concatenate([own_self, agg], axis=1), z, act, root, (act * (root * keep[at])).astype(bf16)
 
     out_at, in_at = slice(0, slots), slice(slots, span)
-    joined2a, z2a, act2a, root2a, h2a = rows_two(sent_rows, own2[local:span], out_at)
+    joined2a, z2a, act2a, root2a, h2a = rows_two(sent_rows, z_sent, own2[local:span], out_at)
     ob2[...] = nn(collect, h2a).astype(bf16)
     sent = exchange(2, ob2, ib2)
 
-    joined2b, z2b, act2b, root2b, h2b = rows_two(own2[0:local].astype(bf16), own2[span:], in_at)
+    joined2b, z2b, act2b, root2b, h2b = rows_two(self_local, z_local, own2[span:], in_at)
     near3 = nn(spread, h2b)
+    self3 = near3[0:seeds].astype(bf16)
+    z_seeds = nn(self3, w3[0:hidden]) + bias[0:1, 2 * hidden : 3 * hidden]
     slope2b = gelu_slope(z2b)
     classes = wht.shape[0]
     classp = round_up(classes, 16)
@@ -406,8 +436,9 @@
     total = near3[seeds:]
     for q in range(peers):
         total = total + ib2[q * seeds : (q + 1) * seeds, :].astype(f32)
-    joined3 = jnp.concatenate([near3[0:seeds].astype(bf16), (total * rdeg3).astype(bf16)], axis=1)
-    z3 = nn(joined3, w3) + bias[0:1, 2 * hidden : 3 * hidden]
+    agg3 = (total * rdeg3).astype(bf16)
+    z3 = z_seeds + nn(agg3, w3[hidden:])
+    joined3 = jnp.concatenate([self3, agg3], axis=1)
     act3 = gelu(z3)
     slope3 = gelu_slope(z3)
     root3 = norm_root(act3, 1)
@@ -421,11 +452,11 @@
     dtop = nn(dlog, wht_low)
 
     dz3 = pull_back(act3, slope3, root3, dtop, 1)
-    dj3 = nt(dz3, w3)
-    dg3 = (dj3[:, hidden:] * rdeg3).astype(bf16)
+    dg3 = (nt(dz3, w3[hidden:]) * rdeg3).astype(bf16)
     ob3[...] = dg3
     sent = exchange(3, ob3, ib3, same=True)
-    dloc = nn(spread_t, jnp.concatenate([dj3[:, 0:hidden].astype(bf16), dg3], axis=0))
+    ds3 = nt(dz3, w3[0:hidden]).astype(bf16)
+    dloc = nn(spread_t, jnp.concatenate([ds3, dg3], axis=0))
 
     seg_a = 4 * hidden
     row_head = seg_a + 2 * finp
@@ -455,8 +486,7 @@
 
     dh2a = nn(scatter, ib3[...]) * keep[out_at]
     dz2a = pull_back(act2a, slope2a, root2a, dh2a, 1)
-    dj2a = nt(dz2a, w2)
-    dg2a = (dj2a[:, hidden:] * rdeg2[out_at]).astype(bf16)
+    dg2a = (nt(dz2a, w2[hidden:]) * rdeg2[out_at]).astype(bf16)
     ob4[...] = (near_ret + nn(far2t[:, out_at], dg2a)).astype(bf16)
     sent = exchange(4, ob4, ib4)
     put(0, nn(flip(joined2a), dz2a) + nn(flip(joined2b), dz2b))
@@ -588,7 +618,7 @@
     )
     both = flip(
         jnp.concatenate(
-            [dj2a[:, 0:hidden].astype(bf16), dj2b[:, 0:hidden].astype(bf16), dg2a, dg2b], axis=0
+            [nt(dz2a, w2[0:hidden]).astype(bf16), dj2b[:, 0:hidden].astype(bf16), dg2a, dg2b], axis=0
         )
     )
     grad1[...] = nn(both, chosen[...])
@@ -608,8 +638,27 @@
     go_on(first, rest, scalars)
     put(cut, nt(joined[size:, :], h1t[...]))
     go_on(second, first)
-    for _ in range(5):
+    def rest_products():
+        count = rtm.shape[1]
+        cols = right_out.shape[1]
+        square = jnp.zeros((1, hidden), f32)
+        for i in range(2):
+            whole = slice(i * 2 * hidden, (i + 1) * 2 * hidden)
+            g = jnp.concatenate([gout[0, whole, :], gout[1, whole, :]], axis=1)
+            mine = rows_of(i * 2 * hidden + rep * count, count)
+            g_rows = jnp.concatenate([gout[0, mine, :], gout[1, mine, :]], axis=1)
+            left_out[i] = nt(g_rows, g)
+            full[i] = nn(flip(g), g)
+            right_out[i] = full[i, pl.ds(pl.multiple_of(rep * cols, 8), cols), :]
+            move_out[i] = three_dot(split_dot(rtm[i], g), rts[1 + i])
+            wide = g.astype(f32)
+            square = square + jnp.sum(wide * wide, axis=0, keepdims=True)
+        square_out[...] = square
+
+    for turn in range(5):
         go_on(second, rest, first, scalars)
+        if turn == 3:
+            rest_products()
     go_on(second, first)
     go_on(second)
     for c in started:
@@ -620,7 +669,7 @@
     return [pltpu.with_memory_space_constraint(a, pltpu.HBM) for a in arrays]
 
 
-def summed_gradients(peers, cap, seeds, fan, nbr, msk, xt, w1, wr, srow, scnt, lab, smask, wht, bias):
+def summed_gradients(peers, cap, seeds, fan, nbr, msk, xt, w1, wr, srow, scnt, lab, smask, wht, bias, rtm, rts):
     fin, nodes = xt.shape
     hidden = w1.shape[1]
     finp = round_up(fin, 16)
@@ -633,7 +682,11 @@
     vmem = pltpu.VMEM
     sems = 64
     some = peers * seeds
+    count, cols = rtm.shape[1], hidden // (2 * hidden // rtm.shape[1])
     scratch = [
+        vmem(rtm.shape, f32),
+        vmem(rts.shape, f32),
+        vmem((2, hidden, hidden), f32),
         vmem(nbr.shape, i32),
         vmem(msk.shape, i32),
         vmem(xt.shape, bf16),
@@ -687,7 +740,7 @@
         vmem((3, 8, 128), f32),
         vmem((4, 8, 128), f32),
         vmem((nz, 8, 128), f32),
-        pltpu.SemaphoreType.DMA((11,)),
+        pltpu.SemaphoreType.DMA((13,)),
         pltpu.SemaphoreType.DMA((6, peers - 1)),
         pltpu.SemaphoreType.DMA((6, peers - 1)),
         pltpu.SemaphoreType.DMA((sems,)),
@@ -700,40 +753,34 @@
         out_shape=(
             jax.ShapeDtypeStruct((2, rows, 128), bf16),
             jax.ShapeDtypeStruct((8, 128), f32),
+            jax.ShapeDtypeStruct((2, count, 2 * hidden), f32),
+            jax.ShapeDtypeStruct((2, cols, hidden), f32),
+            jax.ShapeDtypeStruct((2, count, hidden), f32),
+            jax.ShapeDtypeStruct((1, hidden), f32),
+            jax.ShapeDtypeStruct((count * 2 * fin // (2 * hidden), hidden), f32),
+            jax.ShapeDtypeStruct((2, count, hidden), f32),
         ),
-        in_specs=[outside] * 11,
-        out_specs=(outside, inside),
+        in_specs=[outside] * 13,
+        out_specs=(outside,) + (inside,) * 7,
         scratch_shapes=scratch,
         compiler_params=pltpu.CompilerParams(
-            collective_id=0, has_side_effects=True, vmem_limit_bytes=47 * 2**20
+            collective_id=0, has_side_effects=True, vmem_limit_bytes=51 * 2**20
         ),
         cost_estimate=pl.CostEstimate(flops=24 * 10**9, bytes_accessed=12 * 2**20, transcendentals=2**20),
         name="graph_step",
-    )(*in_hbm(nbr, msk, xt, w1, wr, srow, scnt, lab, smask, wht, bias))
-
-
-def split_dot(a, b):
-    high = a.astype(bf16)
-    low = (a - high.astype(f32)).astype(bf16)
-    return nn(high, b) + nn(low, b)
-
-
-def three_dot(a, b):
-    high = b.astype(bf16)
-    low = (b - high.astype(f32)).astype(bf16)
-    return split_dot(a, high) + nn(a.astype(bf16), low)
+    )(*in_hbm(nbr, msk, xt, w1, wr, srow, scnt, lab, smask, wht, bias, rtm, rts))
 
 
 def update_kernel(
     fin,
-    g_all, scalars, wht, bias, sth, rth, bm, bv,
-    w1, wr, st1, rt1, stm, rtm, sts, rts,
+    g_all, scalars, lefts, rights, moves, rest_square, w_mine, wr_mine, wht, bias, sth, rth, bm, bv,
+    st1, rt1, stm, sts, rts,
     loss_o, total_o, norm_o, gh_o, m_o, v_o, lh_o, nh_o, nb_o, nh_low,
     g1_hbm, gr_hbm, l1_hbm, lm_hbm, ls_hbm, n1_hbm, nr_hbm, n1_low_hbm, nr_low_hbm,
     g1_o, gr_o, l1_o, lm_o, ls_o, n1_o, nr_o, n1_low, nr_low,
-    g1, g_mine, w_mine, full, gb, out_sem,
+    g1, g_mine, full, gb, out_sem,
 ):
-    hidden = w1.shape[1]
+    hidden = w_mine.shape[1]
     classes = wht.shape[0]
     classp = round_up(classes, 16)
     finp = round_up(fin, 16)
@@ -755,12 +802,12 @@
     total = scalars[0:1, 1:2]
     square = jnp.zeros((16, hidden), f32)
     spare = lax.broadcasted_iota(i32, (16, hidden), 0) >= 16 - (finp - fin)
-    for r in range(0, g_all.shape[1], 16):
+    for r in range(seg_a, g_all.shape[1], 16):
         g = grads(r, 16).astype(f32)
         if r == seg_a + 2 * finp - 16:
             g = jnp.where(spare, 0.0, g)
         square = square + g * g
-    square = jnp.sum(jnp.sum(square, axis=0, keepdims=True), axis=1, keepdims=True)
+    square = jnp.sum(jnp.sum(square, axis=0, keepdims=True) + rest_square[...], axis=1, keepdims=True)
     norm = jnp.sqrt(square) / total
     scale = clip_limit / jnp.maximum(norm, clip_limit) / total
     loss_o[...] = scalars[0:1, 0:1]
@@ -780,7 +827,6 @@
         @pl.when(part == i)
         def _():
             g_mine[...] = g1[i * count : (i + 1) * count, :]
-            w_mine[...] = w1[i * count : (i + 1) * count, :]
 
     g_rows = g_mine[...]
     g1_o[...] = g_rows * scale
@@ -795,31 +841,25 @@
     store(l1_o, l1_hbm)
 
     count = stm.shape[1]
-    at = pl.ds(pl.multiple_of(part * count, count), count)
-    products = []
     for i in range(2):
-        g = grads(i * 2 * hidden, 2 * hidden)
         base = pl.ds(pl.multiple_of(i * 2 * hidden + part * count, 16), count)
         g_rows = jnp.concatenate([g_all[0, base, :], g_all[1, base, :]], axis=1)
         gr_o[i] = g_rows.astype(f32) * scale
-        full[1 + i] = nn(flip(g), g)
-        products.append((nt(g_rows, g), three_dot(split_dot(rtm[i], g), rts[1 + i])))
-    store(gr_o, gr_hbm)
-    for i, (product, step) in enumerate(products):
-        lm_o[i] = decay * stm[i] + lift * product
-        fresh = wr[i, at, :] - move * step
+        lm_o[i] = decay * stm[i] + lift * lefts[i]
+        fresh = wr_mine[i] - move * moves[i]
         nr_o[i] = fresh
         nr_low[i] = fresh.astype(bf16)
+    store(gr_o, gr_hbm)
     store(lm_o, lm_hbm)
     store(nr_o, nr_hbm)
     store(nr_low, nr_low_hbm)
 
     gt = grads(seg_a + 2 * finp, classp)
-    full[3] = nn(flip(gt), gt)
+    full[1] = nn(flip(gt), gt)
     count = sts.shape[1]
     mine = pl.ds(pl.multiple_of(part * count, count), count)
-    for i in range(4):
-        ls_o[i] = decay * sts[i] + lift * full[i, mine, :]
+    for i, product in enumerate((full[0, mine, :], rights[0], rights[1], full[1, mine, :])):
+        ls_o[i] = decay * sts[i] + lift * product
     store(ls_o, ls_hbm)
     lh_o[...] = decay * sth[...] + lift * nt(gt, gt)[0:classes, 0:classes]
     root = rts[3, mine, :]
@@ -858,8 +898,8 @@
         copy.wait()
 
 
-def updates(fin, g_all, scalars, w1, wr, wht, bias, st1, rt1, stm, rtm, sts, rts, sth, rth, bm, bv):
-    hidden = w1.shape[1]
+def updates(fin, summed, wht, bias, st1, rt1, stm, sts, rts, sth, rth, bm, bv):
+    hidden = wht.shape[1]
     classes = wht.shape[0]
     count = sts.shape[1]
     n1 = (st1.shape[0], hidden)
@@ -876,25 +916,24 @@
     line = of(bias.shape)
     small = [one, one, one, of(nh), line, line, of(sth.shape), of(nh), line, of(nh, bf16)]
     large = [of(n1), of(nr), of(st1.shape), of(stm.shape), of(sts.shape), of(n1), of(nr), of(n1, bf16), of(nr, bf16)]
-    loaded = [w1, wr, st1, rt1, stm, rtm, sts, rts]
+    loaded = [st1, rt1, stm, sts, rts]
     inside = pl.BlockSpec(memory_space=pltpu.VMEM)
     outside = pl.BlockSpec(memory_space=pl.ANY)
     (loss, total, norm, gh, m, v, lh, nh_new, nb, nh_low, g1, gr, l1, lm, ls, n1_new, nr_new, n1_low, nr_low) = pl.pallas_call(
         functools.partial(update_kernel, fin),
         out_shape=tuple(small + large),
-        in_specs=[inside] * (8 + len(loaded)),
+        in_specs=[inside] * (6 + len(summed) + len(loaded)),
         out_specs=(inside,) * len(small) + (outside,) * len(large),
         scratch_shapes=[room(a) for a in large] + [
             pltpu.VMEM((2 * fin, hidden), f32),
             pltpu.VMEM(n1, f32),
-            pltpu.VMEM(n1, f32),
-            pltpu.VMEM((4, hidden, hidden), f32),
+            pltpu.VMEM((2, hidden, hidden), f32),
             pltpu.VMEM((1, 4 * hidden), f32),
             pltpu.SemaphoreType.DMA((len(large),)),
         ],
         compiler_params=pltpu.CompilerParams(vmem_limit_bytes=40 * 2**20),
         name="update_step",
-    )(g_all, scalars, wht, bias, sth, rth, bm, bv, *loaded)
+    )(*summed, wht, bias, sth, rth, bm, bv, *loaded)
     return [
         loss, total, norm, g1, gr, gh, m, v, l1, lm, ls, lh, n1_new, nr_new, nh_new, nb, n1_low, nr_low, nh_low
     ]
@@ -914,15 +953,15 @@
     def lines(a):
         return jnp.transpose(a, (1, 3, 0, 2))
 
-    g_all, scalars = summed_gradients(
+    summed = summed_gradients(
         peers, cap, seeds, fan,
         lines(nbr_index), lines(nbr_mask), jnp.swapaxes(features[0], 0, 1), w_first, w_rest,
-        send_rows[0, 0], send_count[0], labels, seed_mask, w_head.T, biases,
+        send_rows[0, 0], send_count[0], labels, seed_mask, w_head.T, biases, root_mid, root_sq,
     )
     out = list(
         updates(
-            fin, g_all, scalars, w_first, w_rest, w_head.T, biases,
-            stat_big, root_big, stat_mid, root_mid, stat_sq, root_sq, stat_hr, root_hr,
+            fin, summed, w_head.T, biases,
+            stat_big, root_big, stat_mid, stat_sq, root_sq, stat_hr, root_hr,
             bias_m, bias_v,
         )
     )

time: 80.7 us -> 79.6 us (0.986)
  Pallas kernels: 79.5 us -> 78.4 us
where the time goes in v5:
time: 79.6 us; the launch traced here: 79.5 us
  Pallas kernels  78.4 us (98%)
  between operations  1.01 us (1%)
    pallas_call x1, Pallas kernels, summed_gradients(): pl.pallas_call(functools.partial(graph_kernel, peers, cap, seeds, fan), o...  73.7 us
    pallas_call x1, Pallas kernels, updates(): pl.pallas_call(functools.partial(update_kernel, fin), out_shape=tuple(sma...  4.73 us

profile of v5, /device:TPU:1, one launch (start us, length us, event | category | flops | bytes accessed | tf_op | source)
XLA Modules:
  0.0 79.5 jit_solution(5224892932413764369)
XLA Ops:
  0.7 0.0 copy-start
  0.7 0.0 copy-start.1
  0.7 0.0 copy-start.2
  0.7 0.0 copy-start.3
  0.7 0.0 copy-start.4
  0.7 0.0 copy-start.5
  0.7 0.0 copy-start.6
  0.7 0.0 copy-start.7
  0.7 0.0 copy-start.8
  0.8 0.0 copy-start.9
  0.8 0.0 copy-start.10
  0.8 73.7 %graph_step.1 = (bf16[2,2304,128]{2,1,0:T(8,128)(2,1)S(1)}, f32[8,128]{1,0:T(8,128)S(1)}, f32[2,128,512]{2,1,0:T(8,128)S(1)}, f32[2,64,256]{2,1,0:T(8,128)S(1)},...) custom-call(s32[3,25,1,2048]{3,2,1,0:T(1,128)} %bitcast.17, ...), custom_call_target="tpu_custom_call" | custom-call | flops 24000000000 | bytes 12582912 | tf_op jit(solution)/shard_map/graph_step/pallas_call | solution.py:751
  74.5 0.0 copy-done
  74.5 0.0 copy-done.1
  74.5 0.0 copy-done.2
  74.5 0.0 copy-done.3
  74.5 0.0 copy-done.4
  74.5 0.0 copy-done.5
  74.5 0.0 copy-done.6
  74.5 0.0 copy-done.7
  74.6 0.0 copy-done.8
  74.6 0.0 copy-done.9
  74.6 0.0 copy-done.10
  74.6 4.7 %update_step.1 = (f32[1,1]{1,0:T(1,128)}, f32[1,1]{1,0:T(1,128)}, f32[1,1]{1,0:T(1,128)}, f32[41,64]{1,0:T(8,128)}, f32[809]{0:T(1024)}, /*index=5*/f32[809]{0:T...) custom-call(bf16[2,2304,128]{2,1,0:T(8,128)(2,1)S(1)} %get-tuple-ele, ...), custom_call_target="tpu_custom_call" | custom-call | tf_op jit(solution)/shard_map/update_step/pallas_call | solution.py:922
Async XLA Ops:
  0.7 73.8 %copy-start = (f32[301,1204]{1,0:T(8,128)S(1)}, f32[301,1204]{1,0:T(8,128)}, u32[]{:S(2)}) copy-start(f32[301,1204]{1,0:T(8,128)} %st1.1) | copy-start | bytes 4348852
  0.7 73.8 %copy-start.1 = (f32[301,1204]{1,0:T(8,128)S(1)}, f32[301,1204]{1,0:T(8,128)}, u32[]{:S(2)}) copy-start(f32[301,1204]{1,0:T(8,128)} %rt1.1) | copy-start | bytes 4348852
  0.7 73.8 %copy-start.2 = (f32[4,256,256]{2,1,0:T(8,128)S(1)}, f32[4,256,256]{2,1,0:T(8,128)}, u32[]{:S(2)}) copy-start(f32[4,256,256]{2,1,0:T(8,128)} %rts.1) | copy-start | bytes 3145732
  0.7 73.8 %copy-start.3 = (f32[2,128,512]{2,1,0:T(8,128)S(1)}, f32[2,128,512]{2,1,0:T(8,128)}, u32[]{:S(2)}) copy-start(f32[2,128,512]{2,1,0:T(8,128)} %stm.1) | copy-start | bytes 1572868
  0.7 73.8 %copy-start.4 = (f32[4,64,256]{2,1,0:T(8,128)S(1)}, f32[4,64,256]{2,1,0:T(8,128)}, u32[]{:S(2)}) copy-start(f32[4,64,256]{2,1,0:T(8,128)} %sts.1) | copy-start | bytes 786436
  0.7 73.8 %copy-start.5 = (f32[256,41]{0,1:T(8,128)S(1)}, f32[256,41]{0,1:T(8,128)}, u32[]{:S(2)}) copy-start(f32[256,41]{0,1:T(8,128)} %param.30) | copy-start | bytes 125956
  0.7 73.8 %copy-start.6 = (f32[41,41]{1,0:T(8,128)S(1)}, f32[41,41]{1,0:T(8,128)}, u32[]{:S(2)}) copy-start(f32[41,41]{1,0:T(8,128)} %sth.1) | copy-start | bytes 20176
  0.7 73.8 %copy-start.7 = (f32[41,41]{1,0:T(8,128)S(1)}, f32[41,41]{1,0:T(8,128)}, u32[]{:S(2)}) copy-start(f32[41,41]{1,0:T(8,128)} %rth.1) | copy-start | bytes 20176
  0.7 73.8 %copy-start.8 = (f32[809]{0:T(1024)S(1)}, f32[809]{0:T(1024)}, u32[]{:S(2)}) copy-start(f32[809]{0:T(1024)} %bias.1) | copy-start | bytes 9712
  0.8 73.8 %copy-start.9 = (f32[809]{0:T(1024)S(1)}, f32[809]{0:T(1024)}, u32[]{:S(2)}) copy-start(f32[809]{0:T(1024)} %bm.1) | copy-start | bytes 9712
  0.8 73.8 %copy-start.10 = (f32[809]{0:T(1024)S(1)}, f32[809]{0:T(1024)}, u32[]{:S(2)}) copy-start(f32[809]{0:T(1024)} %bv.1) | copy-start | bytes 9712

commit v6 on v5

--- a/solution.py
+++ b/solution.py
@@ -317,7 +317,7 @@
                 near[at, a * 128 : (a + 1) * 128] = tile.astype(bf16)
         return 0
 
-    lax.fori_loop(0, blocks, build, 0)
+    lax.fori_loop(0, blocks, build, 0, unroll=2)
 
     for load in loads[5:]:
         load.wait()
@@ -381,7 +381,7 @@
         slope1[:, blk] = gelu_slope(grad1[:, blk])
         return 0
 
-    lax.fori_loop(0, blocks, slopes, 0)
+    lax.fori_loop(0, blocks, slopes, 0, unroll=2)
     first_rows = w1_out.shape[0]
     for i in range(2 * fin // first_rows):
 

time: 79.6 us -> 78.9 us (level)
  no operation moved by 1% of the time
where the time goes in v6:
time: 78.9 us; the launch traced here: 78.8 us
  Pallas kernels  77.7 us (98%)
  between operations  1.01 us (1%)
    pallas_call x1, Pallas kernels, summed_gradients(): pl.pallas_call(functools.partial(graph_kernel, peers, cap, seeds, fan), o...  73 us
    pallas_call x1, Pallas kernels, updates(): pl.pallas_call(functools.partial(update_kernel, fin), out_shape=tuple(sma...  4.73 us

profile of v6, /device:TPU:1, one launch (start us, length us, event | category | flops | bytes accessed | tf_op | source)
XLA Modules:
  0.0 78.8 jit_solution(15470534716469405746)
XLA Ops:
  0.7 0.0 copy-start
  0.7 0.0 copy-start.1
  0.7 0.0 copy-start.2
  0.7 0.0 copy-start.3
  0.7 0.0 copy-start.4
  0.7 0.0 copy-start.5
  0.7 0.0 copy-start.6
  0.7 0.0 copy-start.7
  0.7 0.0 copy-start.8
  0.8 0.0 copy-start.9
  0.8 0.0 copy-start.10
  0.8 73.0 %graph_step.1 = (bf16[2,2304,128]{2,1,0:T(8,128)(2,1)S(1)}, f32[8,128]{1,0:T(8,128)S(1)}, f32[2,128,512]{2,1,0:T(8,128)S(1)}, f32[2,64,256]{2,1,0:T(8,128)S(1)},...) custom-call(s32[3,25,1,2048]{3,2,1,0:T(1,128)} %bitcast.17, ...), custom_call_target="tpu_custom_call" | custom-call | flops 24000000000 | bytes 12582912 | tf_op jit(solution)/shard_map/graph_step/pallas_call | solution.py:751
  73.8 0.0 copy-done
  73.8 0.0 copy-done.1
  73.8 0.0 copy-done.2
  73.8 0.0 copy-done.3
  73.8 0.0 copy-done.4
  73.8 0.0 copy-done.5
  73.8 0.0 copy-done.6
  73.9 0.0 copy-done.7
  73.9 0.0 copy-done.8
  73.9 0.0 copy-done.9
  73.9 0.0 copy-done.10
  73.9 4.7 %update_step.1 = (f32[1,1]{1,0:T(1,128)}, f32[1,1]{1,0:T(1,128)}, f32[1,1]{1,0:T(1,128)}, f32[41,64]{1,0:T(8,128)}, f32[809]{0:T(1024)}, /*index=5*/f32[809]{0:T...) custom-call(bf16[2,2304,128]{2,1,0:T(8,128)(2,1)S(1)} %get-tuple-ele, ...), custom_call_target="tpu_custom_call" | custom-call | tf_op jit(solution)/shard_map/update_step/pallas_call | solution.py:922
Async XLA Ops:
  0.7 73.1 %copy-start = (f32[301,1204]{1,0:T(8,128)S(1)}, f32[301,1204]{1,0:T(8,128)}, u32[]{:S(2)}) copy-start(f32[301,1204]{1,0:T(8,128)} %st1.1) | copy-start | bytes 4348852
  0.7 73.1 %copy-start.1 = (f32[301,1204]{1,0:T(8,128)S(1)}, f32[301,1204]{1,0:T(8,128)}, u32[]{:S(2)}) copy-start(f32[301,1204]{1,0:T(8,128)} %rt1.1) | copy-start | bytes 4348852
  0.7 73.1 %copy-start.2 = (f32[4,256,256]{2,1,0:T(8,128)S(1)}, f32[4,256,256]{2,1,0:T(8,128)}, u32[]{:S(2)}) copy-start(f32[4,256,256]{2,1,0:T(8,128)} %rts.1) | copy-start | bytes 3145732
  0.7 73.1 %copy-start.3 = (f32[2,128,512]{2,1,0:T(8,128)S(1)}, f32[2,128,512]{2,1,0:T(8,128)}, u32[]{:S(2)}) copy-start(f32[2,128,512]{2,1,0:T(8,128)} %stm.1) | copy-start | bytes 1572868
  0.7 73.1 %copy-start.4 = (f32[4,64,256]{2,1,0:T(8,128)S(1)}, f32[4,64,256]{2,1,0:T(8,128)}, u32[]{:S(2)}) copy-start(f32[4,64,256]{2,1,0:T(8,128)} %sts.1) | copy-start | bytes 786436
  0.7 73.1 %copy-start.5 = (f32[256,41]{0,1:T(8,128)S(1)}, f32[256,41]{0,1:T(8,128)}, u32[]{:S(2)}) copy-start(f32[256,41]{0,1:T(8,128)} %param.30) | copy-start | bytes 125956
  0.7 73.1 %copy-start.6 = (f32[41,41]{1,0:T(8,128)S(1)}, f32[41,41]{1,0:T(8,128)}, u32[]{:S(2)}) copy-start(f32[41,41]{1,0:T(8,128)} %sth.1) | copy-start | bytes 20176
  0.7 73.1 %copy-start.7 = (f32[41,41]{1,0:T(8,128)S(1)}, f32[41,41]{1,0:T(8,128)}, u32[]{:S(2)}) copy-start(f32[41,41]{1,0:T(8,128)} %rth.1) | copy-start | bytes 20176
  0.7 73.1 %copy-start.8 = (f32[809]{0:T(1024)S(1)}, f32[809]{0:T(1024)}, u32[]{:S(2)}) copy-start(f32[809]{0:T(1024)} %bias.1) | copy-start | bytes 9712
  0.8 73.1 %copy-start.9 = (f32[809]{0:T(1024)S(1)}, f32[809]{0:T(1024)}, u32[]{:S(2)}) copy-start(f32[809]{0:T(1024)} %bm.1) | copy-start | bytes 9712
  0.8 73.1 %copy-start.10 = (f32[809]{0:T(1024)S(1)}, f32[809]{0:T(1024)}, u32[]{:S(2)}) copy-start(f32[809]{0:T(1024)} %bv.1) | copy-start | bytes 9712
